TPU v7x, 32 devices: a whole 2x2x4 slice. The times are simulated.
32 devices in a mesh: ctx: 8 (over z, core), fsdp: 4 (over y, x).
Axes of the slice: x: 2, y: 2, z: 4, core: 2. Of those that a mesh axis runs over, the one named last changes fastest.
Arguments:
- hidden_in: bfloat16 [4, 2048, 2048], P('fsdp', 'ctx'), may hold values from -6 to 6
- out_grad: bfloat16 [4, 2048, 2048], P('fsdp', 'ctx'), may hold values from -6 to 6
- lengths: int32 [4, 2], P('fsdp'), may hold values from 682 to 1024, as said below
- block_order: int32 [4, 16], P('fsdp'), may hold values from 0 to 15, as said below
- ln_gain: bfloat16 [2048], P('fsdp'), may hold values from 0.25 to 1.75
- ln_bias: bfloat16 [2048], P('fsdp'), may hold values from -2 to 2
- w_qkv: bfloat16 [2048, 6144], P('fsdp'), may hold values from -0.125 to 0.125
- b_qkv: bfloat16 [6144], P('fsdp'), may hold values from -2 to 2
- w_out: bfloat16 [2048, 2048], P('fsdp'), may hold values from -2 to 2
- w_gate: bfloat16 [2048, 5632], P('fsdp'), may hold values from -0.125 to 0.125
- w_up: bfloat16 [2048, 5632], P('fsdp'), may hold values from -0.125 to 0.125
- w_down: bfloat16 [5632, 2048], P('fsdp'), may hold values from -0.078125 to 0.078125
Outputs:
- output: bfloat16 [4, 2048, 2048], P('fsdp', 'ctx')
- input_grad: bfloat16 [4, 2048, 2048], P('fsdp', 'ctx')
- grad_ln_gain: float32 [2048], P('fsdp')
- grad_ln_bias: float32 [2048], P('fsdp')
- grad_w_qkv: float32 [2048, 6144], P('fsdp')
- grad_b_qkv: float32 [6144], P('fsdp')
- grad_w_out: float32 [2048, 2048], P('fsdp')
- grad_w_gate: float32 [2048, 5632], P('fsdp')
- grad_w_up: float32 [2048, 5632], P('fsdp')
- grad_w_down: float32 [5632, 2048], P('fsdp')
Inputs may be any that keep to these rules, and one draw needn't show every extreme that they name: Each group's 2 lengths sum to 2048; each is at least 682; in every group at least one sequence has the greatest length, at a position that varies. `block_order`: each group's row is a permutation of 0 to 15 whose entries 2 c and 2 c + 1 sum to 15.
All inputs are finite; a program needn't handle non-finite values.
Results may differ from a plain program's by a relative error of at most 0.012.
Values may be sent and summed in bfloat16 or wider, within the bound.
No kernel may reach another device: no remote copies, remote signals or barrier semaphores. Data moves between devices by JAX's collectives and lax.ppermute only.
A program may use at most 576 MiB of HBM per device.

v0:
```python
import jax
import jax.numpy as jnp
from jax import lax
from jax.sharding import PartitionSpec as P

HD = 64
ROT = 16
BLOCK = 128


def stream_places(order_row, length_row):
    places = (order_row[:, None] * BLOCK + jnp.arange(BLOCK, dtype=jnp.int32)[None, :]).reshape(-1)
    ends = jnp.cumsum(length_row)
    starts = ends - length_row
    begins = jnp.max(jnp.where(starts[None, :] <= places[:, None], starts[None, :], 0), axis=1)
    return (places, begins)


def rotary_tables(places, begins):
    offsets = (places - begins).astype(jnp.float32)
    inverse = 1.0 / 10000.0 ** (jnp.arange(0, ROT, 2).astype(jnp.float32) / ROT)
    angles = offsets[:, None, None] * inverse[None, None, :]
    return (jnp.cos(angles), jnp.sin(angles))


def rotate(values, cosine, sine_table, direction):
    half_rot = ROT // 2
    lead_half = values[..., :half_rot]
    tail_half = values[..., half_rot:ROT]
    return jnp.concatenate(
        [
            lead_half * cosine - direction * tail_half * sine_table,
            tail_half * cosine + direction * lead_half * sine_table,
            values[..., ROT:],
        ],
        axis=-1,
    )


def arrange(values, axis_at):
    ctx_count = lax.axis_size("ctx")
    fsdp_count = lax.axis_size("fsdp")
    shape_in = values.shape
    length = shape_in[axis_at]
    split_shape = (
        shape_in[:axis_at]
        + (fsdp_count, ctx_count, length // (fsdp_count * ctx_count))
        + shape_in[axis_at + 1 :]
    )
    return jnp.swapaxes(values.reshape(split_shape), axis_at, axis_at + 1).reshape(shape_in)


def reduce_pair(first_term, second_term):
    parts = (
        lax.psum_scatter(first_term, ("ctx", "fsdp"), scatter_dimension=0, tiled=True),
        lax.psum_scatter(second_term, ("ctx", "fsdp"), scatter_dimension=0, tiled=True),
    )
    return (
        lax.all_gather(parts[0], "ctx", axis=0, tiled=True),
        lax.all_gather(parts[1], "ctx", axis=0, tiled=True),
    )


def matmul(left, right):
    return jnp.dot(left, right, preferred_element_type=jnp.float32)


def shards(
    hidden_in,
    out_grad,
    lengths,
    block_order,
    ln_gain,
    ln_bias,
    w_qkv,
    b_qkv,
    w_out,
    w_gate,
    w_up,
    w_down,
):
    row_count = hidden_in.shape[1]
    model_width = w_out.shape[1]
    head_count = model_width // HD
    head_span = 4 * HD
    group_count = head_count // 4
    score_scale = HD ** (-0.5)
    ctx_at = lax.axis_index("ctx")
    places_all, begins_all = stream_places(block_order[0], lengths[0])
    key_count = places_all.shape[0]
    places = lax.dynamic_slice_in_dim(places_all, ctx_at * row_count, row_count)
    begins = lax.dynamic_slice_in_dim(begins_all, ctx_at * row_count, row_count)
    allowed = (places_all[None, :] <= places[:, None]) & (places_all[None, :] >= begins[:, None])
    cosine, sine_table = rotary_tables(places, begins)
    gain_full, bias_full, w_attn, b_attn, w_proj, w_gating, w_rising, w_lower = (
        lax.all_gather(ln_gain, "fsdp", axis=0, tiled=True),
        lax.all_gather(ln_bias, "fsdp", axis=0, tiled=True),
        lax.all_gather(w_qkv, "fsdp", axis=0, tiled=True),
        lax.all_gather(b_qkv, "fsdp", axis=0, tiled=True),
        lax.all_gather(w_out, "fsdp", axis=0, tiled=True),
        lax.all_gather(w_gate, "fsdp", axis=0, tiled=True),
        lax.all_gather(w_up, "fsdp", axis=0, tiled=True),
        lax.all_gather(w_down, "fsdp", axis=0, tiled=True),
    )
    float_in = hidden_in[0].astype(jnp.float32)
    centre = jnp.mean(float_in, axis=1, keepdims=True)
    deviation = float_in - centre
    inverse_std = lax.rsqrt(jnp.mean(deviation * deviation, axis=1, keepdims=True) + 1e-05)
    normal_hat = deviation * inverse_std
    normed = (normal_hat * gain_full.astype(jnp.float32) + bias_full.astype(jnp.float32)).astype(
        jnp.bfloat16
    )
    merged_proj = matmul(normed, w_attn) + b_attn.astype(jnp.float32)
    query_all = rotate(
        merged_proj[:, :model_width].reshape(row_count, head_count, HD), cosine, sine_table, 1.0
    )
    query_all = query_all.reshape(row_count, model_width).astype(jnp.bfloat16)
    key_own = rotate(
        merged_proj[:, model_width : 2 * model_width].reshape(row_count, head_count, HD),
        cosine,
        sine_table,
        1.0,
    )
    key_own = key_own.reshape(row_count, model_width).astype(jnp.bfloat16)
    value_own = merged_proj[:, 2 * model_width :].astype(jnp.bfloat16)
    key_all, value_all = (
        lax.all_gather(key_own, "ctx", axis=0, tiled=True),
        lax.all_gather(value_own, "ctx", axis=0, tiled=True),
    )

    def take(array_in, group_at, length):
        return lax.dynamic_slice_in_dim(array_in, group_at * head_span, head_span, 1).reshape(
            length, 4, HD
        )

    def masked_scores(query_part, key_part):
        scores = (
            jnp.einsum("qhd,khd->hqk", query_part, key_part, preferred_element_type=jnp.float32)
            * score_scale
        )
        return jnp.where(allowed[None], scores, -1e30)

    def forward_group(group_at):
        query_part = take(query_all, group_at, row_count)
        key_part = take(key_all, group_at, key_count)
        value_part = take(value_all, group_at, key_count)
        scores = masked_scores(query_part, key_part)
        row_max = jnp.max(scores, axis=2, keepdims=True)
        log_total = row_max + jnp.log(jnp.sum(jnp.exp(scores - row_max), axis=2, keepdims=True))
        probs = jnp.exp(scores - log_total).astype(jnp.bfloat16)
        heads_out = jnp.einsum(
            "hqk,khd->qhd", probs, value_part, preferred_element_type=jnp.float32
        )
        return (heads_out.reshape(row_count, head_span), log_total)

    out_parts, log_totals = lax.map(forward_group, jnp.arange(group_count))

    def whole(parts):
        return jnp.moveaxis(parts, 0, 1).reshape(row_count, model_width)

    attn_mixed = whole(out_parts).astype(jnp.bfloat16)
    gating = matmul(normed, w_gating)
    rising = matmul(normed, w_rising)
    sigma = jax.nn.sigmoid(gating)
    silu_gate = gating * sigma
    activated = (silu_gate * rising).astype(jnp.bfloat16)
    summed = float_in + matmul(attn_mixed, w_proj) + matmul(activated, w_lower)
    output = summed.astype(jnp.bfloat16)[None]
    grad_rows_in = out_grad[0]
    grad_float = grad_rows_in.astype(jnp.float32)
    gain_back, w_attn_back, w_proj_back, w_gating_back, w_rising_back, w_lower_back = (
        lax.all_gather(ln_gain, "fsdp", axis=0, tiled=True),
        lax.all_gather(w_qkv, "fsdp", axis=0, tiled=True),
        lax.all_gather(w_out, "fsdp", axis=0, tiled=True),
        lax.all_gather(w_gate, "fsdp", axis=0, tiled=True),
        lax.all_gather(w_up, "fsdp", axis=0, tiled=True),
        lax.all_gather(w_down, "fsdp", axis=0, tiled=True),
    )
    grad_down, grad_proj = reduce_pair(
        matmul(arrange(activated, 1).T, grad_rows_in),
        matmul(arrange(attn_mixed, 1).T, grad_rows_in),
    )
    grad_act = matmul(grad_rows_in, w_lower_back.T)
    grad_gating = (grad_act * rising * sigma * (1.0 + gating * (1.0 - sigma))).astype(jnp.bfloat16)
    grad_rising = (grad_act * silu_gate).astype(jnp.bfloat16)
    normed_order = arrange(normed, 1)
    grad_gate_w, grad_up_w = reduce_pair(
        matmul(normed_order.T, grad_gating), matmul(normed_order.T, grad_rising)
    )
    grad_normed = matmul(grad_gating, w_gating_back.T) + matmul(grad_rising, w_rising_back.T)
    grad_mixed = matmul(grad_rows_in, w_proj_back.T).astype(jnp.bfloat16)

    def query_side(group_at):
        query_part = take(query_all, group_at, row_count)
        key_part = take(key_all, group_at, key_count)
        value_part = take(value_all, group_at, key_count)
        grad_part = take(grad_mixed, group_at, row_count)
        scores = masked_scores(query_part, key_part)
        probs = jnp.exp(scores - log_totals[group_at])
        grad_probs = jnp.einsum(
            "qhd,khd->hqk", grad_part, value_part, preferred_element_type=jnp.float32
        )
        row_dot = jnp.sum(probs * grad_probs, axis=2, keepdims=True)
        grad_scores = (probs * (grad_probs - row_dot)).astype(jnp.bfloat16)
        grad_query = (
            jnp.einsum("hqk,khd->qhd", grad_scores, key_part, preferred_element_type=jnp.float32)
            * score_scale
        )
        return (query_part, grad_part, probs, grad_scores, grad_query, row_dot)

    def backward_group(group_at):
        query_part, grad_part, probs, grad_scores, grad_query, row_dot = query_side(group_at)
        grad_key = (
            jnp.einsum("hqk,qhd->khd", grad_scores, query_part, preferred_element_type=jnp.float32)
            * score_scale
        )
        grad_value = jnp.einsum(
            "hqk,qhd->khd",
            probs.astype(jnp.bfloat16),
            grad_part,
            preferred_element_type=jnp.float32,
        )
        own_key, own_value = (
            lax.psum_scatter(
                grad_key.reshape(key_count, head_span), "ctx", scatter_dimension=0, tiled=True
            ),
            lax.psum_scatter(
                grad_value.reshape(key_count, head_span), "ctx", scatter_dimension=0, tiled=True
            ),
        )
        return (grad_query.reshape(row_count, head_span), own_key, own_value)

    query_parts, key_parts, value_parts = lax.map(backward_group, jnp.arange(group_count))
    grad_query = rotate(
        whole(query_parts).reshape(row_count, head_count, HD), cosine, sine_table, -1.0
    )
    grad_key = rotate(whole(key_parts).reshape(row_count, head_count, HD), cosine, sine_table, -1.0)
    grad_merged = jnp.concatenate(
        [
            grad_query.reshape(row_count, model_width),
            grad_key.reshape(row_count, model_width),
            whole(value_parts),
        ],
        axis=1,
    ).astype(jnp.bfloat16)
    grad_normed = grad_normed + matmul(grad_merged, w_attn_back.T)
    gain_term = jnp.sum(grad_normed * normal_hat, axis=0)
    bias_term = jnp.sum(grad_normed, axis=0)
    merged_term = jnp.sum(grad_merged, axis=0, dtype=jnp.float32)
    vec_terms = jnp.concatenate(
        [gain_term[:, None], bias_term[:, None], merged_term.reshape(model_width, 3)], axis=1
    )
    grad_attn_w, grad_vecs = reduce_pair(matmul(normed_order.T, grad_merged), arrange(vec_terms, 0))
    grad_hat = grad_normed * gain_back.astype(jnp.float32)
    grad_in = grad_float + inverse_std * (
        grad_hat
        - jnp.mean(grad_hat, axis=1, keepdims=True)
        - normal_hat * jnp.mean(grad_hat * normal_hat, axis=1, keepdims=True)
    )
    return (
        output,
        grad_in.astype(jnp.bfloat16)[None],
        grad_vecs[:, 0],
        grad_vecs[:, 1],
        grad_attn_w,
        grad_vecs[:, 2:].reshape(-1),
        grad_proj,
        grad_gate_w,
        grad_up_w,
        grad_down,
    )


def solution(mesh):
    return jax.shard_map(
        shards,
        mesh=mesh,
        in_specs=(
            P("fsdp", "ctx", None),
            P("fsdp", "ctx", None),
            P("fsdp", None),
            P("fsdp", None),
            P("fsdp"),
            P("fsdp"),
            P("fsdp", None),
            P("fsdp"),
            P("fsdp", None),
            P("fsdp", None),
            P("fsdp", None),
            P("fsdp", None),
        ),
        out_specs=(
            P("fsdp", "ctx", None),
            P("fsdp", "ctx", None),
            P("fsdp"),
            P("fsdp"),
            P("fsdp", None),
            P("fsdp"),
            P("fsdp", None),
            P("fsdp", None),
            P("fsdp", None),
            P("fsdp", None),
        ),
        check_vma=False,
    )
```

profile of v0, /device:TPU:0, one launch (start us, length us, event | category | flops | bytes accessed | tf_op | source)
XLA Modules:
  0.0 6300.6 jit_solution(13347218016224649433)
XLA Ops:
  35.6 204.8 %all-gather.17.cloned.1.call-done = bf16[2048,6144]{1,0:T(8,128)(2,1)} async-done(((bf16[512,6144]{1,0:T(8,128)(2,1)}), bf16[2048,6144]{1,0:T(8,128)(2,1)}) %all-gather.17.cloned.1.call-update) | async-done | bytes 25165840 | tf_op jit(solution)/shard_map/all_gather | solution.py:98
  270.6 59.3 all-gather.23.cloned.1.call-done
  339.2 75.0 %all-gather.19.cloned.1.call-done = bf16[2048,2048]{1,0:T(8,128)(2,1)} async-done(((bf16[256,2048]{1,0:T(8,128)(2,1)}), bf16[2048,2048]{1,0:T(8,128)(2,1)}) %all-gather.19.cloned.1.call-update) | async-done | bytes 8388624 | tf_op jit(solution)/shard_map/all_gather | solution.py:128
  414.2 12.4 copy.84
  426.6 70.7 %all-gather.21.cloned.1.call-done = bf16[2048,2048]{0,1:T(8,128)(2,1)} async-done(((bf16[256,2048]{0,1:T(8,128)(2,1)}), bf16[2048,2048]{0,1:T(8,128)(2,1)}) %all-gather.21.cloned.1.call-update) | async-done | bytes 8388624 | tf_op jit(solution)/shard_map/all_gather | solution.py:127
  497.3 87.7 %while.30 = (s32[]{:T(128)}, bf16[8,256,256]{1,2,0:T(8,128)(2,1)S(1)}, f32[8,4,256,1]{2,1,3,0:T(4,128)S(1)}, s32[8]{0:T(128)S(1)}, bf16[2048,2048]{0,1:T(8,128)(...) while((s32[]{:T(128)}, ...), condition=%wide.region_7.8_spmd.clone.clone, body=%wide.region_4.7_spmd.clone.sunk.clone | while | flops 561511424 | bytes 34384060 | solution.py:156
  585.9 687.2 %while.31 = (s32[]{:T(128)}, f32[8,256,256]{1,2,0:T(8,128)}, f32[8,256,256]{1,2,0:T(8,128)}, bf16[8,256,256]{1,2,0:T(8,128)(2,1)}, s32[8]{0:T(128)S(1)}, /*index...) while((s32[]{:T(128)}, f32[8,256,256]{1,2,0:T(8,128)}, ...), condition=%wide.region_12.13_spmd.clone.clone, body=%wide.region_8.12_spmd.clone.sunk.clone | while | flops 1375796224 | bytes 177773008 | solution.py:233
  614.3 18.2 reduce-scatter.25.cloned.1.call-done
  633.5 36.2 reduce-scatter.23.cloned.1.call-done
  699.6 18.7 reduce-scatter.25.cloned.1.call-done
  719.2 36.6 reduce-scatter.23.cloned.1.call-done
  785.7 18.8 reduce-scatter.25.cloned.1.call-done
  805.5 36.3 reduce-scatter.23.cloned.1.call-done
  871.6 18.8 reduce-scatter.25.cloned.1.call-done
  891.4 36.3 reduce-scatter.23.cloned.1.call-done
  957.5 18.7 reduce-scatter.25.cloned.1.call-done
  977.2 36.4 reduce-scatter.23.cloned.1.call-done
  1043.4 18.8 reduce-scatter.25.cloned.1.call-done
  1063.2 36.4 reduce-scatter.23.cloned.1.call-done
  1129.4 18.8 reduce-scatter.25.cloned.1.call-done
  1149.1 36.4 reduce-scatter.23.cloned.1.call-done
  1215.4 18.8 reduce-scatter.25.cloned.1.call-done
  1235.1 36.3 reduce-scatter.23.cloned.1.call-done
  1299.7 19.7 fusion.29
  1319.5 165.5 %all-gather.25.cloned.1.call-done = bf16[2048,5632]{1,0:T(8,128)(2,1)} async-done(((bf16[512,5632]{1,0:T(8,128)(2,1)}), bf16[2048,5632]{1,0:T(8,128)(2,1)}) %all-gather.25.cloned.1.call-update) | async-done | bytes 23068688 | tf_op jit(solution)/shard_map/all_gather | solution.py:101
  1485.0 14.6 fusion.31
  1499.6 197.7 %all-gather.27.cloned.1.call-done = bf16[2048,5632]{1,0:T(8,128)(2,1)} async-done(((bf16[512,5632]{1,0:T(8,128)(2,1)}), bf16[2048,5632]{1,0:T(8,128)(2,1)}) %all-gather.27.cloned.1.call-update) | async-done | bytes 23068688 | tf_op jit(solution)/shard_map/all_gather | solution.py:102
  1697.3 14.4 fusion.30
  1711.7 198.0 %all-gather.29.cloned.1.call-done = bf16[5632,2048]{1,0:T(8,128)(2,1)} async-done(((bf16[1408,2048]{1,0:T(8,128)(2,1)}), bf16[5632,2048]{1,0:T(8,128)(2,1)}) %all-gather.29.cloned.1.call-update) | async-done | bytes 23068688 | tf_op jit(solution)/shard_map/all_gather | solution.py:103
  1909.7 25.6 multiply_convert_fusion.1
  1942.0 18.0 fusion.21
  1960.1 20.2 fusion.38
  1980.4 19.9 fusion.37
  2000.3 12.9 fusion.36
  2013.2 13.3 convolution_add_fusion.2
  2026.6 14.1 multiply_reduce_fusion.1
  2045.8 223.7 %reduce-scatter.13.cloned.1.call-done = f32[64,2048]{1,0:T(8,128)} async-done(((f32[2048,2048]{1,0:T(8,128)}), f32[64,2048]{1,0:T(8,128)}) %reduce-scatter.13.cloned.1.call-update) | async-done | bytes 524304 | tf_op jit(solution)/shard_map/reduce_scatter | solution.py:56
  2269.6 439.3 %reduce-scatter.11.cloned.1.call-done = f32[64,6144]{1,0:T(8,128)} async-done(((f32[2048,6144]{1,0:T(8,128)}), f32[64,6144]{1,0:T(8,128)}) %reduce-scatter.11.cloned.1.call-update) | async-done | bytes 1572880 | tf_op jit(solution)/shard_map/reduce_scatter | solution.py:55
  2709.0 969.7 %reduce-scatter.19.cloned.1.call-done = f32[176,2048]{1,0:T(8,128)} async-done(((f32[5632,2048]{1,0:T(8,128)}), f32[176,2048]{1,0:T(8,128)}) %reduce-scatter.19.cloned.1.call-update) | async-done | bytes 1441808 | tf_op jit(solution)/shard_map/reduce_scatter | solution.py:55
  3678.8 972.9 %reduce-scatter.17.cloned.1.call-done = f32[64,5632]{1,0:T(8,128)} async-done(((f32[2048,5632]{1,0:T(8,128)}), f32[64,5632]{1,0:T(8,128)}) %reduce-scatter.17.cloned.1.call-update) | async-done | bytes 1441808 | tf_op jit(solution)/shard_map/reduce_scatter | solution.py:56
  4652.0 972.9 %reduce-scatter.15.cloned.1.call-done = f32[64,5632]{1,0:T(8,128)} async-done(((f32[2048,5632]{1,0:T(8,128)}), f32[64,5632]{1,0:T(8,128)}) %reduce-scatter.15.cloned.1.call-update) | async-done | bytes 1441808 | tf_op jit(solution)/shard_map/reduce_scatter | solution.py:55
  5646.5 118.3 %reduce-scatter.21.cloned.1.call-done = f32[64,5]{1,0:T(8,128)} async-done(((f32[2048,5]{1,0:T(8,128)}), f32[64,5]{1,0:T(8,128)}) %reduce-scatter.21.cloned.1.call-update) | async-done | bytes 1296
  5765.6 14.1 all-gather.3
  5781.3 28.3 all-gather.33.cloned.1.call-done
  5809.6 117.2 %all-gather.31.cloned.1.call-done = f32[512,6144]{1,0:T(8,128)} async-done(((f32[64,6144]{1,0:T(8,128)}), f32[512,6144]{1,0:T(8,128)}) %all-gather.31.cloned.1.call-update) | async-done | bytes 12582928 | tf_op jit(solution)/shard_map/all_gather | solution.py:59
  5926.8 108.1 %all-gather.39.cloned.1.call-done = f32[1408,2048]{1,0:T(8,128)} async-done(((f32[176,2048]{1,0:T(8,128)}), f32[1408,2048]{1,0:T(8,128)}) %all-gather.39.cloned.1.call-update) | async-done | bytes 11534352 | tf_op jit(solution)/shard_map/all_gather | solution.py:59
  6034.9 108.0 %all-gather.37.cloned.1.call-done = f32[512,5632]{1,0:T(8,128)} async-done(((f32[64,5632]{1,0:T(8,128)}), f32[512,5632]{1,0:T(8,128)}) %all-gather.37.cloned.1.call-update) | async-done | bytes 11534352 | tf_op jit(solution)/shard_map/all_gather | solution.py:60
  6142.9 108.2 %all-gather.35.cloned.1.call-done = f32[512,5632]{1,0:T(8,128)} async-done(((f32[64,5632]{1,0:T(8,128)}), f32[512,5632]{1,0:T(8,128)}) %all-gather.35.cloned.1.call-update) | async-done | bytes 11534352 | tf_op jit(solution)/shard_map/all_gather | solution.py:59
  (531 shorter events, 480.7 us)
Async XLA Ops:
  7.2 233.2 %all-gather.17.cloned.1.call-start = ((), (), s32[]{:S(2)}) async-start(), calls=%async_computation.8 | async-start | bytes 31457280 | tf_op jit(solution)/shard_map/all_gather | solution.py:98
  7.9 322.0 %all-gather.23.cloned.1.call-start = ((), (), s32[]{:S(2)}) async-start(), calls=%async_computation.11 | async-start | bytes 10485760 | tf_op jit(solution)/shard_map/all_gather | solution.py:100
  8.7 405.5 %all-gather.19.cloned.1.call-start = ((), (), s32[]{:S(2)}) async-start(), calls=%async_computation.9 | async-start | bytes 9437184 | tf_op jit(solution)/shard_map/all_gather | solution.py:128
  18.9 233.3 %copy-start.29 = (f32[4,1,512]{2,1,0:T(1,128)}, f32[4,1,512]{2,1,0:T(1,128)S(1)}, u32[]{:S(2)}) copy-start(f32[4,1,512]{2,1,0:T(1,128)S(1)} %convert_element_type.121) | copy-start | bytes 24580
  27.6 224.6 %copy-start.38 = (f32[4,1,512]{2,1,0:T(1,128)}, f32[4,1,512]{2,1,0:T(1,128)S(1)}, u32[]{:S(2)}) copy-start(f32[4,1,512]{2,1,0:T(1,128)S(1)} %convert_element_type.122) | copy-start | bytes 24580
  35.2 217.0 %copy-start.32 = (f32[256]{0:T(256)}, f32[256]{0:T(256)S(1)}, u32[]{:S(2)}) copy-start(f32[256]{0:T(256)S(1)} %broadcast_multiply_fusion.3) | copy-start | bytes 3076
  35.6 216.6 %copy-start.35 = (f32[256]{0:T(256)}, f32[256]{0:T(256)S(1)}, u32[]{:S(2)}) copy-start(f32[256]{0:T(256)S(1)} %add_rsqrt_fusion) | copy-start | bytes 3076
  256.1 241.2 %all-gather.21.cloned.1.call-start = ((), (), s32[]{:S(2)}) async-start(), calls=%async_computation.10 | async-start | bytes 9437184 | tf_op jit(solution)/shard_map/all_gather | solution.py:127
  269.3 60.6 copy-start.14
  270.6 68.6 %copy-start.5 = (bf16[8,256,256]{1,2,0:T(8,128)(2,1)}, bf16[8,256,256]{1,2,0:T(8,128)(2,1)S(1)}, u32[]{:S(2)}) copy-start(bf16[8,256,256]{1,2,0:T(8,128)(2,1)S(1)} %fusion.33) | copy-start | bytes 3145732
  414.2 83.1 %copy-start.13 = (bf16[8,256,256]{1,2,0:T(8,128)(2,1)S(1)}, bf16[8,256,256]{1,2,0:T(8,128)(2,1)}, u32[]{:S(2)}) copy-start(bf16[8,256,256]{1,2,0:T(8,128)(2,1)} %copy-done.5) | copy-start | bytes 3145732
  586.1 46.4 reduce-scatter.25.cloned.1.call-start
  598.4 71.3 %reduce-scatter.23.cloned.1.call-start = ((), (), s32[]{:S(2)}) async-start(), calls=%async_computation.26 | async-start | bytes 2359296 | tf_op jit(solution)/shard_map/while/body/eval_jaxpr/reduce_scatter | solution.py:224
  671.4 46.8 reduce-scatter.25.cloned.1.call-start
  683.7 72.1 %reduce-scatter.23.cloned.1.call-start = ((), (), s32[]{:S(2)}) async-start(), calls=%async_computation.26 | async-start | bytes 2359296 | tf_op jit(solution)/shard_map/while/body/eval_jaxpr/reduce_scatter | solution.py:224
  719.2 38.3 copy-start.7
  757.5 47.0 reduce-scatter.25.cloned.1.call-start
  769.8 71.9 %reduce-scatter.23.cloned.1.call-start = ((), (), s32[]{:S(2)}) async-start(), calls=%async_computation.26 | async-start | bytes 2359296 | tf_op jit(solution)/shard_map/while/body/eval_jaxpr/reduce_scatter | solution.py:224
  843.4 47.0 reduce-scatter.25.cloned.1.call-start
  855.7 72.0 %reduce-scatter.23.cloned.1.call-start = ((), (), s32[]{:S(2)}) async-start(), calls=%async_computation.26 | async-start | bytes 2359296 | tf_op jit(solution)/shard_map/while/body/eval_jaxpr/reduce_scatter | solution.py:224
  929.4 46.9 reduce-scatter.25.cloned.1.call-start
  941.6 71.9 %reduce-scatter.23.cloned.1.call-start = ((), (), s32[]{:S(2)}) async-start(), calls=%async_computation.26 | async-start | bytes 2359296 | tf_op jit(solution)/shard_map/while/body/eval_jaxpr/reduce_scatter | solution.py:224
  977.2 38.0 copy-start.7
  1015.3 46.9 reduce-scatter.25.cloned.1.call-start
  1027.6 72.0 %reduce-scatter.23.cloned.1.call-start = ((), (), s32[]{:S(2)}) async-start(), calls=%async_computation.26 | async-start | bytes 2359296 | tf_op jit(solution)/shard_map/while/body/eval_jaxpr/reduce_scatter | solution.py:224
  1063.2 38.1 copy-start.7
  1101.2 46.9 reduce-scatter.25.cloned.1.call-start
  1113.5 72.0 %reduce-scatter.23.cloned.1.call-start = ((), (), s32[]{:S(2)}) async-start(), calls=%async_computation.26 | async-start | bytes 2359296 | tf_op jit(solution)/shard_map/while/body/eval_jaxpr/reduce_scatter | solution.py:224
  1149.1 38.1 copy-start.7
  1187.2 46.9 reduce-scatter.25.cloned.1.call-start
  1199.5 72.0 %reduce-scatter.23.cloned.1.call-start = ((), (), s32[]{:S(2)}) async-start(), calls=%async_computation.26 | async-start | bytes 2359296 | tf_op jit(solution)/shard_map/while/body/eval_jaxpr/reduce_scatter | solution.py:224
  1273.1 211.8 %all-gather.25.cloned.1.call-start = ((), (), s32[]{:S(2)}) async-start(), calls=%async_computation.12 | async-start | bytes 28835840 | tf_op jit(solution)/shard_map/all_gather | solution.py:101
  1273.9 423.5 %all-gather.27.cloned.1.call-start = ((), (), s32[]{:S(2)}) async-start(), calls=%async_computation.13 | async-start | bytes 28835840 | tf_op jit(solution)/shard_map/all_gather | solution.py:102
  1274.6 635.1 %all-gather.29.cloned.1.call-start = ((), (), s32[]{:S(2)}) async-start(), calls=%async_computation.14 | async-start | bytes 28835840 | tf_op jit(solution)/shard_map/all_gather | solution.py:103
  1275.4 994.1 %reduce-scatter.13.cloned.1.call-start = ((), (), s32[]{:S(2)}) async-start(), calls=%async_computation.17 | async-start | bytes 17301504 | tf_op jit(solution)/shard_map/reduce_scatter | solution.py:56
  1287.8 1421.1 %reduce-scatter.11.cloned.1.call-start = ((), (), s32[]{:S(2)}) async-start(), calls=%async_computation.15 | async-start | bytes 51904512 | tf_op jit(solution)/shard_map/reduce_scatter | solution.py:55
  1319.4 165.6 %copy-start.30 = (f32[4,1,512]{2,1,0:T(1,128)S(1)}, f32[4,1,512]{2,1,0:T(1,128)}, u32[]{:S(2)}) copy-start(f32[4,1,512]{2,1,0:T(1,128)} %copy-done.29) | copy-start | bytes 24580
  1319.4 165.6 %copy-start.39 = (f32[4,1,512]{2,1,0:T(1,128)S(1)}, f32[4,1,512]{2,1,0:T(1,128)}, u32[]{:S(2)}) copy-start(f32[4,1,512]{2,1,0:T(1,128)} %copy-done.38) | copy-start | bytes 24580
  1319.4 2359.3 %reduce-scatter.19.cloned.1.call-start = ((), (), s32[]{:S(2)}) async-start(), calls=%async_computation.23 | async-start | bytes 47579136 | tf_op jit(solution)/shard_map/reduce_scatter | solution.py:55
  1499.6 410.1 %copy-start.16 = (bf16[1,256,2048]{2,1,0:T(8,128)(2,1)S(1)}, bf16[1,256,2048]{2,1,0:T(8,128)(2,1)}, u32[]{:S(2)}) copy-start(bf16[1,256,2048]{2,1,0:T(8,128)(2,1)} %param.17) | copy-start | bytes 3145732
  1960.0 2691.7 %reduce-scatter.17.cloned.1.call-start = ((), (), s32[]{:S(2)}) async-start(), calls=%async_computation.21 | async-start | bytes 47579136 | tf_op jit(solution)/shard_map/reduce_scatter | solution.py:56
  1980.3 3644.5 %reduce-scatter.15.cloned.1.call-start = ((), (), s32[]{:S(2)}) async-start(), calls=%async_computation.19 | async-start | bytes 47579136 | tf_op jit(solution)/shard_map/reduce_scatter | solution.py:55
  2000.3 3764.5 %reduce-scatter.21.cloned.1.call-start = ((), (), s32[]{:S(2)}) async-start(), calls=%async_computation.25 | async-start | bytes 1081344
  2045.8 3763.8 %all-gather.33.cloned.1.call-start = ((), (), s32[]{:S(2)}) async-start(), calls=%async_computation.18 | async-start | bytes 4718592 | tf_op jit(solution)/shard_map/all_gather | solution.py:60
  2269.5 3657.3 %all-gather.31.cloned.1.call-start = ((), (), s32[]{:S(2)}) async-start(), calls=%async_computation.16 | async-start | bytes 14155776 | tf_op jit(solution)/shard_map/all_gather | solution.py:59
  2709.0 3325.9 %all-gather.39.cloned.1.call-start = ((), (), s32[]{:S(2)}) async-start(), calls=%async_computation.24 | async-start | bytes 12976128 | tf_op jit(solution)/shard_map/all_gather | solution.py:59
  3678.8 2464.1 %all-gather.37.cloned.1.call-start = ((), (), s32[]{:S(2)}) async-start(), calls=%async_computation.22 | async-start | bytes 12976128 | tf_op jit(solution)/shard_map/all_gather | solution.py:60
  4651.7 1599.3 %all-gather.35.cloned.1.call-start = ((), (), s32[]{:S(2)}) async-start(), calls=%async_computation.20 | async-start | bytes 12976128 | tf_op jit(solution)/shard_map/all_gather | solution.py:59
  (75 other events, 653.7 us)
Sparse Core Ops, SparseCore 0:
  9.9 230.4 all-gather.16
  242.3 87.5 all-gather.22
  332.1 82.0 all-gather.18
  416.2 81.0 all-gather.20
  598.6 33.9 reduce-scatter.24
  635.4 34.3 reduce-scatter.22
  683.9 34.3 reduce-scatter.24
  721.2 34.5 reduce-scatter.22
  770.0 34.4 reduce-scatter.24
  807.3 34.3 reduce-scatter.22
  855.8 34.4 reduce-scatter.24
  893.2 34.4 reduce-scatter.22
  941.8 34.4 reduce-scatter.24
  979.1 34.4 reduce-scatter.22
  1027.7 34.4 reduce-scatter.24
  1065.0 34.4 reduce-scatter.22
  1113.7 34.4 reduce-scatter.24
  1151.0 34.4 reduce-scatter.22
  1199.6 34.4 reduce-scatter.24
  1237.0 34.4 reduce-scatter.22
  1275.8 209.0 all-gather.24
  1486.8 210.4 all-gather.26
  1699.2 210.4 all-gather.28
  1911.9 357.5 reduce-scatter.12
  2275.9 432.9 reduce-scatter.10
  2711.1 967.5 reduce-scatter.18
  3680.9 970.7 reduce-scatter.16
  4654.0 970.7 reduce-scatter.14
  5627.7 137.0 reduce-scatter.20
  5766.3 43.2 all-gather.32
  5811.4 115.3 all-gather.30
  5928.6 106.2 all-gather.38
  6036.5 106.3 all-gather.36
  6144.6 106.3 all-gather.34
where the time goes:
time: 6310 us; the launch traced here: 6300 us
  waiting for transfers between devices  5580 us (88%)
  matrix products  392 us (6%)
  local copies, waits for them, and re-layouts  182 us (3%)
    reduce_scatter x3, waiting for transfers between devices, reduce_pair(): lax.psum_scatter(first_term, ('ctx', 'fsdp'), scatter_dimension=0, tiled=...  2380 us
    reduce_scatter x2, waiting for transfers between devices, reduce_pair(): lax.psum_scatter(second_term, ('ctx', 'fsdp'), scatter_dimension=0, tiled...  1200 us
    all_gather x3, waiting for transfers between devices, reduce_pair(): lax.all_gather(parts[0], 'ctx', axis=0, tiled=True)  333 us
    reduce_scatter x8, waiting for transfers between devices, backward_group(): lax.psum_scatter(grad_key.reshape(key_count, head_span), 'ctx', scatter_d...  291 us
    dot_general x15, matrix products, matmul(): return jnp.dot(left, right, preferred_element_type=jnp.float32)  221 us
    all_gather x1, waiting for transfers between devices, shards(): lax.all_gather(w_qkv, 'fsdp', axis=0, tiled=True)  205 us
    all_gather x1, waiting for transfers between devices, shards(): lax.all_gather(w_down, 'fsdp', axis=0, tiled=True)  198 us
    all_gather x1, waiting for transfers between devices, shards(): lax.all_gather(w_up, 'fsdp', axis=0, tiled=True)  198 us
  transfers between devices with their start and end apart: 34, of which 34 were waited for; matrix products, arithmetic and copies ran while one was open for 6% of the time, Pallas kernels for 0%

commit v1 on v0

v1 whole, which is shorter than its diff:
```python
import functools

import jax
import jax.numpy as jnp
from jax import lax
from jax.experimental import pallas as pl
from jax.experimental.pallas import tpu as pltpu
from jax.sharding import PartitionSpec as P

HD = 64
ROT = 16
BLOCK = 128
CHUNK = 256
BF = jnp.bfloat16
F32 = jnp.float32
MASKED = -1e30


def matmul(left, right):
    return jnp.dot(left, right, preferred_element_type=F32)


def matmul_nt(left, right):
    return lax.dot_general(left, right, (((1,), (1,)), ((), ())), preferred_element_type=F32)


def matmul_tn(left, right):
    return lax.dot_general(left, right, (((0,), (0,)), ((), ())), preferred_element_type=F32)


def flip(values, axis, bit):
    count = lax.axis_size(axis)
    return lax.ppermute(values, axis, [(i, i ^ (1 << bit)) for i in range(count)])


def bits_of(count):
    bits = count.bit_length() - 1
    assert count == 1 << bits
    return bits


def gather_rows(values, axis, order):
    me = lax.axis_index(axis)
    count = lax.axis_size(axis)
    held = values[None]
    steps = [0]
    for bit in order:
        other = flip(held, axis, bit)
        held = jnp.concatenate([held, other], axis=0)
        steps = steps + [s ^ (1 << bit) for s in steps]
    rows = values.shape[0]
    out = jnp.zeros((count * rows,) + values.shape[1:], values.dtype)
    for place, step in enumerate(steps):
        out = lax.dynamic_update_slice_in_dim(out, held[place], (me ^ step) * rows, 0)
    return out


def gather_fsdp(values):
    bits = bits_of(lax.axis_size("fsdp"))
    half = values.shape[1] // 2 // 128 * 128
    first = list(range(bits))
    second = first[1:] + first[:1]
    return jnp.concatenate(
        [gather_rows(values[:, :half], "fsdp", first), gather_rows(values[:, half:], "fsdp", second)],
        axis=1,
    )


def scatter_rows(values, axis, order):
    me = lax.axis_index(axis)
    count = lax.axis_size(axis)
    bits = bits_of(count)
    rows = values.shape[0] // count
    held = values.reshape((2,) * bits + (rows,) + values.shape[1:])
    left = list(range(bits))
    for bit in order:
        at = len(left) - 1 - left.index(bit)
        mine = (me >> bit) & 1
        sent = lax.dynamic_index_in_dim(held, 1 - mine, at, keepdims=False).astype(BF)
        kept = lax.dynamic_index_in_dim(held, mine, at, keepdims=False)
        held = kept.astype(F32) + flip(sent, axis, bit).astype(F32)
        left.remove(bit)
    return held


def scatter_fsdp(values):
    bits = bits_of(lax.axis_size("fsdp"))
    half = values.shape[1] // 2 // 128 * 128
    first = list(range(bits))
    second = first[1:] + first[:1]
    return jnp.concatenate(
        [scatter_rows(values[:, :half], "fsdp", first), scatter_rows(values[:, half:], "fsdp", second)],
        axis=1,
    )


def gather_ctx(values):
    return lax.all_gather(values, "ctx", axis=0, tiled=True)


def scatter_ctx(values):
    return lax.psum_scatter(values.astype(BF), "ctx", scatter_dimension=0, tiled=True)


def attention_kernel(
    heads,
    slot_ref,
    low_ref,
    merged_ref,
    grad_mixed_ref,
    cos_ref,
    lead_ref,
    tail_ref,
    begin_ref,
    mixed_ref,
    grad_merged_ref,
    q_ref,
    k_ref,
    v_ref,
    g_ref,
    kt_ref,
    vt_ref,
    qm_ref,
    gm_ref,
    s_ref,
    d_ref,
    p_ref,
    ot_ref,
    dqt_ref,
    dk_ref,
    dv_ref,
):
    width = heads * HD
    tokens = merged_ref.shape[0]
    chunks = tokens // CHUNK
    blocks = tokens // BLOCK
    scale = HD ** (-0.5)

    def tables(rows):
        repeat = width // 128
        return tuple(
            jnp.concatenate([ref[rows, :]] * repeat, axis=1) for ref in (cos_ref, lead_ref, tail_ref)
        )

    def turn(values, rows, direction):
        cosine, lead, tail = tables(rows)
        ahead = pltpu.roll(values, width - ROT // 2, 1)
        behind = pltpu.roll(values, ROT // 2, 1)
        return values * cosine + direction * (ahead * lead + behind * tail)

    def rows_at(index, size):
        return pl.ds(pl.multiple_of(index * size, size), size)

    def prepare(block, carry):
        source = rows_at(slot_ref[block], BLOCK)
        target = rows_at(block, BLOCK)
        query = turn(merged_ref[source, 0:width], source, 1.0).astype(BF)
        key = turn(merged_ref[source, width : 2 * width], source, 1.0).astype(BF)
        value = merged_ref[source, 2 * width : 3 * width].astype(BF)
        q_ref[target, :] = query * jnp.asarray(scale, BF)
        k_ref[target, :] = key
        v_ref[target, :] = value
        kt_ref[:, target] = key.T
        vt_ref[:, target] = value.T
        g_ref[target, :] = grad_mixed_ref[source, :]
        dk_ref[target, :] = jnp.zeros((BLOCK, width), F32)
        dv_ref[target, :] = jnp.zeros((BLOCK, width), F32)
        return carry

    lax.fori_loop(0, blocks, prepare, 0)
    head_of = lax.broadcasted_iota(jnp.int32, (CHUNK, width), 1) // HD
    behind_by = lax.broadcasted_iota(jnp.int32, (CHUNK, CHUNK), 0) - lax.broadcasted_iota(
        jnp.int32, (CHUNK, CHUNK), 1
    )
    row_at = lax.broadcasted_iota(jnp.int32, (CHUNK, CHUNK), 0)

    def query_chunk(i, carry):
        here = rows_at(i, CHUNK)
        query = q_ref[here, :]
        grad = g_ref[here, :]
        zero = jnp.zeros_like(query)
        for h in range(heads):
            qm_ref[h * CHUNK : (h + 1) * CHUNK, :] = jnp.where(head_of == h, query, zero)
            gm_ref[h * CHUNK : (h + 1) * CHUNK, :] = jnp.where(head_of == h, grad, zero)
        ot_ref[...] = jnp.zeros_like(ot_ref)
        dqt_ref[...] = jnp.zeros_like(dqt_ref)
        low = low_ref[i]
        begin = begin_ref[i]

        def score(j, tops):
            there = rows_at(j, CHUNK)
            key = k_ref[there, :]
            allowed = (behind_by <= (i - j) * CHUNK) & (row_at >= begin - j * CHUNK)
            out = []
            for h in range(heads):
                s = matmul_nt(key, qm_ref[h * CHUNK : (h + 1) * CHUNK, :])
                s = jnp.where(allowed, s, MASKED)
                s_ref[h, there, :] = s
                out.append(jnp.maximum(tops[h], jnp.max(s, axis=0, keepdims=True)))
            return tuple(out)

        tops = lax.fori_loop(
            low, i + 1, score, tuple(jnp.full((1, CHUNK), MASKED, F32) for _ in range(heads))
        )

        def total(j, sums):
            there = rows_at(j, CHUNK)
            out = []
            for h in range(heads):
                e = jnp.exp(s_ref[h, there, :] - tops[h])
                s_ref[h, there, :] = e
                out.append(sums[h] + jnp.sum(e, axis=0, keepdims=True))
            return tuple(out)

        zeros = tuple(jnp.zeros((1, CHUNK), F32) for _ in range(heads))
        sums = lax.fori_loop(low, i + 1, total, zeros)
        shares = [1.0 / s for s in sums]

        def value_side(j, dots):
            there = rows_at(j, CHUNK)
            value = v_ref[there, :]
            out = []
            for h in range(heads):
                span = slice(h * HD, (h + 1) * HD)
                probs = s_ref[h, there, :] * shares[h]
                rounded = probs.astype(BF)
                p_ref[:, h * CHUNK : (h + 1) * CHUNK] = rounded
                ot_ref[span, :] += matmul(vt_ref[span, there], rounded)
                d = matmul_nt(value, gm_ref[h * CHUNK : (h + 1) * CHUNK, :])
                d_ref[h, there, :] = d
                out.append(dots[h] + jnp.sum(probs * d, axis=0, keepdims=True))
            dv_ref[there, :] += matmul(p_ref[...], gm_ref[...])
            return tuple(out)

        dots = lax.fori_loop(low, i + 1, value_side, zeros)

        def score_side(j, carry):
            there = rows_at(j, CHUNK)
            for h in range(heads):
                span = slice(h * HD, (h + 1) * HD)
                probs = s_ref[h, there, :] * shares[h]
                ds = (probs * (d_ref[h, there, :] - dots[h])).astype(BF)
                p_ref[:, h * CHUNK : (h + 1) * CHUNK] = ds
                dqt_ref[span, :] += matmul(kt_ref[span, there], ds)
            dk_ref[there, :] += matmul(p_ref[...], qm_ref[...])
            return carry

        lax.fori_loop(low, i + 1, score_side, 0)
        mixed = ot_ref[...].T.astype(BF)
        grad_query = dqt_ref[...].T * scale
        for part in range(CHUNK // BLOCK):
            target = rows_at(slot_ref[i * (CHUNK // BLOCK) + part], BLOCK)
            rows = slice(part * BLOCK, (part + 1) * BLOCK)
            mixed_ref[target, :] = mixed[rows]
            grad_merged_ref[target, 0:width] = turn(grad_query[rows], target, -1.0).astype(BF)
        return carry

    lax.fori_loop(0, chunks, query_chunk, 0)

    def finish(block, carry):
        source = rows_at(block, BLOCK)
        target = rows_at(slot_ref[block], BLOCK)
        grad_merged_ref[target, width : 2 * width] = turn(dk_ref[source, :], target, -1.0).astype(BF)
        grad_merged_ref[target, 2 * width : 3 * width] = dv_ref[source, :].astype(BF)
        return carry

    lax.fori_loop(0, blocks, finish, 0)


def attention(heads, slots, lows, merged, grad_mixed, tables, begins):
    tokens = merged.shape[0]
    width = heads * HD
    whole = pl.BlockSpec(memory_space=pltpu.VMEM)
    scalar = pl.BlockSpec(memory_space=pltpu.SMEM)
    return pl.pallas_call(
        functools.partial(attention_kernel, heads),
        out_shape=(
            jax.ShapeDtypeStruct((tokens, width), BF),
            jax.ShapeDtypeStruct((tokens, 3 * width), BF),
        ),
        in_specs=[scalar, scalar] + [whole] * 6,
        out_specs=(whole, whole),
        scratch_shapes=[
            pltpu.VMEM((tokens, width), BF),
            pltpu.VMEM((tokens, width), BF),
            pltpu.VMEM((tokens, width), BF),
            pltpu.VMEM((tokens, width), BF),
            pltpu.VMEM((width, tokens), BF),
            pltpu.VMEM((width, tokens), BF),
            pltpu.VMEM((heads * CHUNK, width), BF),
            pltpu.VMEM((heads * CHUNK, width), BF),
            pltpu.VMEM((heads, tokens, CHUNK), F32),
            pltpu.VMEM((heads, tokens, CHUNK), F32),
            pltpu.VMEM((CHUNK, heads * CHUNK), BF),
            pltpu.VMEM((width, CHUNK), F32),
            pltpu.VMEM((width, CHUNK), F32),
            pltpu.VMEM((tokens, width), F32),
            pltpu.VMEM((tokens, width), F32),
        ],
        compiler_params=pltpu.CompilerParams(vmem_limit_bytes=56 * 1024 * 1024),
        name="attention",
    )(slots, lows, merged, grad_mixed, *tables, begins)


def assemble_kernel(plan, source_ref, *targets):
    for target, pieces in zip(targets, plan):
        at = 0
        for part, offset, width in pieces:
            target[:, at : at + width] = source_ref[part, :, offset : offset + width].astype(F32)
            at += width


def assemble(gathered, plan):
    parts, rows, columns = gathered.shape
    step = 64
    widths = [sum(piece[2] for piece in pieces) for pieces in plan]
    return pl.pallas_call(
        functools.partial(assemble_kernel, plan),
        grid=(rows // step,),
        out_shape=tuple(jax.ShapeDtypeStruct((rows, w), F32) for w in widths),
        in_specs=[pl.BlockSpec((parts, step, columns), lambda i: (0, i, 0))],
        out_specs=tuple(pl.BlockSpec((step, w), lambda i: (i, 0)) for w in widths),
        compiler_params=pltpu.CompilerParams(vmem_limit_bytes=40 * 1024 * 1024),
        name="assemble",
    )(gathered)


def stream_places(order_row, length_row):
    places = (order_row[:, None] * BLOCK + jnp.arange(BLOCK, dtype=jnp.int32)[None, :]).reshape(-1)
    return places, stream_begins(places, length_row)


def stream_begins(places, length_row):
    ends = jnp.cumsum(length_row)
    starts = ends - length_row
    return jnp.max(jnp.where(starts[None, :] <= places[:, None], starts[None, :], 0), axis=1)


def rotary_tables(places, begins):
    entry = jnp.arange(128) % HD
    turned = entry < ROT
    index = jnp.where(entry < ROT // 2, entry, entry - ROT // 2)
    inverse = 1.0 / 10000.0 ** ((2 * index).astype(F32) / ROT)
    angles = (places - begins).astype(F32)[:, None] * jnp.where(turned, inverse, 0.0)[None, :]
    cosine, sine = jnp.cos(angles), jnp.sin(angles)
    lead = jnp.where((entry < ROT // 2)[None, :], -sine, 0.0)
    tail = jnp.where((turned & (entry >= ROT // 2))[None, :], sine, 0.0)
    return cosine, lead, tail


def take_columns(array, starts, width):
    return [lax.dynamic_slice_in_dim(array, s, width, 1) for s in starts]


def normalise(rows):
    centre = jnp.mean(rows, axis=1, keepdims=True)
    deviation = rows - centre
    inverse_std = lax.rsqrt(jnp.mean(deviation * deviation, axis=1, keepdims=True) + 1e-05)
    return deviation * inverse_std, inverse_std


def shards(
    hidden_in,
    out_grad,
    lengths,
    block_order,
    ln_gain,
    ln_bias,
    w_qkv,
    b_qkv,
    w_out,
    w_gate,
    w_up,
    w_down,
):
    parts = lax.axis_size("ctx")
    shard_count = lax.axis_size("fsdp")
    ctx_at = lax.axis_index("ctx")
    fsdp_at = lax.axis_index("fsdp")
    rows = hidden_in.shape[1]
    model = w_out.shape[1]
    hidden = w_gate.shape[1]
    tokens = rows * parts
    heads = model // HD // parts
    width = heads * HD
    shard_rows = w_qkv.shape[0]

    hidden_all = gather_ctx(hidden_in[0])
    grad_all = gather_ctx(out_grad[0])
    vectors = lax.all_gather(jnp.concatenate([ln_gain, ln_bias, b_qkv]), "fsdp", axis=0)
    gain_full = vectors[:, :shard_rows].reshape(-1).astype(F32)
    bias_full = vectors[:, shard_rows : 2 * shard_rows].reshape(-1).astype(F32)
    b_attn = vectors[:, 2 * shard_rows :].reshape(-1).astype(F32)

    spread = (model // HD) % (shard_count * parts) == 0
    pieces = shard_count if spread else 1
    head_span = model // pieces
    head_width = head_span // parts
    head_starts = [
        s * model + p * head_span + ctx_at * head_width for s in range(3) for p in range(pieces)
    ]
    unit_span = hidden // shard_count
    unit_width = unit_span // parts
    unit_starts = [p * unit_span + ctx_at * unit_width for p in range(shard_count)]

    w_pair_own = jnp.concatenate(
        take_columns(w_gate, unit_starts, unit_width) + take_columns(w_up, unit_starts, unit_width), axis=1
    )
    w_attn_own = jnp.concatenate(take_columns(w_qkv, head_starts, head_width), axis=1)
    b_attn_own = jnp.concatenate([lax.dynamic_slice_in_dim(b_attn, s, head_width, 0) for s in head_starts])
    w_down_own = lax.dynamic_slice_in_dim(w_down, ctx_at * unit_width, unit_width, 0)
    w_attn = gather_fsdp(w_attn_own)
    w_pair = gather_fsdp(w_pair_own)
    w_lower = gather_fsdp(w_down_own)
    if spread:
        w_proj = gather_fsdp(lax.dynamic_slice_in_dim(w_out, ctx_at * head_width, head_width, 0))
    else:
        w_proj = lax.dynamic_slice_in_dim(
            lax.all_gather(w_out, "fsdp", axis=0, tiled=True), ctx_at * width, width, 0
        )

    order_row = block_order[0]
    places, begins = stream_places(order_row, lengths[0])
    tables = rotary_tables(places, begins)
    blocks = order_row.shape[0]
    slots = jnp.sum(
        jnp.where(
            order_row[None, :] == jnp.arange(blocks, dtype=jnp.int32)[:, None],
            jnp.arange(blocks, dtype=jnp.int32)[None, :],
            0,
        ),
        axis=1,
    ).astype(jnp.int32)
    stream_starts = stream_begins(jnp.arange(tokens, dtype=jnp.int32), lengths[0]).astype(jnp.int32)
    lows = stream_starts[::CHUNK] // CHUNK
    stream_starts = stream_starts.reshape(tokens // CHUNK, 1, CHUNK)

    normal_all, _ = normalise(hidden_all.astype(F32))
    normed = (normal_all * gain_full + bias_full).astype(BF)
    merged = matmul(normed, w_attn) + b_attn_own
    pair = matmul(normed, w_pair)
    units = shard_count * unit_width
    gating, rising = pair[:, :units], pair[:, units:]
    sigma = jax.nn.sigmoid(gating)
    silu_gate = gating * sigma
    activated = (silu_gate * rising).astype(BF)

    grad_mixed = matmul_nt(grad_all, w_proj).astype(BF)
    grad_act = matmul_nt(grad_all, w_lower)
    grad_pair = jnp.concatenate(
        [
            (grad_act * rising * sigma * (1.0 + gating * (1.0 - sigma))).astype(BF),
            (grad_act * silu_gate).astype(BF),
        ],
        axis=1,
    )
    pair_sum = scatter_fsdp(matmul_tn(normed, grad_pair))
    down_sum = scatter_fsdp(matmul_tn(activated, grad_all))
    pair_all = gather_ctx(pair_sum.astype(BF)[None])
    down_all = gather_ctx(down_sum.astype(BF))

    mixed, grad_merged = attention(heads, slots, lows, merged, grad_mixed, tables, stream_starts)

    out_rows = scatter_ctx(matmul(mixed, w_proj) + matmul(activated, w_lower))
    float_in = hidden_in[0].astype(F32)
    output = (float_in + out_rows.astype(F32)).astype(BF)[None]

    grad_normed = scatter_ctx(matmul_nt(grad_pair, w_pair) + matmul_nt(grad_merged, w_attn)).astype(F32)

    attn_sum = scatter_fsdp(matmul_tn(normed, grad_merged))
    attn_all = gather_ctx(attn_sum.astype(BF)[None])
    proj_part = matmul_tn(mixed, grad_all)
    if spread:
        proj_all = gather_ctx(scatter_fsdp(proj_part).astype(BF)).astype(F32)
    else:
        proj_all = lax.dynamic_slice_in_dim(
            gather_ctx(lax.psum(proj_part, "fsdp")), fsdp_at * shard_rows, shard_rows, 0
        )

    pair_plan = [
        [
            (c, side * units + p * unit_width, unit_width)
            for p in range(shard_count)
            for c in range(parts)
        ]
        for side in range(2)
    ]
    attn_plan = [
        [
            (c, (s * pieces + p) * head_width, head_width)
            for s in range(3)
            for p in range(pieces)
            for c in range(parts)
        ]
    ]
    grad_gate_w, grad_up_w = assemble(pair_all, pair_plan)
    (grad_attn_w,) = assemble(attn_all, attn_plan)

    normal_hat, inverse_std = normalise(float_in)
    merged_term = jnp.sum(grad_merged, axis=0, dtype=F32)
    merged_terms = jnp.sum(lax.all_gather(merged_term, ("ctx", "fsdp"), axis=0).reshape(parts, shard_count, -1), axis=1)
    merged_full = jnp.moveaxis(merged_terms.reshape(parts, 3, pieces, head_width), 0, 2).reshape(-1)
    b_rows = b_qkv.shape[0]
    grad_b = lax.dynamic_slice_in_dim(merged_full, fsdp_at * b_rows, b_rows, 0)
    terms = jnp.stack([jnp.sum(grad_normed * normal_hat, axis=0), jnp.sum(grad_normed, axis=0)])
    terms = jnp.sum(lax.all_gather(terms, ("ctx", "fsdp"), axis=0), axis=0)
    terms = lax.dynamic_slice_in_dim(terms, fsdp_at * shard_rows, shard_rows, 1)

    grad_hat = grad_normed * gain_full
    grad_in = out_grad[0].astype(F32) + inverse_std * (
        grad_hat
        - jnp.mean(grad_hat, axis=1, keepdims=True)
        - normal_hat * jnp.mean(grad_hat * normal_hat, axis=1, keepdims=True)
    )
    return (
        output,
        grad_in.astype(BF)[None],
        terms[0],
        terms[1],
        grad_attn_w,
        grad_b,
        proj_all,
        grad_gate_w,
        grad_up_w,
        down_all.astype(F32),
    )


def solution(mesh):
    return jax.shard_map(
        shards,
        mesh=mesh,
        in_specs=(
            P("fsdp", "ctx", None),
            P("fsdp", "ctx", None),
            P("fsdp", None),
            P("fsdp", None),
            P("fsdp"),
            P("fsdp"),
            P("fsdp", None),
            P("fsdp"),
            P("fsdp", None),
            P("fsdp", None),
            P("fsdp", None),
            P("fsdp", None),
        ),
        out_specs=(
            P("fsdp", "ctx", None),
            P("fsdp", "ctx", None),
            P("fsdp"),
            P("fsdp"),
            P("fsdp", None),
            P("fsdp"),
            P("fsdp", None),
            P("fsdp", None),
            P("fsdp", None),
            P("fsdp", None),
        ),
        check_vma=False,
    )
```

time: 6310 us -> 786 us (0.12)
  waiting for transfers between devices: 5580 us -> 233 us
  matrix products: 392 us -> 150 us
  blocking collectives: 39 us -> 165 us
  local copies, waits for them, and re-layouts: 182 us -> 61.8 us
  Pallas kernels: 0 us -> 63.8 us
    reduce_scatter x21 -> x2, waiting for transfers between devices: 4020 us -> 0.01 us  [scatter_ctx(): lax.psum_scatter(values.astype(BF), 'ctx', scatter_dimension=0, tiled=True)]
    all_gather x12 -> x6, waiting for transfers between devices: 1440 us -> 76.6 us  [gather_ctx(): return lax.all_gather(values, 'ctx', axis=0, tiled=True)]
    dot_general x71 -> x12, matrix products: 392 us -> 150 us  [the longest x4 56.1 us: matmul_nt(): lax.dot_general(left, right, (((1,), (1,)), ((), ())), preferred_element_...]
    ppermute x0 -> x32, waiting for transfers between devices: none -> 156 us  [flip(): return lax.ppermute(values, axis, [(i, i ^ 1 << bit) for i in range(count)])]
    all_gather x4 -> x3, blocking collectives: 39 us -> 165 us  [the longest x1 78.7 us: shards(): terms = jnp.sum(lax.all_gather(terms, ('ctx', 'fsdp'), axis=0), axis=0)]
    unnamed x19 -> x8, waiting for transfers between devices: 122 us -> 0.8 us
    pallas_call x0 -> x3, Pallas kernels: none -> 63.8 us  [the longest x1 48 us: attention(): pl.pallas_call(functools.partial(attention_kernel, heads), out_shape=(jax...]
  transfers between devices with their start and end apart: 34 -> 40, of which waited for: 34 -> 22; matrix products, arithmetic and copies ran while one was open for 6% -> 30% of each run, Pallas kernels for 0% -> 1%
where the time goes in v1:
time: 786 us; the launch traced here: 781 us
  waiting for transfers between devices  233 us (30%)
  blocking collectives  165 us (21%)
  matrix products  150 us (19%)
  Pallas kernels  63.8 us (8%)
  local copies, waits for them, and re-layouts  61.8 us (8%)
  other arithmetic  55.9 us (7%)
  starting transfers between devices  35.1 us (4%)
  between operations  15.7 us (2%)
    ppermute x32, waiting for transfers between devices, flip(): return lax.ppermute(values, axis, [(i, i ^ 1 << bit) for i in range(count)])  156 us
    all_gather x1, blocking collectives, shards(): terms = jnp.sum(lax.all_gather(terms, ('ctx', 'fsdp'), axis=0), axis=0)  78.7 us
    all_gather x6, waiting for transfers between devices, gather_ctx(): return lax.all_gather(values, 'ctx', axis=0, tiled=True)  76.6 us
    all_gather x1, blocking collectives, shards(): lax.all_gather(merged_term, ('ctx', 'fsdp'), axis=0)  67.4 us
    dot_general x4, matrix products, matmul_nt(): lax.dot_general(left, right, (((1,), (1,)), ((), ())), preferred_element_...  56.1 us
    dot_general x4, matrix products, matmul(): return jnp.dot(left, right, preferred_element_type=F32)  51.6 us
    pallas_call x1, Pallas kernels, attention(): pl.pallas_call(functools.partial(attention_kernel, heads), out_shape=(jax...  48 us
    dot_general x4, matrix products, matmul_tn(): lax.dot_general(left, right, (((0,), (0,)), ((), ())), preferred_element_...  42.1 us
  transfers between devices with their start and end apart: 40, of which 22 were waited for; matrix products, arithmetic and copies ran while one was open for 30% of the time, Pallas kernels for 1%

profile of v1, /device:TPU:0, one launch (start us, length us, event | category | flops | bytes accessed | tf_op | source)
XLA Modules:
  0.0 780.5 jit_solution(10376243920837758542)
XLA Ops:
  10.4 3.0 collective-permute-start.2
  18.5 4.1 constant_dynamic-slice_fusion.1
  30.5 19.2 %all-gather.5 = bf16[4,1,2560]{2,1,0:T(2,128)(2,1)S(1)} all-gather(bf16[1,1,2560]{2,1,0:T(2,128)(2,1)S(1)} %reshape.275), channel_id=3, replica_groups=mesh['ctx'=8,'fsdp'=4] {'fsdp'}, dimensions={0}, use_global_device_ids=true | all-gather | bytes 25600 | tf_op jit(solution)/shard_map/all_gather | solution.py:390
  60.8 6.3 fusion.48
  78.3 16.9 %collective-permute-done.12 = bf16[1,176,1024]{2,1,0:T(8,128)(2,1)S(1)} collective-permute-done((bf16[1,176,1024]{2,1,0:T(8,128)(2,1)S(1)}, bf16[1,176,1024]{2,1,0:T(8,128)(2,1)S(1)}, u32[]{:S(2)}, u32[]{:S(2)}) %collective-permute-start.12) | collective-permute-done | bytes 360480 | tf_op jit(solution)/shard_map/ppermute | solution.py:33
  96.0 5.7 collective-permute-done.7
  103.5 6.7 collective-permute-done.5
  122.2 7.1 collective-permute-done.15
  130.9 15.2 %collective-permute-done.3 = bf16[2,512,384]{2,1,0:T(8,128)(2,1)S(1)} collective-permute-done((bf16[2,512,384]{2,1,0:T(8,128)(2,1)S(1)}, bf16[2,512,384]{2,1,0:T(8,128)(2,1)S(1)}, u32[]{:S(2)}, u32[]{:S(2)}) %collective-permute-start.3) | collective-permute-done | bytes 786464 | tf_op jit(solution)/shard_map/ppermute | solution.py:33
  147.5 20.9 %collective-permute-done.9 = bf16[2,512,640]{2,1,0:T(8,128)(2,1)S(1)} collective-permute-done((bf16[2,512,640]{2,1,0:T(8,128)(2,1)S(1)}, bf16[2,512,640]{2,1,0:T(8,128)(2,1)S(1)}, u32[]{:S(2)}, u32[]{:S(2)}) %collective-permute-start.9) | collective-permute-done | bytes 1310752 | tf_op jit(solution)/shard_map/ppermute | solution.py:33
  172.3 4.7 convert_reduce_fusion
  178.1 2.3 fusion.3
  180.4 3.7 fusion.6
  184.1 3.4 copy-done.4
  187.5 8.7 %broadcast_add_fusion.merged_ref = f32[2048,768]{1,0:T(8,128)} fusion(f32[768]{0:T(1024)S(1)} %concatenate.103, bf16[2048,2048]{1,0:T(8,128)(2,1)S(1)} %fusion.6, bf16[2048,384]{1,0:T(8,128)(2,1)S(1)} %copy-done.15, bf16[2048,384]{1,0:T(8,128)(2,1)S(1)} %copy-done.19), kind=kOutput, calls=%fused_computation.39 | convolution fusion | flops 6450315264 | bytes 17828864 | tf_op jit(solution)/shard_map/dot_general | solution.py:20
  196.3 6.9 fusion.33.grad_mixed_ref
  203.2 48.0 %attention.1 = (bf16[2048,256]{1,0:T(8,128)(2,1)}, bf16[2048,768]{1,0:T(8,128)(2,1)}) custom-call(s32[16]{0:T(128)} %select_reduce_fusion.slot_ref, s32[8]{0:T(128)} %and_select_fusion.1.low_ref, f32[2048,768]{1,0:T(8,128)} %broadcast_add_fusion.merged_ref, bf16[2048,256]{1,0:T(8,128)(2,1)} %fusion.33.grad_mixed_ref, f32[2048,128]{1,0:T(8,128)} %get-tuple-element.83.cos_ref, ...), custom_call_target="tpu_custom_call" | custom-call | tf_op jit(solution)/shard_map/attention/pallas_call | solution.py:275
  251.2 6.1 fusion.9
  260.9 19.0 %fusion.21 = f32[2048,1408]{0,1:T(8,128)} fusion(bf16[2048,2048]{1,0:T(8,128)(2,1)} %copy-done.4, bf16[2048,768]{1,0:T(8,128)(2,1)} %fusion.59, bf16[2048,640]{1,0:T(8,128)(2,1)} %fusion.69), kind=kOutput, calls=%fused_computation.32 | convolution fusion | flops 11822694400 | bytes 25690112 | tf_op jit(solution)/shard_map/dot_general | solution.py:20
  280.0 15.7 %fusion.17 = (bf16[2048,704]{0,1:T(8,128)(2,1)}, bf16[2048,704]{0,1:T(8,128)(2,1)}, bf16[2048,704]{0,1:T(8,128)(2,1)}) fusion(f32[2048,1408]{0,1:T(8,128)} %fusion.21, bf16[1,2048,2048]{2,1,0:T(8,128)(2,1)} %all-gather.25.cloned.1.call-done, bf16[704,1024]{1,0:T(8,128)(2,1)} %fusion.81, bf16[704,1024]{1,0:T(8,128)(2,1)S(1)} %copy-done.21), kind=kOutput, calls=%fused_computation.26 | convolution fusion | flops 5932974080 | bytes 31457280 | tf_op jit(solution)/shard_map/dot_general | solution.py:24
  304.3 9.8 %fusion.7 = f32[704,2048]{1,0:T(8,128)S(1)} fusion(bf16[2048,704]{0,1:T(8,128)(2,1)} %get-tuple-element.26, bf16[1,2048,2048]{2,1,0:T(8,128)(2,1)} %all-gather.25.cloned.1.call-done), kind=kOutput, calls=%fused_computation.11 | convolution fusion | flops 5905580032 | bytes 17039360 | tf_op jit(solution)/shard_map/dot_general | solution.py:28
  317.6 12.9 %collective-permute-done.30 = bf16[2,176,1024]{2,1,0:T(8,128)(2,1)S(1)} collective-permute-done((bf16[2,176,1024]{2,1,0:T(8,128)(2,1)S(1)}, bf16[2,176,1024]{2,1,0:T(8,128)(2,1)S(1)}, u32[]{:S(2)}, u32[]{:S(2)}) %collective-permute-start.30) | collective-permute-done | bytes 720928 | tf_op jit(solution)/shard_map/ppermute | solution.py:33
  333.2 5.0 collective-permute-done.31
  341.1 9.5 %fusion.113 = f32[2048,768]{1,0:T(8,128)S(1)} fusion(bf16[2048,2048]{1,0:T(8,128)(2,1)} %copy-done.4, bf16[2048,768]{1,0:T(8,128)(2,1)S(1)} %copy-done.8), kind=kOutput, calls=%fused_computation.265 | convolution fusion | flops 6442450944 | bytes 17825792 | tf_op jit(solution)/shard_map/dot_general | solution.py:28
  353.4 13.9 %collective-permute-done.18 = bf16[2,512,384]{2,1,0:T(8,128)(2,1)S(1)} collective-permute-done((bf16[2,512,384]{2,1,0:T(8,128)(2,1)S(1)}, bf16[2,512,384]{2,1,0:T(8,128)(2,1)S(1)}, u32[]{:S(2)}, u32[]{:S(2)}) %collective-permute-start.18) | collective-permute-done | bytes 786464 | tf_op jit(solution)/shard_map/ppermute | solution.py:33
  370.1 5.3 collective-permute-done.19
  377.5 11.8 %fusion.44 = f32[2048,2048]{1,0:T(8,128)} fusion(bf16[2048,768]{1,0:T(8,128)(2,1)S(1)} %copy-done.8, bf16[2048,384]{1,0:T(8,128)(2,1)} %copy-done.14, bf16[2048,384]{1,0:T(8,128)(2,1)} %copy-done.18), kind=kOutput, calls=%fused_computation.63 | convolution fusion | flops 6448742400 | bytes 23068672 | tf_op jit(solution)/shard_map/dot_general | solution.py:24
  389.2 21.6 %add_convert_fusion = bf16[2048,2048]{1,0:T(8,128)(2,1)} fusion(f32[2048,2048]{1,0:T(8,128)} %fusion.44, bf16[2048,704]{0,1:T(8,128)(2,1)} %get-tuple-element.25, bf16[2048,704]{0,1:T(8,128)(2,1)} %get-tuple-element.24, bf16[2048,768]{1,0:T(8,128)(2,1)} %fusion.59, bf16[2048,640]{1,0:T(8,128)(2,1)} %fusion.69), kind=kOutput, calls=%fused_computation.9 | convolution fusion | flops 11842617344 | bytes 36700160 | tf_op jit(solution)/shard_map/dot_general | solution.py:24
  412.5 12.1 %fusion.45 = f32[2048,2048]{1,0:T(8,128)} fusion(bf16[2048,704]{0,1:T(8,128)(2,1)} %get-tuple-element.26, bf16[704,1024]{1,0:T(8,128)(2,1)} %fusion.81, bf16[704,1024]{1,0:T(8,128)(2,1)S(1)} %copy-done.22), kind=kOutput, calls=%fused_computation.64 | convolution fusion | flops 5911347200 | bytes 22544384 | tf_op jit(solution)/shard_map/dot_general | solution.py:20
  424.6 11.8 %add_convert_fusion.1 = bf16[2048,2048]{1,0:T(8,128)(2,1)} fusion(f32[2048,2048]{1,0:T(8,128)} %fusion.45, bf16[2048,256]{1,0:T(8,128)(2,1)S(1)} %copy-done.5, bf16[256,1024]{1,0:T(8,128)(2,1)S(1)} %copy-done.11, bf16[256,1024]{1,0:T(8,128)(2,1)} %fusion.93), kind=kOutput, calls=%fused_computation.10 | convolution fusion | flops 2157969408 | bytes 27262976 | tf_op jit(solution)/shard_map/dot_general | solution.py:20
  438.3 16.7 %fusion.20 = f32[2048,1408]{1,0:T(8,128)S(1)} fusion(bf16[2048,2048]{1,0:T(8,128)(2,1)} %copy-done.4, bf16[2048,704]{0,1:T(8,128)(2,1)} %get-tuple-element.25, bf16[2048,704]{0,1:T(8,128)(2,1)S(1)} %copy-done.34), kind=kOutput, calls=%fused_computation.31 | convolution fusion | flops 11822694400 | bytes 25690112 | tf_op jit(solution)/shard_map/dot_general | solution.py:28
  458.6 18.1 %collective-permute-done.24 = bf16[2,512,640]{2,1,0:T(8,128)(2,1)S(1)} collective-permute-done((bf16[2,512,640]{2,1,0:T(8,128)(2,1)S(1)}, bf16[2,512,640]{2,1,0:T(8,128)(2,1)S(1)}, u32[]{:S(2)}, u32[]{:S(2)}) %collective-permute-start.24) | collective-permute-done | bytes 1310752 | tf_op jit(solution)/shard_map/ppermute | solution.py:33
  477.1 2.6 collective-permute-start.25
  479.7 8.5 %collective-permute-done.26 = bf16[2,512,768]{2,1,0:T(8,128)(2,1)S(1)} collective-permute-done((bf16[2,512,768]{2,1,0:T(8,128)(2,1)S(1)}, bf16[2,512,768]{2,1,0:T(8,128)(2,1)S(1)}, u32[]{:S(2)}, u32[]{:S(2)}) %collective-permute-start.26) | collective-permute-done | bytes 1572896 | tf_op jit(solution)/shard_map/ppermute | solution.py:33
  489.2 6.0 collective-permute-done.25
  495.3 5.3 collective-permute-done.27
  503.2 2.4 convert_reduce_fusion.1
  505.6 67.4 %all-gather.7 = f32[32,1,768]{2,1,0:T(1,128)S(1)} all-gather(f32[1,1,768]{2,1,0:T(1,128)S(1)} %reshape.279), channel_id=6, replica_groups=mesh['ctx'=8,'fsdp'=4] {'ctx','fsdp'}, dimensions={0}, use_global_device_ids=true | all-gather | bytes 101376 | tf_op jit(solution)/shard_map/all_gather | solution.py:501
  574.2 4.1 convert_element_type.303
  578.4 8.7 %convert_element_type.328 = f32[1408,2048]{1,0:T(8,128)} convert(bf16[1408,2048]{1,0:T(8,128)(2,1)} %all-gather.21.cloned.1.call-done) | non-fusion elementwise | flops 2883584 | bytes 17301504 | tf_op jit(solution)/shard_map/convert_element_type | solution.py:525
  587.1 2.8 copy-done.1
  589.9 6.8 assemble.2
  596.8 2.4 fusion.43
  599.2 78.7 %all-gather.6 = f32[32,2,2048]{2,1,0:T(2,128)} all-gather(f32[1,2,2048]{2,1,0:T(2,128)S(1)} %maximum_bitcast_fusion), channel_id=5, replica_groups=mesh['ctx'=8,'fsdp'=4] {'ctx','fsdp'}, dimensions={0}, use_global_device_ids=true | all-gather | bytes 540672 | tf_op jit(solution)/shard_map/all_gather | solution.py:506
  679.8 3.7 fusion.54
  683.5 76.6 %all-gather.19.cloned.1.call-done.source_ref = bf16[8,512,1408]{2,1,0:T(8,128)(2,1)} async-done(((bf16[1,512,1408]{2,1,0:T(8,128)(2,1)}), bf16[8,512,1408]{2,1,0:T(8,128)(2,1)}) %all-gather.19.cloned.1.call-update) | async-done | bytes 11534352 | tf_op jit(solution)/shard_map/all_gather | solution.py:98
  760.0 4.3 copy-done
  764.3 9.0 %assemble.3 = (f32[512,5632]{1,0:T(8,128)}, f32[512,5632]{1,0:T(8,128)}) custom-call(bf16[8,512,1408]{2,1,0:T(8,128)(2,1)S(1)} %copy-done), custom_call_target="tpu_custom_call" | custom-call | tf_op jit(solution)/shard_map/assemble/pallas_call | solution.py:317
  (271 shorter events, 103.4 us)
Async XLA Ops:
  7.2 165.1 %all-gather.23.cloned.1.call-start = ((), (), s32[]{:S(2)}) async-start(), calls=%async_computation.8 | async-start | bytes 9437184 | tf_op jit(solution)/shard_map/all_gather | solution.py:98
  7.9 188.3 %all-gather.25.cloned.1.call-start = ((), (), s32[]{:S(2)}) async-start(), calls=%async_computation.9 | async-start | bytes 9437184 | tf_op jit(solution)/shard_map/all_gather | solution.py:98
  10.4 101.0 %collective-permute-start.2 = (bf16[1,512,384]{2,1,0:T(8,128)(2,1)S(1)}, bf16[1,512,384]{2,1,0:T(8,128)(2,1)}, u32[]{:S(2)}, u32[]{:S(2)}) collective-permute-start(bf16[1,512,384]{2,1,0:T(8,128)(2,1)S(1)} %bitcast.342), channel_id=1, source_target_pairs={{0,2},{1,3},{2,0},{3,1},{4,6},{5,7},{6,4},{7,5},{8,10},{9,11},{10,... | collective-permute-start | bytes 1179656 | tf_op jit(solution)/shard_map/ppermute | solution.py:33
  13.9 101.7 %collective-permute-start = (bf16[1,512,384]{2,1,0:T(8,128)(2,1)S(1)}, bf16[1,512,384]{2,1,0:T(8,128)(2,1)}, u32[]{:S(2)}, u32[]{:S(2)}) collective-permute-start(bf16[1,512,384]{2,1,0:T(8,128)(2,1)S(1)} %bitcast.344), channel_id=1, source_target_pairs={{0,1},{1,0},{2,3},{3,2},{4,5},{5,4},{6,7},{7,6},{8,9},{9,8},{10,11... | collective-permute-start | bytes 1179656 | tf_op jit(solution)/shard_map/ppermute | solution.py:33
  18.0 50.5 %collective-permute-start.6 = (bf16[1,64,1024]{2,1,0:T(8,128)(2,1)}, bf16[1,64,1024]{2,1,0:T(8,128)(2,1)}, u32[]{:S(2)}, u32[]{:S(2)}) collective-permute-start(bf16[1,64,1024]{2,1,0:T(8,128)(2,1)} %get-tuple-element.57), channel_id=1, source_target_pairs={{0,2},{1,3},{2,0},{3,1},{4,6},{5,7},{6,4},{7,5},{8,10},{9,11},{10,... | collective-permute-start | bytes 393224 | tf_op jit(solution)/shard_map/ppermute | solution.py:33
  18.5 54.2 %collective-permute-start.4 = (bf16[1,64,1024]{2,1,0:T(8,128)(2,1)}, bf16[1,64,1024]{2,1,0:T(8,128)(2,1)S(1)}, u32[]{:S(2)}, u32[]{:S(2)}) collective-permute-start(bf16[1,64,1024]{2,1,0:T(8,128)(2,1)} %get-tuple-element.56), channel_id=1, source_target_pairs={{0,1},{1,0},{2,3},{3,2},{4,5},{5,4},{6,7},{7,6},{8,9},{9,8},{10,11... | collective-permute-start | bytes 393224 | tf_op jit(solution)/shard_map/ppermute | solution.py:33
  27.8 93.3 %collective-permute-start.10 = (bf16[1,512,768]{2,1,0:T(8,128)(2,1)S(1)}, bf16[1,512,768]{2,1,0:T(8,128)(2,1)S(1)}, u32[]{:S(2)}, u32[]{:S(2)}) collective-permute-start(bf16[1,512,768]{2,1,0:T(8,128)(2,1)S(1)} %get-tuple-element.63), channel_id=1, source_target_pairs={{0,2},{1,3},{2,0},{3,1},{4,6},{5,7},{6,4},{7,5},{8,10},{9,11},{10,... | collective-permute-start | bytes 2359304 | tf_op jit(solution)/shard_map/ppermute | solution.py:33
  29.8 544.4 %all-gather.17.cloned.1.call-start = ((), (), s32[]{:S(2)}) async-start(), calls=%async_computation.5 | async-start | bytes 2359296 | tf_op jit(solution)/shard_map/all_gather | solution.py:98
  30.3 24.8 %copy-start.28 = (s32[2048]{0:T(1024)}, s32[2048]{0:T(1024)S(1)}, u32[]{:S(2)}) copy-start(s32[2048]{0:T(1024)S(1)} %get-tuple-element.23) | copy-start | bytes 24580
  49.8 130.6 %copy-start.26 = (f32[1,4,4,128]{3,1,2,0:T(4,128)}, f32[1,4,4,128]{3,1,2,0:T(4,128)S(1)}, u32[]{:S(2)}) copy-start(f32[1,4,4,128]{3,1,2,0:T(4,128)S(1)} %copy.49) | copy-start | bytes 24580
  68.5 7.5 collective-permute-start.14
  72.7 45.2 %collective-permute-start.8 = (bf16[1,512,640]{2,1,0:T(8,128)(2,1)S(1)}, bf16[1,512,640]{2,1,0:T(8,128)(2,1)S(1)}, u32[]{:S(2)}, u32[]{:S(2)}) collective-permute-start(bf16[1,512,640]{2,1,0:T(8,128)(2,1)S(1)} %get-tuple-element.61), channel_id=1, source_target_pairs={{0,1},{1,0},{2,3},{3,2},{4,5},{5,4},{6,7},{7,6},{8,9},{9,8},{10,11... | collective-permute-start | bytes 1966088 | tf_op jit(solution)/shard_map/ppermute | solution.py:33
  74.3 39.2 %copy-start.13 = (bf16[2048,384]{1,0:T(8,128)(2,1)S(1)}, bf16[2048,384]{1,0:T(8,128)(2,1)}, u32[]{:S(2)}) copy-start(bf16[2048,384]{1,0:T(8,128)(2,1)} %copy-done.12) | copy-start | bytes 4718596
  76.0 19.3 %collective-permute-start.12 = (bf16[1,176,1024]{2,1,0:T(8,128)(2,1)S(1)}, bf16[1,176,1024]{2,1,0:T(8,128)(2,1)S(1)}, u32[]{:S(2)}, u32[]{:S(2)}) collective-permute-start(bf16[1,176,1024]{2,1,0:T(8,128)(2,1)S(1)} %get-tuple-element.43), channel_id=1, source_target_pairs={{0,1},{1,0},{2,3},{3,2},{4,5},{5,4},{6,7},{7,6},{8,9},{9,8},{10,11... | collective-permute-start | bytes 1081352 | tf_op jit(solution)/shard_map/ppermute | solution.py:33
  95.3 6.4 collective-permute-start.7
  101.7 8.5 %collective-permute-start.5 = (bf16[2,64,1024]{2,1,0:T(8,128)(2,1)S(1)}, bf16[2,64,1024]{2,1,0:T(8,128)(2,1)S(1)}, u32[]{:S(2)}, u32[]{:S(2)}) collective-permute-start(bf16[2,64,1024]{2,1,0:T(8,128)(2,1)S(1)} %pad_maximum_fusion.27), channel_id=1, source_target_pairs={{0,2},{1,3},{2,0},{3,1},{4,6},{5,7},{6,4},{7,5},{8,10},{9,11},{10,... | collective-permute-start | bytes 786440 | tf_op jit(solution)/shard_map/ppermute | solution.py:33
  110.1 19.1 %collective-permute-start.15 = (bf16[2,176,1024]{2,1,0:T(8,128)(2,1)S(1)}, bf16[2,176,1024]{2,1,0:T(8,128)(2,1)S(1)}, u32[]{:S(2)}, u32[]{:S(2)}) collective-permute-start(bf16[2,176,1024]{2,1,0:T(8,128)(2,1)S(1)} %pad_maximum_fusion.20), channel_id=1, source_target_pairs={{0,1},{1,0},{2,3},{3,2},{4,5},{5,4},{6,7},{7,6},{8,9},{9,8},{10,11... | collective-permute-start | bytes 2162696 | tf_op jit(solution)/shard_map/ppermute | solution.py:33
  111.5 19.3 %collective-permute-start.13 = (bf16[2,176,1024]{2,1,0:T(8,128)(2,1)S(1)}, bf16[2,176,1024]{2,1,0:T(8,128)(2,1)S(1)}, u32[]{:S(2)}, u32[]{:S(2)}) collective-permute-start(bf16[2,176,1024]{2,1,0:T(8,128)(2,1)S(1)} %pad_maximum_fusion.19), channel_id=1, source_target_pairs={{0,2},{1,3},{2,0},{3,1},{4,6},{5,7},{6,4},{7,5},{8,10},{9,11},{10,... | collective-permute-start | bytes 2162696 | tf_op jit(solution)/shard_map/ppermute | solution.py:33
  115.6 30.5 %collective-permute-start.3 = (bf16[2,512,384]{2,1,0:T(8,128)(2,1)S(1)}, bf16[2,512,384]{2,1,0:T(8,128)(2,1)S(1)}, u32[]{:S(2)}, u32[]{:S(2)}) collective-permute-start(bf16[2,512,384]{2,1,0:T(8,128)(2,1)S(1)} %pad_maximum_fusion.17), channel_id=1, source_target_pairs={{0,1},{1,0},{2,3},{3,2},{4,5},{5,4},{6,7},{7,6},{8,9},{9,8},{10,11... | collective-permute-start | bytes 2359304 | tf_op jit(solution)/shard_map/ppermute | solution.py:33
  117.9 29.5 %collective-permute-start.1 = (bf16[2,512,384]{2,1,0:T(8,128)(2,1)S(1)}, bf16[2,512,384]{2,1,0:T(8,128)(2,1)S(1)}, u32[]{:S(2)}, u32[]{:S(2)}) collective-permute-start(bf16[2,512,384]{2,1,0:T(8,128)(2,1)S(1)} %pad_maximum_fusion.16), channel_id=1, source_target_pairs={{0,2},{1,3},{2,0},{3,1},{4,6},{5,7},{6,4},{7,5},{8,10},{9,11},{10,... | collective-permute-start | bytes 2359304 | tf_op jit(solution)/shard_map/ppermute | solution.py:33
  121.1 47.4 %collective-permute-start.9 = (bf16[2,512,640]{2,1,0:T(8,128)(2,1)S(1)}, bf16[2,512,640]{2,1,0:T(8,128)(2,1)S(1)}, u32[]{:S(2)}, u32[]{:S(2)}) collective-permute-start(bf16[2,512,640]{2,1,0:T(8,128)(2,1)S(1)} %pad_maximum_fusion.14), channel_id=1, source_target_pairs={{0,2},{1,3},{2,0},{3,1},{4,6},{5,7},{6,4},{7,5},{8,10},{9,11},{10,... | collective-permute-start | bytes 3932168 | tf_op jit(solution)/shard_map/ppermute | solution.py:33
  129.2 41.2 %collective-permute-start.11 = (bf16[2,512,768]{2,1,0:T(8,128)(2,1)S(1)}, bf16[2,512,768]{2,1,0:T(8,128)(2,1)S(1)}, u32[]{:S(2)}, u32[]{:S(2)}) collective-permute-start(bf16[2,512,768]{2,1,0:T(8,128)(2,1)S(1)} %pad_maximum_fusion.12), channel_id=1, source_target_pairs={{0,1},{1,0},{2,3},{3,2},{4,5},{5,4},{6,7},{7,6},{8,9},{9,8},{10,11... | collective-permute-start | bytes 4718600 | tf_op jit(solution)/shard_map/ppermute | solution.py:33
  130.8 39.4 %copy-start.20 = (bf16[704,1024]{1,0:T(8,128)(2,1)}, bf16[704,1024]{1,0:T(8,128)(2,1)S(1)}, u32[]{:S(2)}) copy-start(bf16[704,1024]{1,0:T(8,128)(2,1)S(1)} %fusion.83) | copy-start | bytes 4325380
  146.2 25.1 %copy-start.14 = (bf16[2048,384]{1,0:T(8,128)(2,1)}, bf16[2048,384]{1,0:T(8,128)(2,1)S(1)}, u32[]{:S(2)}) copy-start(bf16[2048,384]{1,0:T(8,128)(2,1)S(1)} %fusion.75) | copy-start | bytes 4718596
  147.5 22.8 %copy-start.18 = (bf16[2048,384]{1,0:T(8,128)(2,1)}, bf16[2048,384]{1,0:T(8,128)(2,1)S(1)}, u32[]{:S(2)}) copy-start(bf16[2048,384]{1,0:T(8,128)(2,1)S(1)} %fusion.77) | copy-start | bytes 4718596
  258.2 37.5 %collective-permute-start.22 = (bf16[2,64,1024]{2,1,0:T(8,128)(2,1)}, bf16[2,64,1024]{2,1,0:T(8,128)(2,1)}, u32[]{:S(2)}, u32[]{:S(2)}) collective-permute-start(bf16[2,64,1024]{2,1,0:T(8,128)(2,1)} %fusion.85), channel_id=1, source_target_pairs={{0,2},{1,3},{2,0},{3,1},{4,6},{5,7},{6,4},{7,5},{8,10},{9,11},{10,... | collective-permute-start | bytes 786440 | tf_op jit(solution)/shard_map/ppermute | solution.py:33
  259.5 37.9 %collective-permute-start.20 = (bf16[2,64,1024]{2,1,0:T(8,128)(2,1)}, bf16[2,64,1024]{2,1,0:T(8,128)(2,1)}, u32[]{:S(2)}, u32[]{:S(2)}) collective-permute-start(bf16[2,64,1024]{2,1,0:T(8,128)(2,1)} %fusion.86), channel_id=1, source_target_pairs={{0,1},{1,0},{2,3},{3,2},{4,5},{5,4},{6,7},{7,6},{8,9},{9,8},{10,11... | collective-permute-start | bytes 786440 | tf_op jit(solution)/shard_map/ppermute | solution.py:33
  296.8 5.0 collective-permute-start.23
  298.4 5.0 collective-permute-start.21
  304.2 274.1 %all-gather.21.cloned.1.call-start = ((), (), s32[]{:S(2)}) async-start(), calls=%async_computation.7 | async-start | bytes 6488064 | tf_op jit(solution)/shard_map/all_gather | solution.py:98
  315.2 15.2 %collective-permute-start.30 = (bf16[2,176,1024]{2,1,0:T(8,128)(2,1)S(1)}, bf16[2,176,1024]{2,1,0:T(8,128)(2,1)S(1)}, u32[]{:S(2)}, u32[]{:S(2)}) collective-permute-start(bf16[2,176,1024]{2,1,0:T(8,128)(2,1)S(1)} %fusion.63), channel_id=1, source_target_pairs={{0,2},{1,3},{2,0},{3,1},{4,6},{5,7},{6,4},{7,5},{8,10},{9,11},{10,... | collective-permute-start | bytes 2162696 | tf_op jit(solution)/shard_map/ppermute | solution.py:33
  316.9 15.3 %collective-permute-start.28 = (bf16[2,176,1024]{2,1,0:T(8,128)(2,1)S(1)}, bf16[2,176,1024]{2,1,0:T(8,128)(2,1)S(1)}, u32[]{:S(2)}, u32[]{:S(2)}) collective-permute-start(bf16[2,176,1024]{2,1,0:T(8,128)(2,1)S(1)} %fusion.64), channel_id=1, source_target_pairs={{0,1},{1,0},{2,3},{3,2},{4,5},{5,4},{6,7},{7,6},{8,9},{9,8},{10,11... | collective-permute-start | bytes 2162696 | tf_op jit(solution)/shard_map/ppermute | solution.py:33
  330.7 7.5 collective-permute-start.31
  332.5 7.5 collective-permute-start.29
  341.1 246.0 %all-gather.15.cloned.1.call-start = ((), (), s32[]{:S(2)}) async-start(), calls=%async_computation.4 | async-start | bytes 7077888 | tf_op jit(solution)/shard_map/all_gather | solution.py:98
  351.1 16.2 %collective-permute-start.18 = (bf16[2,512,384]{2,1,0:T(8,128)(2,1)S(1)}, bf16[2,512,384]{2,1,0:T(8,128)(2,1)S(1)}, u32[]{:S(2)}, u32[]{:S(2)}) collective-permute-start(bf16[2,512,384]{2,1,0:T(8,128)(2,1)S(1)} %fusion.56), channel_id=1, source_target_pairs={{0,2},{1,3},{2,0},{3,1},{4,6},{5,7},{6,4},{7,5},{8,10},{9,11},{10,... | collective-permute-start | bytes 2359304 | tf_op jit(solution)/shard_map/ppermute | solution.py:33
  351.9 16.4 %collective-permute-start.16 = (bf16[2,512,384]{2,1,0:T(8,128)(2,1)S(1)}, bf16[2,512,384]{2,1,0:T(8,128)(2,1)S(1)}, u32[]{:S(2)}, u32[]{:S(2)}) collective-permute-start(bf16[2,512,384]{2,1,0:T(8,128)(2,1)S(1)} %fusion.55), channel_id=1, source_target_pairs={{0,1},{1,0},{2,3},{3,2},{4,5},{5,4},{6,7},{7,6},{8,9},{9,8},{10,11... | collective-permute-start | bytes 2359304 | tf_op jit(solution)/shard_map/ppermute | solution.py:33
  367.6 7.8 %collective-permute-start.19 = (bf16[512,384]{1,0:T(8,128)(2,1)S(1)}, bf16[512,384]{1,0:T(8,128)(2,1)S(1)}, u32[]{:S(2)}, u32[]{:S(2)}) collective-permute-start(bf16[512,384]{1,0:T(8,128)(2,1)S(1)} %fusion.72), channel_id=1, source_target_pairs={{0,1},{1,0},{2,3},{3,2},{4,5},{5,4},{6,7},{7,6},{8,9},{9,8},{10,11... | collective-permute-start | bytes 1179656 | tf_op jit(solution)/shard_map/ppermute | solution.py:33
  368.5 7.8 %collective-permute-start.17 = (bf16[512,384]{1,0:T(8,128)(2,1)S(1)}, bf16[512,384]{1,0:T(8,128)(2,1)S(1)}, u32[]{:S(2)}, u32[]{:S(2)}) collective-permute-start(bf16[512,384]{1,0:T(8,128)(2,1)S(1)} %fusion.71), channel_id=1, source_target_pairs={{0,2},{1,3},{2,0},{3,1},{4,6},{5,7},{6,4},{7,5},{8,10},{9,11},{10,... | collective-permute-start | bytes 1179656 | tf_op jit(solution)/shard_map/ppermute | solution.py:33
  377.4 219.3 %reduce-scatter.5.cloned.1.call-start = ((), (), s32[]{:S(2)}) async-start(), calls=%async_computation.3 | async-start | bytes 9437184 | tf_op jit(solution)/shard_map/reduce_scatter | solution.py:102
  410.9 268.9 %reduce-scatter.3.cloned.1.call-start = ((), (), s32[]{:S(2)}) async-start(), calls=%async_computation.2 | async-start | bytes 9437184 | tf_op jit(solution)/shard_map/reduce_scatter | solution.py:102
  436.5 323.6 %all-gather.19.cloned.1.call-start = ((), (), s32[]{:S(2)}) async-start(), calls=%async_computation.6 | async-start | bytes 12976128 | tf_op jit(solution)/shard_map/all_gather | solution.py:98
  455.5 21.2 %collective-permute-start.24 = (bf16[2,512,640]{2,1,0:T(8,128)(2,1)S(1)}, bf16[2,512,640]{2,1,0:T(8,128)(2,1)S(1)}, u32[]{:S(2)}, u32[]{:S(2)}) collective-permute-start(bf16[2,512,640]{2,1,0:T(8,128)(2,1)S(1)} %fusion.50), channel_id=1, source_target_pairs={{0,1},{1,0},{2,3},{3,2},{4,5},{5,4},{6,7},{7,6},{8,9},{9,8},{10,11... | collective-permute-start | bytes 3932168 | tf_op jit(solution)/shard_map/ppermute | solution.py:33
  457.6 30.6 %collective-permute-start.26 = (bf16[2,512,768]{2,1,0:T(8,128)(2,1)S(1)}, bf16[2,512,768]{2,1,0:T(8,128)(2,1)S(1)}, u32[]{:S(2)}, u32[]{:S(2)}) collective-permute-start(bf16[2,512,768]{2,1,0:T(8,128)(2,1)S(1)} %fusion.46), channel_id=1, source_target_pairs={{0,2},{1,3},{2,0},{3,1},{4,6},{5,7},{6,4},{7,5},{8,10},{9,11},{10,... | collective-permute-start | bytes 4718600 | tf_op jit(solution)/shard_map/ppermute | solution.py:33
  477.1 18.1 %collective-permute-start.25 = (bf16[512,640]{1,0:T(8,128)(2,1)S(1)}, bf16[512,640]{1,0:T(8,128)(2,1)S(1)}, u32[]{:S(2)}, u32[]{:S(2)}) collective-permute-start(bf16[512,640]{1,0:T(8,128)(2,1)S(1)} %fusion.67), channel_id=1, source_target_pairs={{0,2},{1,3},{2,0},{3,1},{4,6},{5,7},{6,4},{7,5},{8,10},{9,11},{10,... | collective-permute-start | bytes 1966088 | tf_op jit(solution)/shard_map/ppermute | solution.py:33
  488.6 12.1 %collective-permute-start.27 = (bf16[512,768]{1,0:T(8,128)(2,1)S(1)}, bf16[512,768]{1,0:T(8,128)(2,1)S(1)}, u32[]{:S(2)}, u32[]{:S(2)}) collective-permute-start(bf16[512,768]{1,0:T(8,128)(2,1)S(1)} %fusion.57), channel_id=1, source_target_pairs={{0,1},{1,0},{2,3},{3,2},{4,5},{5,4},{6,7},{7,6},{8,9},{9,8},{10,11... | collective-permute-start | bytes 2359304 | tf_op jit(solution)/shard_map/ppermute | solution.py:33
  596.7 83.0 %copy-start.6 = (bf16[1,256,2048]{2,1,0:T(8,128)(2,1)S(1)}, bf16[1,256,2048]{2,1,0:T(8,128)(2,1)}, u32[]{:S(2)}) copy-start(bf16[1,256,2048]{2,1,0:T(8,128)(2,1)} %param.13) | copy-start | bytes 3145732
  596.8 83.0 %copy-start.7 = (bf16[256,2048]{1,0:T(8,128)(2,1)S(1)}, bf16[256,2048]{1,0:T(8,128)(2,1)}, u32[]{:S(2)}) copy-start(bf16[256,2048]{1,0:T(8,128)(2,1)} %reduce-scatter.5.cloned.1.call-done) | copy-start | bytes 3145732
  (27 other events, 175.6 us)
Sparse Core Ops, SparseCore 0:
  9.6 84.7 all-gather.22
  96.0 80.5 all-gather.24
  304.4 29.4 all-gather.16
  341.2 60.7 all-gather.20
  404.0 63.4 all-gather.14
  470.2 88.6 reduce-scatter.4
  561.3 90.0 reduce-scatter.2
  653.6 106.3 all-gather.18

commit v2 on v1

v2 whole, which is shorter than its diff:
```python
import functools

import jax
import jax.numpy as jnp
from jax import lax
from jax.experimental import pallas as pl
from jax.experimental.pallas import tpu as pltpu
from jax.sharding import PartitionSpec as P

HD = 64
ROT = 16
BLOCK = 128
CHUNK = 256
BF = jnp.bfloat16
F32 = jnp.float32
MASKED = -1e30


def matmul(left, right):
    return jnp.dot(left, right, preferred_element_type=F32)


def matmul_nt(left, right):
    return lax.dot_general(left, right, (((1,), (1,)), ((), ())), preferred_element_type=F32)


def matmul_tn(left, right):
    return lax.dot_general(left, right, (((0,), (0,)), ((), ())), preferred_element_type=F32)


def flip(values, axis, bit):
    count = lax.axis_size(axis)
    return lax.ppermute(values, axis, [(i, i ^ (1 << bit)) for i in range(count)])


def bits_of(count):
    bits = count.bit_length() - 1
    assert count == 1 << bits
    return bits


def gather_rows(values, axis, order):
    me = lax.axis_index(axis)
    count = lax.axis_size(axis)
    held = values[None]
    steps = [0]
    for bit in order:
        other = flip(held, axis, bit)
        held = jnp.concatenate([held, other], axis=0)
        steps = steps + [s ^ (1 << bit) for s in steps]
    rows = values.shape[0]
    out = jnp.zeros((count * rows,) + values.shape[1:], values.dtype)
    for place, step in enumerate(steps):
        out = lax.dynamic_update_slice_in_dim(out, held[place], (me ^ step) * rows, 0)
    return out


def placed(pieces, places, total):
    out = jnp.zeros((total,) + pieces[0].shape[1:], pieces[0].dtype)
    for piece, place in zip(pieces, places):
        out = lax.dynamic_update_slice_in_dim(out, piece, place, 0)
    return out


def gather_first(values):
    if lax.axis_size("fsdp") != 4:
        return [gather_rows(values, "fsdp", list(range(bits_of(lax.axis_size("fsdp")))))]
    return [flip(values, "fsdp", 0), flip(values, "fsdp", 1)]


def gather_second(values, first):
    if lax.axis_size("fsdp") != 4:
        return []
    half = values.shape[0] // 2 // 16 * 16
    return [flip(first[0][:half], "fsdp", 1), flip(first[1][half:], "fsdp", 0)]


def gathered_pieces(values, first, second, rows):
    count = lax.axis_size("fsdp")
    shard = values.shape[0]
    if count != 4:
        return [(first[0], i * shard, rows, i * rows) for i in range(count)]
    me = lax.axis_index("fsdp")
    half = shard // 2 // 16 * 16
    return [
        (values, 0, rows, me * rows),
        (first[0], 0, rows, (me ^ 1) * rows),
        (first[1], 0, rows, (me ^ 2) * rows),
        (second[0], 0, half, (me ^ 3) * rows),
        (second[1], 0, rows - half, (me ^ 3) * rows + half),
    ]


def gathered_rest(values, first, second, rows):
    count = lax.axis_size("fsdp")
    shard = values.shape[0]
    if count != 4:
        return first[0].reshape(count, shard, -1)[:, rows:]
    me = lax.axis_index("fsdp")
    half = shard // 2 // 16 * 16
    tails = [values[rows:], first[0][rows:], first[1][rows:], second[1][rows - half :]]
    return placed([t[None] for t in tails], [me, me ^ 1, me ^ 2, me ^ 3], count)


def others_of(values, axis, stride, count):
    size = lax.axis_size(axis)
    digit = lax.axis_index(axis) // stride % count

    def moved(i, by):
        at = i // stride % count
        return i + ((at + by) % count - at) * stride

    return [lax.ppermute(values, axis, [(i, moved(i, by)) for i in range(size)]) for by in range(1, count)], digit


def sum_of(values, others, digit):
    count = len(others) + 1
    out = jnp.zeros((count,) + values.shape, values.dtype)
    for by, piece in enumerate([values] + others):
        out = lax.dynamic_update_slice_in_dim(out, piece[None], (digit + count - by) % count, 0)
    total = out[0]
    for at in range(1, count):
        total = total + out[at]
    return total


def scatter_rows(values, axis, order):
    me = lax.axis_index(axis)
    count = lax.axis_size(axis)
    bits = bits_of(count)
    rows = values.shape[0] // count
    held = values.reshape((2,) * bits + (rows,) + values.shape[1:])
    left = list(range(bits))
    for bit in order:
        at = len(left) - 1 - left.index(bit)
        mine = (me >> bit) & 1
        sent = lax.dynamic_index_in_dim(held, 1 - mine, at, keepdims=False).astype(BF)
        kept = lax.dynamic_index_in_dim(held, mine, at, keepdims=False)
        held = kept.astype(F32) + flip(sent, axis, bit).astype(F32)
        left.remove(bit)
    return held


def fsdp_block(part, index):
    rows = part.shape[0] // lax.axis_size("fsdp")
    return lax.dynamic_slice_in_dim(part, index * rows, rows, 0)


def halves(part):
    half = part.shape[1] // 2 // 128 * 128
    return part[:, :half], part[:, half:]


def scatter_first(sides):
    if lax.axis_size("fsdp") != 4:
        return [scatter_rows(part, "fsdp", list(range(bits_of(lax.axis_size("fsdp"))))) for part in sides]
    me = lax.axis_index("fsdp")
    return [
        flip(fsdp_block(sides[1], me ^ 3), "fsdp", 0),
        flip(fsdp_block(sides[0], me ^ 3), "fsdp", 1),
        flip(fsdp_block(sides[1], me ^ 1), "fsdp", 0),
        flip(fsdp_block(sides[0], me ^ 2), "fsdp", 1),
    ]


def scatter_second(sides, first):
    if lax.axis_size("fsdp") != 4:
        return []
    me = lax.axis_index("fsdp")
    across = fsdp_block(sides[0], me ^ 1).astype(F32) + first[1].astype(F32)
    along = fsdp_block(sides[1], me ^ 2).astype(F32) + first[0].astype(F32)
    return [flip(across.astype(BF), "fsdp", 0), flip(along.astype(BF), "fsdp", 1)]


def scatter_last(sides, first, second):
    if lax.axis_size("fsdp") != 4:
        return first[0].astype(BF), first[1].astype(BF)
    me = lax.axis_index("fsdp")
    left = fsdp_block(sides[0], me).astype(F32) + first[3].astype(F32) + second[0].astype(F32)
    right = fsdp_block(sides[1], me).astype(F32) + first[2].astype(F32) + second[1].astype(F32)
    return left.astype(BF), right.astype(BF)


def gather_ctx(values):
    return lax.all_gather(values, "ctx", axis=0, tiled=True)


def scatter_ctx(values):
    return lax.psum_scatter(values, "ctx", scatter_dimension=0, tiled=True)


def split_cores(part):
    parts = lax.axis_size("ctx")
    core = lax.axis_index("ctx") % 2
    blocks = part.reshape(parts // 2, 2, part.shape[0] // parts, part.shape[1])
    return [lax.dynamic_index_in_dim(blocks, k, 1, keepdims=False) for k in (core, 1 - core)]


def scatter_places(values):
    places, rows, columns = values.shape
    lines = [[2 * p + k for p in range(places)] for k in range(2)]
    return lax.psum_scatter(
        values.reshape(places * rows, columns), "ctx", scatter_dimension=0, axis_index_groups=lines, tiled=True
    )


def nothing_kernel(*refs):
    return None


def tie(values, after):
    anywhere = pl.BlockSpec(memory_space=pl.ANY)
    return pl.pallas_call(
        nothing_kernel,
        out_shape=tuple(jax.ShapeDtypeStruct(v.shape, v.dtype) for v in values),
        in_specs=[anywhere] * (len(values) + len(after)),
        out_specs=tuple([anywhere] * len(values)),
        input_output_aliases={i: i for i in range(len(values))},
        name="tie",
    )(*values, *after)


def stage(*groups):
    leaves, tree = jax.tree.flatten(groups)
    return jax.tree.unflatten(tree, tie(leaves, []))


def rows_at(index, size):
    return pl.ds(pl.multiple_of(index * size, size), size)


def turn(values, tables, rows, direction):
    width = values.shape[1]
    cosine, lead, tail = (jnp.concatenate([ref[rows, :]] * (width // 128), axis=1) for ref in tables)
    ahead = pltpu.roll(values, width - ROT // 2, 1)
    behind = pltpu.roll(values, ROT // 2, 1)
    return values * cosine + direction * (ahead * lead + behind * tail)


def split_heads(target, values, heads):
    head_of = lax.broadcasted_iota(jnp.int32, values.shape, 1) // HD
    for h in range(heads):
        target[h * CHUNK : (h + 1) * CHUNK, :] = jnp.where(head_of == h, values, jnp.zeros_like(values))


def visible(i, j, begin):
    key_at = lax.broadcasted_iota(jnp.int32, (CHUNK, CHUNK), 0)
    query_at = lax.broadcasted_iota(jnp.int32, (CHUNK, CHUNK), 1)
    return (key_at - query_at <= (i - j) * CHUNK) & (key_at >= begin - j * CHUNK)


def forward_kernel(
    heads,
    slot_ref,
    low_ref,
    merged_ref,
    cos_ref,
    lead_ref,
    tail_ref,
    begin_ref,
    mixed_ref,
    q_ref,
    k_ref,
    v_ref,
    total_ref,
    ot_ref,
    vt_ref,
    qm_ref,
    s_ref,
):
    width = heads * HD
    tokens = merged_ref.shape[0]
    tables = (cos_ref, lead_ref, tail_ref)

    def prepare(block, carry):
        source = rows_at(slot_ref[block], BLOCK)
        target = rows_at(block, BLOCK)
        query = turn(merged_ref[source, 0:width], tables, source, 1.0).astype(BF)
        key = turn(merged_ref[source, width : 2 * width], tables, source, 1.0).astype(BF)
        value = merged_ref[source, 2 * width : 3 * width].astype(BF)
        q_ref[target, :] = query * jnp.asarray(HD ** (-0.5), BF)
        k_ref[target, :] = key
        v_ref[target, :] = value
        vt_ref[:, target] = value.T
        return carry

    lax.fori_loop(0, tokens // BLOCK, prepare, 0)

    def query_chunk(i, carry):
        here = rows_at(i, CHUNK)
        split_heads(qm_ref, q_ref[here, :], heads)
        ot_ref[:, here] = jnp.zeros((width, CHUNK), F32)
        low = low_ref[i]
        begin = begin_ref[i]

        def score(j, tops):
            there = rows_at(j, CHUNK)
            key = k_ref[there, :]
            allowed = visible(i, j, begin)
            out = []
            for h in range(heads):
                s = matmul_nt(key, qm_ref[h * CHUNK : (h + 1) * CHUNK, :])
                s = jnp.where(allowed, s, MASKED)
                s_ref[h, there, :] = s
                out.append(jnp.maximum(tops[h], jnp.max(s, axis=0, keepdims=True)))
            return tuple(out)

        tops = lax.fori_loop(
            low, i + 1, score, tuple(jnp.full((1, CHUNK), MASKED, F32) for _ in range(heads))
        )

        def value_side(j, sums):
            there = rows_at(j, CHUNK)
            out = []
            for h in range(heads):
                span = slice(h * HD, (h + 1) * HD)
                e = jnp.exp(s_ref[h, there, :] - tops[h])
                out.append(sums[h] + jnp.sum(e, axis=0, keepdims=True))
                ot_ref[span, here] += matmul(vt_ref[span, there], e.astype(BF))
            return tuple(out)

        sums = lax.fori_loop(low, i + 1, value_side, tuple(jnp.zeros((1, CHUNK), F32) for _ in range(heads)))
        for h in range(heads):
            span = slice(h * HD, (h + 1) * HD)
            ot_ref[span, here] = ot_ref[span, here] * (1.0 / sums[h])
            total_ref[i, h : h + 1, :] = tops[h] + jnp.log(sums[h])
        mixed = ot_ref[:, here].T.astype(BF)
        for part in range(CHUNK // BLOCK):
            target = rows_at(slot_ref[i * (CHUNK // BLOCK) + part], BLOCK)
            mixed_ref[target, :] = mixed[part * BLOCK : (part + 1) * BLOCK]
        return carry

    lax.fori_loop(0, tokens // CHUNK, query_chunk, 0)


def backward_kernel(
    heads,
    slot_ref,
    low_ref,
    q_ref,
    k_ref,
    v_ref,
    total_ref,
    ot_ref,
    grad_mixed_ref,
    cos_ref,
    lead_ref,
    tail_ref,
    begin_ref,
    grad_merged_ref,
    kt_ref,
    qm_ref,
    gm_ref,
    p_ref,
    ds_ref,
    dqt_ref,
    dk_ref,
    dv_ref,
):
    width = heads * HD
    tokens = q_ref.shape[0]
    tables = (cos_ref, lead_ref, tail_ref)

    def prepare(block, carry):
        here = rows_at(block, BLOCK)
        kt_ref[:, here] = k_ref[here, :].T
        dk_ref[here, :] = jnp.zeros((BLOCK, width), F32)
        dv_ref[here, :] = jnp.zeros((BLOCK, width), F32)
        return carry

    lax.fori_loop(0, tokens // BLOCK, prepare, 0)

    def query_chunk(i, carry):
        here = rows_at(i, CHUNK)
        targets = [rows_at(slot_ref[i * (CHUNK // BLOCK) + part], BLOCK) for part in range(CHUNK // BLOCK)]
        grad = jnp.concatenate([grad_mixed_ref[target, :] for target in targets], axis=0)
        split_heads(qm_ref, q_ref[here, :], heads)
        split_heads(gm_ref, grad, heads)
        dqt_ref[...] = jnp.zeros_like(dqt_ref)
        product = grad.T.astype(F32) * ot_ref[:, here]
        dots = [jnp.sum(product[h * HD : (h + 1) * HD], axis=0, keepdims=True) for h in range(heads)]
        totals = [total_ref[i, h : h + 1, :] for h in range(heads)]
        begin = begin_ref[i]

        def key_chunk(j, carry):
            there = rows_at(j, CHUNK)
            key = k_ref[there, :]
            value = v_ref[there, :]
            allowed = visible(i, j, begin)
            for h in range(heads):
                span = slice(h * HD, (h + 1) * HD)
                part = slice(h * CHUNK, (h + 1) * CHUNK)
                s = matmul_nt(key, qm_ref[part, :])
                probs = jnp.exp(jnp.where(allowed, s, MASKED) - totals[h])
                p_ref[:, part] = probs.astype(BF)
                ds = (probs * (matmul_nt(value, gm_ref[part, :]) - dots[h])).astype(BF)
                ds_ref[:, part] = ds
                dqt_ref[span, :] += matmul(kt_ref[span, there], ds)
            dv_ref[there, :] += matmul(p_ref[...], gm_ref[...])
            dk_ref[there, :] += matmul(ds_ref[...], qm_ref[...])
            return carry

        lax.fori_loop(low_ref[i], i + 1, key_chunk, 0)
        grad_query = dqt_ref[...].T * HD ** (-0.5)
        for part, target in enumerate(targets):
            rows = slice(part * BLOCK, (part + 1) * BLOCK)
            grad_merged_ref[target, 0:width] = turn(grad_query[rows], tables, target, -1.0).astype(BF)
        return carry

    lax.fori_loop(0, tokens // CHUNK, query_chunk, 0)

    def finish(block, carry):
        source = rows_at(block, BLOCK)
        target = rows_at(slot_ref[block], BLOCK)
        grad_merged_ref[target, width : 2 * width] = turn(dk_ref[source, :], tables, target, -1.0).astype(BF)
        grad_merged_ref[target, 2 * width : 3 * width] = dv_ref[source, :].astype(BF)
        return carry

    lax.fori_loop(0, tokens // BLOCK, finish, 0)


WHOLE = pl.BlockSpec(memory_space=pltpu.VMEM)
SCALAR = pl.BlockSpec(memory_space=pltpu.SMEM)
ANYWHERE = pl.BlockSpec(memory_space=pl.ANY)


def attention_forward(heads, slots, lows, merged, tables, begins):
    tokens = merged.shape[0]
    width = heads * HD
    rows = jax.ShapeDtypeStruct((tokens, width), BF)
    return pl.pallas_call(
        functools.partial(forward_kernel, heads),
        out_shape=(
            rows,
            rows,
            rows,
            rows,
            jax.ShapeDtypeStruct((tokens // CHUNK, heads, CHUNK), F32),
            jax.ShapeDtypeStruct((width, tokens), F32),
        ),
        in_specs=[SCALAR, SCALAR] + [WHOLE] * 5,
        out_specs=(WHOLE,) * 6,
        scratch_shapes=[
            pltpu.VMEM((width, tokens), BF),
            pltpu.VMEM((heads * CHUNK, width), BF),
            pltpu.VMEM((heads, tokens, CHUNK), F32),
        ],
        compiler_params=pltpu.CompilerParams(vmem_limit_bytes=48 * 1024 * 1024),
        cost_estimate=pl.CostEstimate(flops=25_000_000_000, transcendentals=0, bytes_accessed=0),
        name="attention_forward",
    )(slots, lows, merged, *tables, begins)


def attention_backward(heads, slots, lows, kept, grad_mixed, tables, begins):
    tokens, width = grad_mixed.shape
    return pl.pallas_call(
        functools.partial(backward_kernel, heads),
        out_shape=jax.ShapeDtypeStruct((tokens, 3 * width), BF),
        in_specs=[SCALAR, SCALAR] + [WHOLE] * 10,
        out_specs=WHOLE,
        scratch_shapes=[
            pltpu.VMEM((width, tokens), BF),
            pltpu.VMEM((heads * CHUNK, width), BF),
            pltpu.VMEM((heads * CHUNK, width), BF),
            pltpu.VMEM((CHUNK, heads * CHUNK), BF),
            pltpu.VMEM((CHUNK, heads * CHUNK), BF),
            pltpu.VMEM((width, CHUNK), F32),
            pltpu.VMEM((tokens, width), F32),
            pltpu.VMEM((tokens, width), F32),
        ],
        compiler_params=pltpu.CompilerParams(vmem_limit_bytes=48 * 1024 * 1024),
        cost_estimate=pl.CostEstimate(flops=40_000_000_000, transcendentals=0, bytes_accessed=0),
        name="attention_backward",
    )(slots, lows, *kept, grad_mixed, *tables, begins)


def fetch(at_ref, pieces, spans, target, sem):
    copies = []
    for n, (piece, (first, rows)) in enumerate(zip(pieces, spans)):
        place = pl.ds(pl.multiple_of(at_ref[n], 16), rows)
        copies.append(pltpu.make_async_copy(piece.at[pl.ds(first, rows), :], target.at[place, :], sem.at[n]))
    for copy in copies:
        copy.start()
    return copies


def attn_kernel(spans, at_ref, hidden_ref, gain_ref, bias_ref, shift_ref, *refs):
    n = len(spans)
    normed_ref, merged_ref, w_attn, sem = refs[n:]

    @pl.when(pl.program_id(0) == 0)
    def _():
        for copy in fetch(at_ref, refs[:n], spans, w_attn, sem):
            copy.wait()

    normal, _ = normalise(hidden_ref[...].astype(F32))
    normed = (normal * gain_ref[...] + bias_ref[...]).astype(BF)
    normed_ref[...] = normed
    merged_ref[...] = matmul(normed, w_attn[...]) + shift_ref[...]


def pair_kernel(spans, at_ref, normed_ref, *refs):
    n = len(spans)
    gate_pieces, up_pieces = refs[:n], refs[n : 2 * n]
    act_ref, slope_ref, silu_ref, w_gate, w_up, *sems = refs[2 * n :]

    @pl.when(pl.program_id(0) == 0)
    def _():
        copies = fetch(at_ref, gate_pieces, spans, w_gate, sems[0])
        copies += fetch(at_ref, up_pieces, spans, w_up, sems[1])
        for copy in copies:
            copy.wait()

    normed = normed_ref[...]
    gating = matmul(normed, w_gate[...])
    rising = matmul(normed, w_up[...])
    sigma = jax.nn.sigmoid(gating)
    silu = gating * sigma
    act_ref[...] = (silu * rising).astype(BF)
    slope_ref[...] = (rising * sigma * (1.0 + gating * (1.0 - sigma))).astype(BF)
    silu_ref[...] = silu.astype(BF)


def row_block(width):
    return pl.BlockSpec((CHUNK, width), lambda i: (i, 0))


def full_block(array):
    return pl.BlockSpec(array.shape, lambda i: (0, 0))


def split_pieces(pieces):
    at = jnp.stack([jnp.asarray(piece[3], jnp.int32) for piece in pieces])
    return at, [piece[0] for piece in pieces], tuple((piece[1], piece[2]) for piece in pieces)


def attn_side(hidden, gain, bias, shift, pieces):
    tokens, model = hidden.shape
    at, arrays, spans = split_pieces(pieces)
    n = len(spans)
    width = arrays[0].shape[1]
    return pl.pallas_call(
        functools.partial(attn_kernel, spans),
        grid=(tokens // CHUNK,),
        out_shape=(jax.ShapeDtypeStruct((tokens, model), BF), jax.ShapeDtypeStruct((tokens, width), F32)),
        in_specs=[SCALAR, row_block(model), full_block(gain), full_block(bias), full_block(shift)] + [ANYWHERE] * n,
        out_specs=(row_block(model), row_block(width)),
        scratch_shapes=[pltpu.VMEM((model, width), BF), pltpu.SemaphoreType.DMA((n,))],
        compiler_params=pltpu.CompilerParams(vmem_limit_bytes=56 * 1024 * 1024),
        cost_estimate=pl.CostEstimate(flops=18_000_000_000, transcendentals=0, bytes_accessed=0),
        name="attn_side",
    )(at, hidden, gain, bias, shift, *arrays)


def pair_side(normed, gate_pieces, up_pieces):
    tokens, model = normed.shape
    at, gates, spans = split_pieces(gate_pieces)
    ups = split_pieces(up_pieces)[1]
    n = len(spans)
    units = gates[0].shape[1]
    return pl.pallas_call(
        functools.partial(pair_kernel, spans),
        grid=(tokens // CHUNK,),
        out_shape=(jax.ShapeDtypeStruct((tokens, units), BF),) * 3,
        in_specs=[SCALAR, row_block(model)] + [ANYWHERE] * (2 * n),
        out_specs=(row_block(units),) * 3,
        scratch_shapes=[
            pltpu.VMEM((model, units), BF),
            pltpu.VMEM((model, units), BF),
            pltpu.SemaphoreType.DMA((n,)),
            pltpu.SemaphoreType.DMA((n,)),
        ],
        compiler_params=pltpu.CompilerParams(vmem_limit_bytes=56 * 1024 * 1024),
        cost_estimate=pl.CostEstimate(flops=28_000_000_000, transcendentals=0, bytes_accessed=0),
        name="pair_side",
    )(at, normed, *gates, *ups)


def grad_kernel(grad_ref, slope_ref, silu_ref, lower_ref, proj_ref, gate_ref, up_ref, mixed_ref):
    grad = grad_ref[...]
    act = matmul_nt(grad, lower_ref[...])
    mixed_ref[...] = matmul_nt(grad, proj_ref[...]).astype(BF)
    gate_ref[...] = (act * slope_ref[...].astype(F32)).astype(BF)
    up_ref[...] = (act * silu_ref[...].astype(F32)).astype(BF)


def grad_side(grad, slope, silu, lower, proj):
    tokens, model = grad.shape
    units, width = slope.shape[1], proj.shape[0]
    return pl.pallas_call(
        grad_kernel,
        grid=(tokens // CHUNK,),
        out_shape=(
            jax.ShapeDtypeStruct((tokens, units), BF),
            jax.ShapeDtypeStruct((tokens, units), BF),
            jax.ShapeDtypeStruct((tokens, width), BF),
        ),
        in_specs=[
            row_block(model),
            row_block(units),
            row_block(units),
            full_block(lower),
            full_block(proj),
        ],
        out_specs=(row_block(units), row_block(units), row_block(width)),
        compiler_params=pltpu.CompilerParams(vmem_limit_bytes=56 * 1024 * 1024),
        cost_estimate=pl.CostEstimate(flops=18_000_000_000, transcendentals=0, bytes_accessed=0),
        name="grad_side",
    )(grad, slope, silu, lower, proj)


def out_kernel(mixed_ref, act_ref, proj_ref, lower_ref, out_ref):
    out_ref[...] = (matmul(mixed_ref[...], proj_ref[...]) + matmul(act_ref[...], lower_ref[...])).astype(BF)


def out_side(mixed, act, proj, lower):
    tokens, model = mixed.shape[0], proj.shape[1]
    return pl.pallas_call(
        out_kernel,
        grid=(tokens // CHUNK,),
        out_shape=jax.ShapeDtypeStruct((tokens, model), BF),
        in_specs=[row_block(mixed.shape[1]), row_block(act.shape[1]), full_block(proj), full_block(lower)],
        out_specs=row_block(model),
        compiler_params=pltpu.CompilerParams(vmem_limit_bytes=56 * 1024 * 1024),
        cost_estimate=pl.CostEstimate(flops=15_000_000_000, transcendentals=0, bytes_accessed=0),
        name="out_side",
    )(mixed, act, proj, lower)


def input_kernel(spans, at_ref, gate_ref, up_ref, merged_ref, hidden_ref, *refs):
    n = len(spans)
    gate_pieces, up_pieces, attn_pieces = refs[:n], refs[n : 2 * n], refs[2 * n : 3 * n]
    part_ref, terms_ref, w_gate, w_up, w_attn, *sems = refs[3 * n :]

    @pl.when(pl.program_id(0) == 0)
    def _():
        copies = fetch(at_ref, gate_pieces, spans, w_gate, sems[0])
        copies += fetch(at_ref, up_pieces, spans, w_up, sems[1])
        copies += fetch(at_ref, attn_pieces, spans, w_attn, sems[2])
        terms_ref[...] = jnp.zeros_like(terms_ref)
        for copy in copies:
            copy.wait()

    part = matmul_nt(gate_ref[...], w_gate[...]) + matmul_nt(up_ref[...], w_up[...])
    part = part + matmul_nt(merged_ref[...], w_attn[...])
    part_ref[...] = part.astype(BF)
    normal, _ = normalise(hidden_ref[...].astype(F32))
    terms_ref[0:1, :] += jnp.sum(part * normal, axis=0, keepdims=True)
    terms_ref[1:2, :] += jnp.sum(part, axis=0, keepdims=True)


def input_side(grad_gate, grad_up, grad_merged, hidden, gate_pieces, up_pieces, attn_pieces):
    tokens, model = hidden.shape
    at, gates, spans = split_pieces(gate_pieces)
    ups, attns = split_pieces(up_pieces)[1], split_pieces(attn_pieces)[1]
    n = len(spans)
    units, width = grad_gate.shape[1], grad_merged.shape[1]
    return pl.pallas_call(
        functools.partial(input_kernel, spans),
        grid=(tokens // CHUNK,),
        out_shape=(jax.ShapeDtypeStruct((tokens, model), BF), jax.ShapeDtypeStruct((2, model), F32)),
        in_specs=[SCALAR, row_block(units), row_block(units), row_block(width), row_block(model)]
        + [ANYWHERE] * (3 * n),
        out_specs=(row_block(model), pl.BlockSpec((2, model), lambda i: (0, 0))),
        scratch_shapes=[
            pltpu.VMEM((model, units), BF),
            pltpu.VMEM((model, units), BF),
            pltpu.VMEM((model, width), BF),
            pltpu.SemaphoreType.DMA((n,)),
            pltpu.SemaphoreType.DMA((n,)),
            pltpu.SemaphoreType.DMA((n,)),
        ],
        compiler_params=pltpu.CompilerParams(vmem_limit_bytes=56 * 1024 * 1024),
        cost_estimate=pl.CostEstimate(flops=30_000_000_000, transcendentals=0, bytes_accessed=0),
        name="input_side",
    )(at, grad_gate, grad_up, grad_merged, hidden, *gates, *ups, *attns)


def assemble_kernel(plan, source_ref, *targets):
    for target, pieces in zip(targets, plan):
        at = 0
        for part, offset, width in pieces:
            target[:, at : at + width] = source_ref[part, :, offset : offset + width].astype(F32)
            at += width


def assemble(gathered, plan):
    parts, rows, columns = gathered.shape
    step = 64
    widths = [sum(piece[2] for piece in pieces) for pieces in plan]
    return pl.pallas_call(
        functools.partial(assemble_kernel, plan),
        grid=(rows // step,),
        out_shape=tuple(jax.ShapeDtypeStruct((rows, w), F32) for w in widths),
        in_specs=[pl.BlockSpec((parts, step, columns), lambda i: (0, i, 0))],
        out_specs=tuple(pl.BlockSpec((step, w), lambda i: (i, 0)) for w in widths),
        compiler_params=pltpu.CompilerParams(vmem_limit_bytes=40 * 1024 * 1024),
        name="assemble",
    )(gathered)


def stream_places(order_row, length_row):
    places = (order_row[:, None] * BLOCK + jnp.arange(BLOCK, dtype=jnp.int32)[None, :]).reshape(-1)
    return places, stream_begins(places, length_row)


def stream_begins(places, length_row):
    ends = jnp.cumsum(length_row)
    starts = ends - length_row
    return jnp.max(jnp.where(starts[None, :] <= places[:, None], starts[None, :], 0), axis=1)


def rotary_tables(places, begins):
    entry = jnp.arange(128) % HD
    turned = entry < ROT
    index = jnp.where(entry < ROT // 2, entry, entry - ROT // 2)
    inverse = 1.0 / 10000.0 ** ((2 * index).astype(F32) / ROT)
    angles = (places - begins).astype(F32)[:, None] * jnp.where(turned, inverse, 0.0)[None, :]
    cosine, sine = jnp.cos(angles), jnp.sin(angles)
    lead = jnp.where((entry < ROT // 2)[None, :], -sine, 0.0)
    tail = jnp.where((turned & (entry >= ROT // 2))[None, :], sine, 0.0)
    return cosine, lead, tail


def take_columns(array, starts, width):
    return [lax.dynamic_slice_in_dim(array, s, width, 1) for s in starts]


def normalise(rows):
    centre = jnp.mean(rows, axis=1, keepdims=True)
    deviation = rows - centre
    inverse_std = lax.rsqrt(jnp.mean(deviation * deviation, axis=1, keepdims=True) + 1e-05)
    return deviation * inverse_std, inverse_std


def shards(
    hidden_in,
    out_grad,
    lengths,
    block_order,
    ln_gain,
    ln_bias,
    w_qkv,
    b_qkv,
    w_out,
    w_gate,
    w_up,
    w_down,
):
    parts = lax.axis_size("ctx")
    shard_count = lax.axis_size("fsdp")
    ctx_at = lax.axis_index("ctx")
    fsdp_at = lax.axis_index("fsdp")
    rows = hidden_in.shape[1]
    model = w_out.shape[1]
    hidden = w_gate.shape[1]
    tokens = rows * parts
    heads = model // HD // parts
    width = heads * HD
    shard_rows = w_qkv.shape[0]

    hidden_all = gather_ctx(hidden_in[0])
    grad_all = gather_ctx(out_grad[0])

    spread = (model // HD) % (shard_count * parts) == 0
    pieces = shard_count if spread else 1
    head_span = model // pieces
    head_width = head_span // parts
    head_starts = [
        s * model + p * head_span + ctx_at * head_width for s in range(3) for p in range(pieces)
    ]
    unit_span = hidden // shard_count
    unit_width = unit_span // parts
    unit_starts = [p * unit_span + ctx_at * unit_width for p in range(shard_count)]

    units = shard_count * unit_width
    spare = -units % 128
    empty = jnp.zeros((shard_rows, spare), BF)
    vectors = jnp.concatenate([ln_gain, ln_bias, b_qkv])
    vector_rows = -(-vectors.shape[0] // (3 * width)) + 15
    vector_rows = vector_rows // 16 * 16
    vectors = jnp.pad(vectors, (0, vector_rows * 3 * width - vectors.shape[0])).reshape(vector_rows, 3 * width)
    w_attn_own = jnp.concatenate(take_columns(w_qkv, head_starts, head_width), axis=1)
    w_attn_own = jnp.concatenate([w_attn_own, vectors], axis=0)
    attn_near = gather_first(w_attn_own)
    w_gate_own = jnp.concatenate(take_columns(w_gate, unit_starts, unit_width) + [empty], axis=1)
    gate_near = gather_first(w_gate_own)
    w_up_own = jnp.concatenate(take_columns(w_up, unit_starts, unit_width) + [empty], axis=1)
    attn_near, w_up_own = stage(attn_near, w_up_own)
    attn_far = gather_second(w_attn_own, attn_near)
    up_near = gather_first(w_up_own)
    gate_near, attn_far = stage(gate_near, attn_far)
    gate_far = gather_second(w_gate_own, gate_near)
    w_down_own = lax.dynamic_slice_in_dim(w_down, ctx_at * unit_width, unit_width, 0)
    if spread:
        w_out_own = lax.dynamic_slice_in_dim(w_out, ctx_at * head_width, head_width, 0)
        w_rest_own = jnp.concatenate([w_down_own, w_out_own], axis=0)
    else:
        w_rest_own = w_down_own
    attn_pieces = gathered_pieces(w_attn_own, attn_near, attn_far, shard_rows)
    vectors = gathered_rest(w_attn_own, attn_near, attn_far, shard_rows).reshape(shard_count, -1)
    gain_full = vectors[:, :shard_rows].reshape(-1).astype(F32)
    bias_full = vectors[:, shard_rows : 2 * shard_rows].reshape(-1).astype(F32)
    b_attn = vectors[:, 2 * shard_rows : 2 * shard_rows + b_qkv.shape[0]].reshape(-1).astype(F32)
    b_attn_own = jnp.concatenate([lax.dynamic_slice_in_dim(b_attn, s, head_width, 0) for s in head_starts])

    order_row = block_order[0]
    blocks = order_row.shape[0]
    places, begins = stream_places(order_row, lengths[0])
    tables = rotary_tables(places, begins)
    slots = jnp.sum(
        jnp.where(
            order_row[None, :] == jnp.arange(blocks, dtype=jnp.int32)[:, None],
            jnp.arange(blocks, dtype=jnp.int32)[None, :],
            0,
        ),
        axis=1,
    ).astype(jnp.int32)
    stream_starts = stream_begins(jnp.arange(tokens, dtype=jnp.int32), lengths[0]).astype(jnp.int32)
    lows = stream_starts[::CHUNK] // CHUNK
    stream_starts = stream_starts.reshape(tokens // CHUNK, 1, CHUNK)

    normed, merged = attn_side(hidden_all, gain_full[None], bias_full[None], b_attn_own[None], attn_pieces)
    merged, up_near, w_rest_own = stage(merged, up_near, w_rest_own)
    up_far = gather_second(w_up_own, up_near)
    rest_near = gather_first(w_rest_own)
    mixed, *kept = attention_forward(heads, slots, lows, merged, tables, stream_starts)
    mixed, gate_far, up_far, rest_near = stage(mixed, gate_far, up_far, rest_near)
    gate_pieces = gathered_pieces(w_gate_own, gate_near, gate_far, shard_rows)
    up_pieces = gathered_pieces(w_up_own, up_near, up_far, shard_rows)
    rest_far = gather_second(w_rest_own, rest_near)
    act, slope, silu = pair_side(normed, gate_pieces, up_pieces)
    if spread:
        me = lax.axis_index("fsdp")
        if shard_count == 4:
            rest_pieces = [w_rest_own, rest_near[0], rest_near[1], jnp.concatenate(rest_far, axis=0)]
            origin = [me, me ^ 1, me ^ 2, me ^ 3]
        else:
            rest_pieces = [rest_near[0].reshape(shard_count, -1, model)[i] for i in range(shard_count)]
            origin = list(range(shard_count))
        w_lower = placed([p[:unit_width] for p in rest_pieces], [o * unit_width for o in origin], units + spare)
        w_proj = placed([p[unit_width:] for p in rest_pieces], [o * head_width for o in origin], width)
    else:
        w_lower = placed(rest_near, [0], units + spare)
        w_proj = lax.dynamic_slice_in_dim(
            lax.all_gather(w_out, "fsdp", axis=0, tiled=True), ctx_at * width, width, 0
        )
    out_part = out_side(mixed, act, w_proj, w_lower)
    out_rows = scatter_ctx(out_part)

    (grad_all,) = tie([grad_all], [out_part])
    down_part = matmul_tn(act, grad_all).astype(BF)
    proj_part = matmul_tn(mixed, grad_all).astype(BF)
    if spread:
        rest_part = jnp.concatenate(
            [p.reshape(shard_count, -1, model) for p in (down_part[:units], proj_part)], axis=1
        ).reshape(-1, model)
    else:
        rest_part = down_part[:units]
    rest_part, grad_all = stage(rest_part, grad_all)
    rest_first = scatter_first(halves(rest_part))
    grad_gate, grad_up, grad_mixed = grad_side(grad_all, slope, silu, w_lower, w_proj)
    grad_gate, grad_up, grad_mixed, rest_first = stage(grad_gate, grad_up, grad_mixed, rest_first)

    rest_second = scatter_second(halves(rest_part), rest_first)
    gate_part = matmul_tn(normed, grad_gate).astype(BF)
    up_part = matmul_tn(normed, grad_up).astype(BF)
    rest_sum = jnp.concatenate(scatter_last(halves(rest_part), rest_first, rest_second), axis=1)
    gate_part, up_part, rest_sum, grad_mixed = stage(gate_part, up_part, rest_sum, grad_mixed)
    rest_all = gather_ctx(rest_sum)

    pair_first = scatter_first((gate_part, up_part))
    grad_merged = attention_backward(heads, slots, lows, kept, grad_mixed, tables, stream_starts)
    grad_merged, pair_first = stage(grad_merged, pair_first)

    pair_second = scatter_second((gate_part, up_part), pair_first)
    grad_part, terms = input_side(
        grad_gate, grad_up, grad_merged, hidden_all, gate_pieces, up_pieces, attn_pieces
    )
    merged_term = jnp.sum(grad_merged, axis=0, dtype=F32).reshape(3, pieces, 1, head_width)
    merged_term = jnp.where(
        lax.broadcasted_iota(jnp.int32, (3, pieces, parts, head_width), 2) == ctx_at, merged_term, 0.0
    )
    terms = jnp.concatenate([terms.reshape(-1), merged_term.reshape(-1)]).reshape(-1, 128)
    pair_sum = jnp.concatenate(
        [p[:, :units] for p in scatter_last((gate_part, up_part), pair_first, pair_second)], axis=1
    )
    grad_part, terms, pair_sum, grad_merged = stage(grad_part, terms, pair_sum, grad_merged)
    pair_all = gather_ctx(pair_sum[None])

    part_own, part_other = split_cores(grad_part)
    part_other = flip(part_other, "ctx", 0)
    other_terms = others_of(terms, "ctx", 1, 2)
    attn_part = matmul_tn(normed, grad_merged).astype(BF)
    attn_part, part_other, terms, others = stage(attn_part, part_other, terms, other_terms[0])
    terms = sum_of(terms, others, other_terms[1])
    part_places = (part_own.astype(F32) + part_other.astype(F32)).astype(BF)

    attn_first = scatter_first(halves(attn_part))
    other_terms = others_of(terms, "fsdp", 1, shard_count)
    attn_first, terms, others, part_places = stage(attn_first, terms, other_terms[0], part_places)
    terms = sum_of(terms, others, other_terms[1])
    grad_normed = scatter_places(part_places)

    attn_second = scatter_second(halves(attn_part), attn_first)
    attn_sum = jnp.concatenate(scatter_last(halves(attn_part), attn_first, attn_second), axis=1)
    attn_all = gather_ctx(attn_sum[None])
    other_terms = others_of(terms, "ctx", 2, parts // 2)
    terms, others = stage(terms, other_terms[0])
    terms = sum_of(terms, others, other_terms[1]).reshape(-1)

    float_in = hidden_in[0].astype(F32)
    (out_rows,) = tie([out_rows], [attn_sum, terms])
    output = (float_in + out_rows.astype(F32)).astype(BF)[None]
    (rest_all,) = tie([rest_all], [output])
    rest_blocks = rest_all.reshape(parts, -1, model)
    grad_down_w = rest_blocks[:, :unit_width].reshape(-1, model).astype(F32)
    if spread:
        grad_proj_w = rest_blocks[:, unit_width:].reshape(-1, model).astype(F32)
    else:
        grad_proj_w = lax.dynamic_slice_in_dim(
            gather_ctx(lax.psum(proj_part.astype(F32), "fsdp")), fsdp_at * shard_rows, shard_rows, 0
        )
    grad_down_w, grad_proj_w = stage(grad_down_w, grad_proj_w)
    (pair_all,) = tie([pair_all], [grad_down_w])

    pair_plan = [
        [
            (c, side * units + p * unit_width, unit_width)
            for p in range(shard_count)
            for c in range(parts)
        ]
        for side in range(2)
    ]
    attn_plan = [
        [
            (c, (s * pieces + p) * head_width, head_width)
            for s in range(3)
            for p in range(pieces)
            for c in range(parts)
        ]
    ]
    grad_gate_w, grad_up_w = assemble(pair_all, pair_plan)
    (grad_normed,) = tie([grad_normed], [grad_gate_w])
    grad_normed = grad_normed.astype(F32)

    normal_hat, inverse_std = normalise(float_in)
    b_rows = b_qkv.shape[0]
    grad_b_attn = lax.dynamic_slice_in_dim(terms, 2 * model + fsdp_at * b_rows, b_rows, 0)
    grad_gain = lax.dynamic_slice_in_dim(terms, fsdp_at * shard_rows, shard_rows, 0)
    grad_bias = lax.dynamic_slice_in_dim(terms, model + fsdp_at * shard_rows, shard_rows, 0)

    grad_hat = grad_normed * gain_full
    grad_in = out_grad[0].astype(F32) + inverse_std * (
        grad_hat
        - jnp.mean(grad_hat, axis=1, keepdims=True)
        - normal_hat * jnp.mean(grad_hat * normal_hat, axis=1, keepdims=True)
    )
    grad_in = grad_in.astype(BF)[None]
    (attn_all,) = tie([attn_all], [grad_in])
    (grad_attn_w,) = assemble(attn_all, attn_plan)
    return (
        output,
        grad_in,
        grad_gain,
        grad_bias,
        grad_attn_w,
        grad_b_attn,
        grad_proj_w,
        grad_gate_w,
        grad_up_w,
        grad_down_w,
    )


def solution(mesh):
    return jax.shard_map(
        shards,
        mesh=mesh,
        in_specs=(
            P("fsdp", "ctx", None),
            P("fsdp", "ctx", None),
            P("fsdp", None),
            P("fsdp", None),
            P("fsdp"),
            P("fsdp"),
            P("fsdp", None),
            P("fsdp"),
            P("fsdp", None),
            P("fsdp", None),
            P("fsdp", None),
            P("fsdp", None),
        ),
        out_specs=(
            P("fsdp", "ctx", None),
            P("fsdp", "ctx", None),
            P("fsdp"),
            P("fsdp"),
            P("fsdp", None),
            P("fsdp"),
            P("fsdp", None),
            P("fsdp", None),
            P("fsdp", None),
            P("fsdp", None),
        ),
        check_vma=False,
    )
```

time: 786 us -> 659 us (0.84)
  blocking collectives: 165 us -> 0 us
  Pallas kernels: 63.8 us -> 179 us
  matrix products: 150 us -> 47.8 us
  local copies, waits for them, and re-layouts: 61.8 us -> 83.8 us
  waiting for transfers between devices: 233 us -> 213 us
  starting transfers between devices: 35.1 us -> 48.1 us
    all_gather x3 -> x0, blocking collectives: 165 us -> none  [the longest x1 78.7 us: shards(): terms = jnp.sum(lax.all_gather(terms, ('ctx', 'fsdp'), axis=0), axis=0)]
    pallas_call x1 -> x26, Pallas kernels: 48 us -> 163 us  [the longest x1 41.9 us: attention_backward(): pl.pallas_call(functools.partial(backward_kernel, heads), out_shape=jax.S...]
    dot_general x8 -> x0, matrix products: 108 us -> none  [the longest x4 56.1 us: matmul_nt(): lax.dot_general(left, right, (((1,), (1,)), ((), ())), preferred_element_...]
    ppermute x32 -> x35, waiting for transfers between devices: 156 us -> 49 us  [flip(): return lax.ppermute(values, axis, [(i, i ^ 1 << bit) for i in range(count)])]
    reduce_scatter x2, waiting for transfers between devices: 0.01 us -> 64.1 us  [the longest x1 64.1 us: scatter_places(): lax.psum_scatter(values.reshape(places * rows, columns), 'ctx', scatter_d...]
    all_gather x6 -> x5, waiting for transfers between devices: 76.6 us -> 93.5 us  [gather_ctx(): return lax.all_gather(values, 'ctx', axis=0, tiled=True)]
    convert_element_type x4 -> x16, other arithmetic: 16.6 us -> 33.4 us  [the longest x6 8.46 us: scatter_last(): return (left.astype(BF), right.astype(BF))]
    slice x6 -> x13, local copies, waits for them, and re-layouts: 3.11 us -> 18.8 us  [the longest x8 8.82 us: gather_second(): return [flip(first[0][:half], 'fsdp', 1), flip(first[1][half:], 'fsdp', 0)]]
  transfers between devices with their start and end apart: 40 -> 49, of which waited for: 22 -> 19; matrix products, arithmetic and copies ran while one was open for 30% -> 26% of each run, Pallas kernels for 1% -> 27%
where the time goes in v2:
time: 659 us; the launch traced here: 648 us
  waiting for transfers between devices  213 us (32%)
  Pallas kernels  179 us (27%)
  local copies, waits for them, and re-layouts  83.8 us (13%)
  other arithmetic  60 us (9%)
  starting transfers between devices  48.1 us (7%)
  matrix products  47.8 us (7%)
  between operations  15.8 us (2%)
    all_gather x5, waiting for transfers between devices, gather_ctx(): return lax.all_gather(values, 'ctx', axis=0, tiled=True)  93.5 us
    reduce_scatter x1, waiting for transfers between devices, scatter_places(): lax.psum_scatter(values.reshape(places * rows, columns), 'ctx', scatter_d...  64.1 us
    ppermute x35, waiting for transfers between devices, flip(): return lax.ppermute(values, axis, [(i, i ^ 1 << bit) for i in range(count)])  49 us
    dot_general x5, matrix products, matmul_tn(): lax.dot_general(left, right, (((0,), (0,)), ((), ())), preferred_element_...  47.8 us
    pallas_call x1, Pallas kernels, attention_backward(): pl.pallas_call(functools.partial(backward_kernel, heads), out_shape=jax.S...  41.9 us
    ppermute x35, starting transfers between devices, flip(): return lax.ppermute(values, axis, [(i, i ^ 1 << bit) for i in range(count)])  39.4 us
    pallas_call x1, Pallas kernels, input_side(): pl.pallas_call(functools.partial(input_kernel, spans), grid=(tokens // CH...  30.5 us
    unnamed x145, local copies, waits for them, and re-layouts  24.5 us
  transfers between devices with their start and end apart: 49, of which 19 were waited for; matrix products, arithmetic and copies ran while one was open for 26% of the time, Pallas kernels for 27%

profile of v2, /device:TPU:0, one launch (start us, length us, event | category | flops | bytes accessed | tf_op | source)
XLA Modules:
  0.0 647.9 jit_solution(8222252054128115704)
XLA Ops:
  9.3 2.9 constant_dynamic-slice_fusion.22
  12.2 2.8 concatenate.40
  16.8 2.9 collective-permute-start
  21.3 4.6 constant_dynamic-slice_fusion.14
  25.9 2.4 concatenate.43.refs_0_
  29.5 2.3 concatenate.42.refs_2_
  33.8 5.6 fusion.15
  49.2 6.7 %collective-permute-done.2.refs_0_ = bf16[512,768]{1,0:T(8,128)(2,1)} collective-permute-done((bf16[512,768]{1,0:T(8,128)(2,1)}, bf16[512,768]{1,0:T(8,128)(2,1)}, u32[]{:S(2)}, u32[]{:S(2)}) %collective-permute-start.2) | collective-permute-done | bytes 786464 | tf_op jit(solution)/shard_map/ppermute | solution.py:33
  55.8 2.1 collective-permute-start.7
  57.9 8.4 %collective-permute-done.4.refs_2_ = bf16[256,768]{1,0:T(8,128)(2,1)} collective-permute-done((bf16[256,768]{1,0:T(8,128)(2,1)S(1)}, bf16[256,768]{1,0:T(8,128)(2,1)}, u32[]{:S(2)}, u32[]{:S(2)}) %collective-permute-start.4) | collective-permute-done | bytes 393248 | tf_op jit(solution)/shard_map/ppermute | solution.py:33
  76.2 18.3 %all-gather.12.cloned.1.call-done = bf16[1,2048,2048]{2,1,0:T(8,128)(2,1)} async-done(((bf16[1,256,2048]{2,1,0:T(8,128)(2,1)}), bf16[1,2048,2048]{2,1,0:T(8,128)(2,1)}) %all-gather.12.cloned.1.call-update) | async-done | bytes 8388624 | tf_op jit(solution)/shard_map/all_gather | solution.py:185
  94.4 16.9 %attn_side.1 = (bf16[2048,2048]{1,0:T(8,128)(2,1)}, f32[2048,768]{1,0:T(8,128)}) custom-call(s32[5]{0:T(128)} %stack.17.at_ref, bf16[2048,2048]{1,0:T(8,128)(2,1)} %bitcast.159, f32[1,2048]{1,0:T(1,128)} %bitcast.157, f32[1,2048]{1,0:T(1,128)} %bitcast.158, f32[1,768]{1,0:T(1,128)} %broadcast_in_dim.158.shift_ref, ...), custom_call_target="tpu_custom_call" | custom-call | flops 17999998976 | tf_op jit(solution)/shard_map/attn_side/pallas_call | solution.py:542
  117.1 22.7 %attention_forward.1 = (bf16[2048,256]{1,0:T(8,128)(2,1)S(1)}, bf16[2048,256]{1,0:T(8,128)(2,1)S(1)}, bf16[2048,256]{1,0:T(8,128)(2,1)S(1)}, bf16[2048,256]{1,0:...) custom-call(s32[16]{0:T(128)S(1)} %select_reduce_fusion.slot_ref, s32[8]{0:T(128)S(1)} %and_select_fusion.1.low_ref, ...), custom_call_target="tpu_custom_call" | custom-call | flops 24999999488 | tf_op jit(solution)/shard_map/attention_forward/pallas_call | solution.py:431
  147.0 5.3 collective-permute-done.11.refs_4_
  157.4 2.1 slice_dynamic-update-slice_fusion.1
  161.5 20.7 %pair_side.1 = (bf16[2048,768]{1,0:T(8,128)(2,1)}, bf16[2048,768]{1,0:T(8,128)(2,1)}, bf16[2048,768]{1,0:T(8,128)(2,1)}) custom-call(s32[5]{0:T(128)} %stack.17.at_ref, bf16[2048,2048]{1,0:T(8,128)(2,1)} %get-tuple-element.101.normed_ref, bf16[512,768]{1,0:T(8,128)(2,1)} %concatenate.43.refs_0_, bf16[512,768]{1,0:T(8,128)(2,1)} %get-tuple-element.95.refs_1_, ...), custom_call_target="tpu_custom_call" | custom-call | flops 28000000000 | tf_op jit(solution)/shard_map/pair_side/pallas_call | solution.py:561
  186.1 14.1 %out_side.1.refs_1_ = bf16[2048,2048]{1,0:T(8,128)(2,1)} custom-call(bf16[2048,256]{1,0:T(8,128)(2,1)} %get-tuple-element.100.mixed_ref, bf16[2048,768]{1,0:T(8,128)(2,1)} %get-tuple-element.106.act_ref, bf16[256,2048]{1,0:T(8,128)(2,1)} %copy-done.44, bf16[768,2048]{1,0:T(8,128)(2,1)} %fusion.20.lower_ref), custom_call_target="tpu_custom_call" | custom-call | flops 15000000512 | tf_op jit(solution)/shard_map/out_side/pallas_call | solution.py:618
  200.8 10.4 %fusion.36 = bf16[768,2048]{1,0:T(8,128)(2,1)S(1)} fusion(bf16[2048,768]{1,0:T(8,128)(2,1)} %get-tuple-element.106.act_ref, bf16[2048,2048]{1,0:T(8,128)(2,1)} %tie.23.refs_1_), kind=kOutput, calls=%fused_computation.161 | convolution fusion | flops 6442450944 | bytes 14680064 | tf_op jit(solution)/shard_map/dot_general | solution.py:28
  212.5 2.4 convolution_convert_fusion.3
  214.8 2.5 pad_maximum_fusion
  217.3 2.6 fusion.32
  225.2 16.4 %grad_side.1 = (bf16[2048,768]{1,0:T(8,128)(2,1)}, bf16[2048,768]{1,0:T(8,128)(2,1)}, bf16[2048,256]{1,0:T(8,128)(2,1)}) custom-call(bf16[2048,2048]{1,0:T(8,128)(2,1)} %get-tuple-element.109.grad_ref, bf16[2048,768]{1,0:T(8,128)(2,1)} %get-tuple-element.110.slope_ref, bf16[2048,768]{1,0:T(8,128)(2,1)} %get-tuple-element.111.silu_ref, ...), custom_call_target="tpu_custom_call" | custom-call | flops 17999998976 | tf_op jit(solution)/shard_map/grad_side/pallas_call | solution.py:590
  249.0 11.6 %convolution_convert_fusion.2.refs_0_ = bf16[2048,768]{1,0:T(8,128)(2,1)} fusion(bf16[2048,2048]{1,0:T(8,128)(2,1)} %get-tuple-element.101.normed_ref, bf16[2048,768]{1,0:T(8,128)(2,1)} %get-tuple-element.116.gate_ref), kind=kOutput, calls=%fused_computation.9 | convolution fusion | flops 6444023808 | bytes 14680064 | tf_op jit(solution)/shard_map/dot_general | solution.py:28
  260.6 10.9 %convolution_convert_fusion.1.refs_1_ = bf16[2048,768]{1,0:T(8,128)(2,1)} fusion(bf16[2048,2048]{1,0:T(8,128)(2,1)} %get-tuple-element.101.normed_ref, bf16[2048,768]{1,0:T(8,128)(2,1)S(1)} %copy-done.23), kind=kOutput, calls=%fused_computation.8 | convolution fusion | flops 6444023808 | bytes 14680064 | tf_op jit(solution)/shard_map/dot_general | solution.py:28
  281.3 41.9 %attention_backward.1.refs_0_ = bf16[2048,768]{1,0:T(8,128)(2,1)} custom-call(s32[16]{0:T(128)S(1)} %select_reduce_fusion.slot_ref, s32[8]{0:T(128)S(1)} %and_select_fusion.1.low_ref, bf16[2048,256]{1,0:T(8,128)(2,1)S(1)} %get-tuple-element.118.q_ref, bf16[2048,256]{1,0:T(8,128)(2,1)S(1)} %copy-done.8, bf16[2048,256]{1,0:T(8,128)(2,1)S(1)} %copy-done.10, ...), custom_call_target="tpu_custom_call" | custom-call | flops 40000000000 | tf_op jit(solution)/shard_map/attention_backward/pallas_call | solution.py:456
  327.1 30.5 %input_side.1 = (bf16[2048,2048]{1,0:T(8,128)(2,1)}, f32[2,2048]{1,0:T(2,128)}) custom-call(s32[5]{0:T(128)} %stack.17.at_ref, bf16[2048,768]{1,0:T(8,128)(2,1)} %get-tuple-element.116.gate_ref, bf16[2048,768]{1,0:T(8,128)(2,1)} %get-tuple-element.117.up_ref, bf16[2048,768]{1,0:T(8,128)(2,1)} %get-tuple-element.131.merged_ref.refs_3_, ...), custom_call_target="tpu_custom_call" | custom-call | flops 30000001024 | tf_op jit(solution)/shard_map/input_side/pallas_call | solution.py:658
  363.0 11.0 %collective-permute-done.26 = bf16[512,768]{1,0:T(8,128)(2,1)} collective-permute-done((bf16[512,768]{1,0:T(8,128)(2,1)S(1)}, bf16[512,768]{1,0:T(8,128)(2,1)}, u32[]{:S(2)}, u32[]{:S(2)}) %collective-permute-start.26) | collective-permute-done | bytes 786464 | tf_op jit(solution)/shard_map/ppermute | solution.py:33
  377.5 4.8 dynamic-slice_bitcast_fusion
  382.8 12.6 %convolution_convert_fusion.refs_0_ = bf16[2048,768]{1,0:T(8,128)(2,1)} fusion(bf16[2048,2048]{1,0:T(8,128)(2,1)} %get-tuple-element.101.normed_ref, bf16[2048,768]{1,0:T(8,128)(2,1)} %get-tuple-element.138), kind=kOutput, calls=%fused_computation.7 | convolution fusion | flops 6444023808 | bytes 14680064 | tf_op jit(solution)/shard_map/dot_general | solution.py:28
  399.2 2.1 collective-permute-start.36
  401.3 2.2 fusion.33
  409.0 7.8 %fusion.refs_8_ = bf16[4,256,2048]{2,1,0:T(8,128)(2,1)} fusion(bf16[4,256,2048]{2,1,0:T(8,128)(2,1)} %get-tuple-element.144, bf16[4,2,256,2048]{3,2,1,0:T(8,128)(2,1)} %bitcast.145, s32[]{:T(128)S(6)} %select_n.377), kind=kLoop, calls=%fused_computation.1 | loop fusion | flops 8388608 | bytes 12582916 | tf_op jit(solution)/shard_map/convert_element_type | solution.py:897
  417.0 6.3 collective-permute-done.32.refs_2_
  431.0 5.3 collective-permute-done.38
  442.3 3.2 collective-permute-start.41
  445.5 3.0 collective-permute-done.39.refs_1_
  456.2 2.7 fusion.12
  458.9 3.2 slice.195
  463.8 2.7 bitcast_convert_fusion.1.refs_1_
  466.5 6.4 bitcast_convert_fusion.refs_0_
  472.9 13.4 %all-gather.16.cloned.1.call-done = bf16[4096,1408]{1,0:T(8,128)(2,1)} async-done(((bf16[512,1408]{1,0:T(8,128)(2,1)}), bf16[4096,1408]{1,0:T(8,128)(2,1)}) %all-gather.16.cloned.1.call-update) | async-done | bytes 11534352 | tf_op jit(solution)/shard_map/all_gather | solution.py:185
  486.2 4.3 copy-done.2
  490.5 9.3 %assemble.2 = (f32[512,5632]{1,0:T(8,128)}, f32[512,5632]{1,0:T(8,128)}) custom-call(bf16[8,512,1408]{2,1,0:T(8,128)(2,1)S(1)} %copy-done.2), custom_call_target="tpu_custom_call" | custom-call | tf_op jit(solution)/shard_map/assemble/pallas_call | solution.py:691
  499.8 64.1 %reduce-scatter.5.cloned.1.call-done.refs_0_ = bf16[256,2048]{1,0:T(8,128)(2,1)} async-done(((bf16[1024,2048]{1,0:T(8,128)(2,1)}), bf16[256,2048]{1,0:T(8,128)(2,1)}) %reduce-scatter.5.cloned.1.call-update) | async-done | bytes 1048592 | tf_op jit(solution)/shard_map/reduce_scatter | solution.py:202
  565.9 3.1 fusion.19.refs_1_
  569.1 61.9 %all-gather.18.cloned.1.call-done = bf16[4096,768]{1,0:T(8,128)(2,1)} async-done(((bf16[512,768]{1,0:T(8,128)(2,1)}), bf16[4096,768]{1,0:T(8,128)(2,1)}) %all-gather.18.cloned.1.call-update) | async-done | bytes 6291472 | tf_op jit(solution)/shard_map/all_gather | solution.py:185
  631.0 2.8 copy-done.3
  633.8 6.8 %assemble.3 = f32[512,6144]{1,0:T(8,128)} custom-call(bf16[8,512,768]{2,1,0:T(8,128)(2,1)S(1)} %copy-done.3), custom_call_target="tpu_custom_call" | custom-call | tf_op jit(solution)/shard_map/assemble/pallas_call | solution.py:691
  (353 shorter events, 123.4 us)
Async XLA Ops:
  7.2 87.2 %all-gather.12.cloned.1.call-start = ((), (), s32[]{:S(2)}) async-start(), calls=%async_computation.5 | async-start | bytes 9437184 | tf_op jit(solution)/shard_map/all_gather | solution.py:185
  7.9 192.9 %all-gather.14.cloned.1.call-start = ((), (), s32[]{:S(2)}) async-start(), calls=%async_computation.6 | async-start | bytes 9437184 | tf_op jit(solution)/shard_map/all_gather | solution.py:185
  16.8 23.7 %collective-permute-start = (bf16[528,768]{1,0:T(8,128)(2,1)}, bf16[528,768]{1,0:T(8,128)(2,1)}, u32[]{:S(2)}, u32[]{:S(2)}) collective-permute-start(bf16[528,768]{1,0:T(8,128)(2,1)} %pad_maximum_fusion.4.refs_0_.refs_10_), channel_id=1, source_target_pairs={{0,1},{1,0},{2,3},{3,2},{4,5},{5,4},{6,7},{7,6},{8,9},{9,8},{10,11... | collective-permute-start | bytes 2433032 | tf_op jit(solution)/shard_map/ppermute | solution.py:33
  19.8 21.2 %collective-permute-start.1 = (bf16[528,768]{1,0:T(8,128)(2,1)}, bf16[528,768]{1,0:T(8,128)(2,1)S(1)}, u32[]{:S(2)}, u32[]{:S(2)}) collective-permute-start(bf16[528,768]{1,0:T(8,128)(2,1)} %pad_maximum_fusion.4.refs_0_.refs_10_), channel_id=1, source_target_pairs={{0,2},{1,3},{2,0},{3,1},{4,6},{5,7},{6,4},{7,5},{8,10},{9,11},{10,... | collective-permute-start | bytes 2433032 | tf_op jit(solution)/shard_map/ppermute | solution.py:33
  28.3 27.6 %collective-permute-start.2 = (bf16[512,768]{1,0:T(8,128)(2,1)}, bf16[512,768]{1,0:T(8,128)(2,1)}, u32[]{:S(2)}, u32[]{:S(2)}) collective-permute-start(bf16[512,768]{1,0:T(8,128)(2,1)} %concatenate.43.refs_0_), channel_id=1, source_target_pairs={{0,1},{1,0},{2,3},{3,2},{4,5},{5,4},{6,7},{7,6},{8,9},{9,8},{10,11... | collective-permute-start | bytes 2359304 | tf_op jit(solution)/shard_map/ppermute | solution.py:33
  28.7 29.2 %collective-permute-start.3 = (bf16[512,768]{1,0:T(8,128)(2,1)}, bf16[512,768]{1,0:T(8,128)(2,1)}, u32[]{:S(2)}, u32[]{:S(2)}) collective-permute-start(bf16[512,768]{1,0:T(8,128)(2,1)} %concatenate.43.refs_0_), channel_id=1, source_target_pairs={{0,2},{1,3},{2,0},{3,1},{4,6},{5,7},{6,4},{7,5},{8,10},{9,11},{10,... | collective-permute-start | bytes 2359304 | tf_op jit(solution)/shard_map/ppermute | solution.py:33
  28.8 427.4 %reduce-scatter.3.cloned.1.call-start = ((), (), s32[]{:S(2)}) async-start(), calls=%async_computation.2 | async-start | bytes 9437184 | tf_op jit(solution)/shard_map/reduce_scatter | solution.py:189
  42.9 23.4 %collective-permute-start.4 = (bf16[256,768]{1,0:T(8,128)(2,1)S(1)}, bf16[256,768]{1,0:T(8,128)(2,1)}, u32[]{:S(2)}, u32[]{:S(2)}) collective-permute-start(bf16[256,768]{1,0:T(8,128)(2,1)S(1)} %slice.137), channel_id=1, source_target_pairs={{0,2},{1,3},{2,0},{3,1},{4,6},{5,7},{6,4},{7,5},{8,10},{9,11},{10,... | collective-permute-start | bytes 1179656 | tf_op jit(solution)/shard_map/ppermute | solution.py:33
  45.6 20.8 %collective-permute-start.5 = (bf16[272,768]{1,0:T(8,128)(2,1)S(1)}, bf16[272,768]{1,0:T(8,128)(2,1)S(1)}, u32[]{:S(2)}, u32[]{:S(2)}) collective-permute-start(bf16[272,768]{1,0:T(8,128)(2,1)S(1)} %slice.138), channel_id=1, source_target_pairs={{0,1},{1,0},{2,3},{3,2},{4,5},{5,4},{6,7},{7,6},{8,9},{9,8},{10,11... | collective-permute-start | bytes 1253384 | tf_op jit(solution)/shard_map/ppermute | solution.py:33
  47.2 64.1 %collective-permute-start.6 = (bf16[512,768]{1,0:T(8,128)(2,1)}, bf16[512,768]{1,0:T(8,128)(2,1)S(1)}, u32[]{:S(2)}, u32[]{:S(2)}) collective-permute-start(bf16[512,768]{1,0:T(8,128)(2,1)} %get-tuple-element.92.refs_5_), channel_id=1, source_target_pairs={{0,1},{1,0},{2,3},{3,2},{4,5},{5,4},{6,7},{7,6},{8,9},{9,8},{10,11... | collective-permute-start | bytes 2359304 | tf_op jit(solution)/shard_map/ppermute | solution.py:33
  55.8 55.5 %collective-permute-start.7 = (bf16[512,768]{1,0:T(8,128)(2,1)}, bf16[512,768]{1,0:T(8,128)(2,1)S(1)}, u32[]{:S(2)}, u32[]{:S(2)}) collective-permute-start(bf16[512,768]{1,0:T(8,128)(2,1)} %get-tuple-element.92.refs_5_), channel_id=1, source_target_pairs={{0,2},{1,3},{2,0},{3,1},{4,6},{5,7},{6,4},{7,5},{8,10},{9,11},{10,... | collective-permute-start | bytes 2359304 | tf_op jit(solution)/shard_map/ppermute | solution.py:33
  72.3 69.5 %collective-permute-start.8 = (bf16[256,768]{1,0:T(8,128)(2,1)}, bf16[256,768]{1,0:T(8,128)(2,1)S(1)}, u32[]{:S(2)}, u32[]{:S(2)}) collective-permute-start(bf16[256,768]{1,0:T(8,128)(2,1)} %slice.143), channel_id=1, source_target_pairs={{0,2},{1,3},{2,0},{3,1},{4,6},{5,7},{6,4},{7,5},{8,10},{9,11},{10,... | collective-permute-start | bytes 1179656 | tf_op jit(solution)/shard_map/ppermute | solution.py:33
  75.6 67.8 %collective-permute-start.9 = (bf16[256,768]{1,0:T(8,128)(2,1)}, bf16[256,768]{1,0:T(8,128)(2,1)}, u32[]{:S(2)}, u32[]{:S(2)}) collective-permute-start(bf16[256,768]{1,0:T(8,128)(2,1)} %slice.144), channel_id=1, source_target_pairs={{0,1},{1,0},{2,3},{3,2},{4,5},{5,4},{6,7},{7,6},{8,9},{9,8},{10,11... | collective-permute-start | bytes 1179656 | tf_op jit(solution)/shard_map/ppermute | solution.py:33
  112.5 40.6 %collective-permute-start.12 = (bf16[240,2048]{1,0:T(8,128)(2,1)}, bf16[240,2048]{1,0:T(8,128)(2,1)}, u32[]{:S(2)}, u32[]{:S(2)}) collective-permute-start(bf16[240,2048]{1,0:T(8,128)(2,1)} %get-tuple-element.99), channel_id=1, source_target_pairs={{0,1},{1,0},{2,3},{3,2},{4,5},{5,4},{6,7},{7,6},{8,9},{9,8},{10,11... | collective-permute-start | bytes 2949128 | tf_op jit(solution)/shard_map/ppermute | solution.py:33
  114.0 39.1 %collective-permute-start.13 = (bf16[240,2048]{1,0:T(8,128)(2,1)}, bf16[240,2048]{1,0:T(8,128)(2,1)}, u32[]{:S(2)}, u32[]{:S(2)}) collective-permute-start(bf16[240,2048]{1,0:T(8,128)(2,1)} %get-tuple-element.99), channel_id=1, source_target_pairs={{0,2},{1,3},{2,0},{3,1},{4,6},{5,7},{6,4},{7,5},{8,10},{9,11},{10,... | collective-permute-start | bytes 2949128 | tf_op jit(solution)/shard_map/ppermute | solution.py:33
  116.5 29.8 %collective-permute-start.10 = (bf16[256,768]{1,0:T(8,128)(2,1)S(1)}, bf16[256,768]{1,0:T(8,128)(2,1)S(1)}, u32[]{:S(2)}, u32[]{:S(2)}) collective-permute-start(bf16[256,768]{1,0:T(8,128)(2,1)S(1)} %slice.145), channel_id=1, source_target_pairs={{0,2},{1,3},{2,0},{3,1},{4,6},{5,7},{6,4},{7,5},{8,10},{9,11},{10,... | collective-permute-start | bytes 1179656 | tf_op jit(solution)/shard_map/ppermute | solution.py:33
  141.8 10.5 %collective-permute-start.11 = (bf16[256,768]{1,0:T(8,128)(2,1)S(1)}, bf16[256,768]{1,0:T(8,128)(2,1)S(1)}, u32[]{:S(2)}, u32[]{:S(2)}) collective-permute-start(bf16[256,768]{1,0:T(8,128)(2,1)S(1)} %slice.146), channel_id=1, source_target_pairs={{0,1},{1,0},{2,3},{3,2},{4,5},{5,4},{6,7},{7,6},{8,9},{9,8},{10,11... | collective-permute-start | bytes 1179656 | tf_op jit(solution)/shard_map/ppermute | solution.py:33
  154.3 29.9 %collective-permute-start.14 = (bf16[128,2048]{1,0:T(8,128)(2,1)S(1)}, bf16[128,2048]{1,0:T(8,128)(2,1)S(1)}, u32[]{:S(2)}, u32[]{:S(2)}) collective-permute-start(bf16[128,2048]{1,0:T(8,128)(2,1)S(1)} %slice.150), channel_id=1, source_target_pairs={{0,1},{1,0},{2,3},{3,2},{4,5},{5,4},{6,7},{7,6},{8,9},{9,8},{10,11... | collective-permute-start | bytes 1572872 | tf_op jit(solution)/shard_map/ppermute | solution.py:33
  155.8 28.3 %collective-permute-start.15 = (bf16[112,2048]{1,0:T(8,128)(2,1)S(1)}, bf16[112,2048]{1,0:T(8,128)(2,1)S(1)}, u32[]{:S(2)}, u32[]{:S(2)}) collective-permute-start(bf16[112,2048]{1,0:T(8,128)(2,1)S(1)} %slice.155), channel_id=1, source_target_pairs={{0,2},{1,3},{2,0},{3,1},{4,6},{5,7},{6,4},{7,5},{8,10},{9,11},{10,... | collective-permute-start | bytes 1376264 | tf_op jit(solution)/shard_map/ppermute | solution.py:33
  200.2 258.6 %all-gather.10.cloned.1.call-start = ((), (), s32[]{:S(2)}) async-start(), calls=%async_computation.4 | async-start | bytes 8847360 | tf_op jit(solution)/shard_map/all_gather | solution.py:185
  220.0 21.7 %collective-permute-start.16 = (bf16[240,1024]{1,0:T(8,128)(2,1)S(1)}, bf16[240,1024]{1,0:T(8,128)(2,1)S(1)}, u32[]{:S(2)}, u32[]{:S(2)}) collective-permute-start(bf16[240,1024]{1,0:T(8,128)(2,1)S(1)} %get-tuple-element.199), channel_id=1, source_target_pairs={{0,1},{1,0},{2,3},{3,2},{4,5},{5,4},{6,7},{7,6},{8,9},{9,8},{10,11... | collective-permute-start | bytes 1474568 | tf_op jit(solution)/shard_map/ppermute | solution.py:33
  221.8 19.9 %collective-permute-start.17 = (bf16[240,1024]{1,0:T(8,128)(2,1)S(1)}, bf16[240,1024]{1,0:T(8,128)(2,1)S(1)}, u32[]{:S(2)}, u32[]{:S(2)}) collective-permute-start(bf16[240,1024]{1,0:T(8,128)(2,1)S(1)} %get-tuple-element.197), channel_id=1, source_target_pairs={{0,2},{1,3},{2,0},{3,1},{4,6},{5,7},{6,4},{7,5},{8,10},{9,11},{10,... | collective-permute-start | bytes 1474568 | tf_op jit(solution)/shard_map/ppermute | solution.py:33
  222.2 19.5 %collective-permute-start.18 = (bf16[240,1024]{1,0:T(8,128)(2,1)S(1)}, bf16[240,1024]{1,0:T(8,128)(2,1)S(1)}, u32[]{:S(2)}, u32[]{:S(2)}) collective-permute-start(bf16[240,1024]{1,0:T(8,128)(2,1)S(1)} %get-tuple-element.198), channel_id=1, source_target_pairs={{0,1},{1,0},{2,3},{3,2},{4,5},{5,4},{6,7},{7,6},{8,9},{9,8},{10,11... | collective-permute-start | bytes 1474568 | tf_op jit(solution)/shard_map/ppermute | solution.py:33
  223.7 19.6 %collective-permute-start.19 = (bf16[240,1024]{1,0:T(8,128)(2,1)S(1)}, bf16[240,1024]{1,0:T(8,128)(2,1)S(1)}, u32[]{:S(2)}, u32[]{:S(2)}) collective-permute-start(bf16[240,1024]{1,0:T(8,128)(2,1)S(1)} %get-tuple-element.196), channel_id=1, source_target_pairs={{0,2},{1,3},{2,0},{3,1},{4,6},{5,7},{6,4},{7,5},{8,10},{9,11},{10,... | collective-permute-start | bytes 1474568 | tf_op jit(solution)/shard_map/ppermute | solution.py:33
  245.5 26.0 %collective-permute-start.21 = (bf16[240,1024]{1,0:T(8,128)(2,1)S(1)}, bf16[240,1024]{1,0:T(8,128)(2,1)S(1)}, u32[]{:S(2)}, u32[]{:S(2)}) collective-permute-start(bf16[240,1024]{1,0:T(8,128)(2,1)S(1)} %add_convert_fusion.5), channel_id=1, source_target_pairs={{0,2},{1,3},{2,0},{3,1},{4,6},{5,7},{6,4},{7,5},{8,10},{9,11},{10,... | collective-permute-start | bytes 1474568 | tf_op jit(solution)/shard_map/ppermute | solution.py:33
  247.4 25.4 %collective-permute-start.20 = (bf16[240,1024]{1,0:T(8,128)(2,1)S(1)}, bf16[240,1024]{1,0:T(8,128)(2,1)S(1)}, u32[]{:S(2)}, u32[]{:S(2)}) collective-permute-start(bf16[240,1024]{1,0:T(8,128)(2,1)S(1)} %add_convert_fusion.7), channel_id=1, source_target_pairs={{0,1},{1,0},{2,3},{3,2},{4,5},{5,4},{6,7},{7,6},{8,9},{9,8},{10,11... | collective-permute-start | bytes 1474568 | tf_op jit(solution)/shard_map/ppermute | solution.py:33
  275.2 211.0 %all-gather.16.cloned.1.call-start = ((), (), s32[]{:S(2)}) async-start(), calls=%async_computation.7 | async-start | bytes 12976128 | tf_op jit(solution)/shard_map/all_gather | solution.py:185
  277.0 46.2 %collective-permute-start.22 = (bf16[512,768]{1,0:T(8,128)(2,1)S(1)}, bf16[512,768]{1,0:T(8,128)(2,1)S(1)}, u32[]{:S(2)}, u32[]{:S(2)}) collective-permute-start(bf16[512,768]{1,0:T(8,128)(2,1)S(1)} %get-tuple-element.195), channel_id=1, source_target_pairs={{0,1},{1,0},{2,3},{3,2},{4,5},{5,4},{6,7},{7,6},{8,9},{9,8},{10,11... | collective-permute-start | bytes 2359304 | tf_op jit(solution)/shard_map/ppermute | solution.py:33
  277.8 45.4 %collective-permute-start.23 = (bf16[512,768]{1,0:T(8,128)(2,1)S(1)}, bf16[512,768]{1,0:T(8,128)(2,1)}, u32[]{:S(2)}, u32[]{:S(2)}) collective-permute-start(bf16[512,768]{1,0:T(8,128)(2,1)S(1)} %get-tuple-element.193), channel_id=1, source_target_pairs={{0,2},{1,3},{2,0},{3,1},{4,6},{5,7},{6,4},{7,5},{8,10},{9,11},{10,... | collective-permute-start | bytes 2359304 | tf_op jit(solution)/shard_map/ppermute | solution.py:33
  279.3 43.9 %collective-permute-start.24 = (bf16[512,768]{1,0:T(8,128)(2,1)S(1)}, bf16[512,768]{1,0:T(8,128)(2,1)}, u32[]{:S(2)}, u32[]{:S(2)}) collective-permute-start(bf16[512,768]{1,0:T(8,128)(2,1)S(1)} %get-tuple-element.194), channel_id=1, source_target_pairs={{0,1},{1,0},{2,3},{3,2},{4,5},{5,4},{6,7},{7,6},{8,9},{9,8},{10,11... | collective-permute-start | bytes 2359304 | tf_op jit(solution)/shard_map/ppermute | solution.py:33
  280.7 42.5 %collective-permute-start.25 = (bf16[512,768]{1,0:T(8,128)(2,1)S(1)}, bf16[512,768]{1,0:T(8,128)(2,1)}, u32[]{:S(2)}, u32[]{:S(2)}) collective-permute-start(bf16[512,768]{1,0:T(8,128)(2,1)S(1)} %get-tuple-element.192), channel_id=1, source_target_pairs={{0,2},{1,3},{2,0},{3,1},{4,6},{5,7},{6,4},{7,5},{8,10},{9,11},{10,... | collective-permute-start | bytes 2359304 | tf_op jit(solution)/shard_map/ppermute | solution.py:33
  325.6 35.7 %collective-permute-start.27 = (bf16[512,768]{1,0:T(8,128)(2,1)S(1)}, bf16[512,768]{1,0:T(8,128)(2,1)S(1)}, u32[]{:S(2)}, u32[]{:S(2)}) collective-permute-start(bf16[512,768]{1,0:T(8,128)(2,1)S(1)} %add_convert_fusion.1), channel_id=1, source_target_pairs={{0,2},{1,3},{2,0},{3,1},{4,6},{5,7},{6,4},{7,5},{8,10},{9,11},{10,... | collective-permute-start | bytes 2359304 | tf_op jit(solution)/shard_map/ppermute | solution.py:33
  359.2 14.7 %collective-permute-start.26 = (bf16[512,768]{1,0:T(8,128)(2,1)S(1)}, bf16[512,768]{1,0:T(8,128)(2,1)}, u32[]{:S(2)}, u32[]{:S(2)}) collective-permute-start(bf16[512,768]{1,0:T(8,128)(2,1)S(1)} %add_convert_fusion.3), channel_id=1, source_target_pairs={{0,1},{1,0},{2,3},{3,2},{4,5},{5,4},{6,7},{7,6},{8,9},{9,8},{10,11... | collective-permute-start | bytes 2359304 | tf_op jit(solution)/shard_map/ppermute | solution.py:33
  377.4 186.5 %reduce-scatter.5.cloned.1.call-start = ((), (), s32[]{:S(2)}) async-start(), calls=%async_computation.3 | async-start | bytes 5242880 | tf_op jit(solution)/shard_map/reduce_scatter | solution.py:202
  382.3 13.2 %collective-permute-start.28 = (bf16[4,256,2048]{2,1,0:T(8,128)(2,1)}, bf16[4,256,2048]{2,1,0:T(8,128)(2,1)}, u32[]{:S(2)}, u32[]{:S(2)}) collective-permute-start(bf16[4,256,2048]{2,1,0:T(8,128)(2,1)} %dynamic-slice_bitcast_fusion), channel_id=1, source_target_pairs={{0,4},{4,0},{8,12},{12,8},{16,20},{20,16},{24,28},{28,24},{1,5},{5... | collective-permute-start | bytes 12582920 | tf_op jit(solution)/shard_map/ppermute | solution.py:33
  382.3 13.1 %collective-permute-start.29 = (f32[80,128]{1,0:T(8,128)S(1)}, f32[80,128]{1,0:T(8,128)S(1)}, u32[]{:S(2)}, u32[]{:S(2)}) collective-permute-start(f32[80,128]{1,0:T(8,128)S(1)} %copy-done.45), channel_id=1, source_target_pairs={{0,4},{4,0},{8,12},{12,8},{16,20},{20,16},{24,28},{28,24},{1,5},{5... | collective-permute-start | bytes 122888 | tf_op jit(solution)/shard_map/ppermute | solution.py:113
  397.7 8.9 %collective-permute-start.34 = (f32[80,128]{1,0:T(8,128)S(1)}, f32[80,128]{1,0:T(8,128)S(1)}, u32[]{:S(2)}, u32[]{:S(2)}) collective-permute-start(f32[80,128]{1,0:T(8,128)S(1)} %fusion.26.refs_4_), channel_id=1, source_target_pairs={{0,1},{1,2},{2,3},{3,0},{4,5},{5,6},{6,7},{7,4},{8,9},{9,10},{10,1... | collective-permute-start | bytes 122888 | tf_op jit(solution)/shard_map/ppermute | solution.py:113
  398.8 9.6 %collective-permute-start.35 = (f32[80,128]{1,0:T(8,128)S(1)}, f32[80,128]{1,0:T(8,128)S(1)}, u32[]{:S(2)}, u32[]{:S(2)}) collective-permute-start(f32[80,128]{1,0:T(8,128)S(1)} %fusion.26.refs_4_), channel_id=1, source_target_pairs={{0,2},{1,3},{2,0},{3,1},{4,6},{5,7},{6,4},{7,5},{8,10},{9,11},{10,... | collective-permute-start | bytes 122888 | tf_op jit(solution)/shard_map/ppermute | solution.py:113
  399.2 17.6 %collective-permute-start.36 = (f32[80,128]{1,0:T(8,128)S(1)}, f32[80,128]{1,0:T(8,128)S(1)}, u32[]{:S(2)}, u32[]{:S(2)}) collective-permute-start(f32[80,128]{1,0:T(8,128)S(1)} %fusion.26.refs_4_), channel_id=1, source_target_pairs={{0,3},{1,0},{2,1},{3,2},{4,7},{5,4},{6,5},{7,6},{8,11},{9,8},{10,9... | collective-permute-start | bytes 122888 | tf_op jit(solution)/shard_map/ppermute | solution.py:113
  404.7 12.1 %collective-permute-start.30 = (bf16[512,384]{1,0:T(8,128)(2,1)S(1)}, bf16[512,384]{1,0:T(8,128)(2,1)S(1)}, u32[]{:S(2)}, u32[]{:S(2)}) collective-permute-start(bf16[512,384]{1,0:T(8,128)(2,1)S(1)} %get-tuple-element.203), channel_id=1, source_target_pairs={{0,1},{1,0},{2,3},{3,2},{4,5},{5,4},{6,7},{7,6},{8,9},{9,8},{10,11... | collective-permute-start | bytes 1179656 | tf_op jit(solution)/shard_map/ppermute | solution.py:33
  404.9 12.1 %collective-permute-start.31 = (bf16[512,384]{1,0:T(8,128)(2,1)S(1)}, bf16[512,384]{1,0:T(8,128)(2,1)S(1)}, u32[]{:S(2)}, u32[]{:S(2)}) collective-permute-start(bf16[512,384]{1,0:T(8,128)(2,1)S(1)} %get-tuple-element.201), channel_id=1, source_target_pairs={{0,2},{1,3},{2,0},{3,1},{4,6},{5,7},{6,4},{7,5},{8,10},{9,11},{10,... | collective-permute-start | bytes 1179656 | tf_op jit(solution)/shard_map/ppermute | solution.py:33
  406.5 16.8 %collective-permute-start.32 = (bf16[512,384]{1,0:T(8,128)(2,1)S(1)}, bf16[512,384]{1,0:T(8,128)(2,1)S(1)}, u32[]{:S(2)}, u32[]{:S(2)}) collective-permute-start(bf16[512,384]{1,0:T(8,128)(2,1)S(1)} %get-tuple-element.202), channel_id=1, source_target_pairs={{0,1},{1,0},{2,3},{3,2},{4,5},{5,4},{6,7},{7,6},{8,9},{9,8},{10,11... | collective-permute-start | bytes 1179656 | tf_op jit(solution)/shard_map/ppermute | solution.py:33
  408.4 15.3 %collective-permute-start.33 = (bf16[512,384]{1,0:T(8,128)(2,1)S(1)}, bf16[512,384]{1,0:T(8,128)(2,1)S(1)}, u32[]{:S(2)}, u32[]{:S(2)}) collective-permute-start(bf16[512,384]{1,0:T(8,128)(2,1)S(1)} %get-tuple-element.200), channel_id=1, source_target_pairs={{0,2},{1,3},{2,0},{3,1},{4,6},{5,7},{6,4},{7,5},{8,10},{9,11},{10,... | collective-permute-start | bytes 1179656 | tf_op jit(solution)/shard_map/ppermute | solution.py:33
  424.9 206.1 %all-gather.18.cloned.1.call-start = ((), (), s32[]{:S(2)}) async-start(), calls=%async_computation.8 | async-start | bytes 7077888 | tf_op jit(solution)/shard_map/all_gather | solution.py:185
  426.9 9.4 %collective-permute-start.38 = (bf16[512,384]{1,0:T(8,128)(2,1)S(1)}, bf16[512,384]{1,0:T(8,128)(2,1)S(1)}, u32[]{:S(2)}, u32[]{:S(2)}) collective-permute-start(bf16[512,384]{1,0:T(8,128)(2,1)S(1)} %add_convert_fusion.9), channel_id=1, source_target_pairs={{0,2},{1,3},{2,0},{3,1},{4,6},{5,7},{6,4},{7,5},{8,10},{9,11},{10,... | collective-permute-start | bytes 1179656 | tf_op jit(solution)/shard_map/ppermute | solution.py:33
  429.7 9.3 %collective-permute-start.37 = (bf16[512,384]{1,0:T(8,128)(2,1)S(1)}, bf16[512,384]{1,0:T(8,128)(2,1)S(1)}, u32[]{:S(2)}, u32[]{:S(2)}) collective-permute-start(bf16[512,384]{1,0:T(8,128)(2,1)S(1)} %add_convert_fusion.11), channel_id=1, source_target_pairs={{0,1},{1,0},{2,3},{3,2},{4,5},{5,4},{6,7},{7,6},{8,9},{9,8},{10,11... | collective-permute-start | bytes 1179656 | tf_op jit(solution)/shard_map/ppermute | solution.py:33
  441.7 8.1 %collective-permute-start.40 = (f32[80,128]{1,0:T(8,128)S(1)}, f32[80,128]{1,0:T(8,128)S(1)}, u32[]{:S(2)}, u32[]{:S(2)}) collective-permute-start(f32[80,128]{1,0:T(8,128)S(1)} %fusion.25.refs_0_), channel_id=1, source_target_pairs={{0,16},{4,20},{8,24},{12,28},{16,0},{20,4},{24,8},{28,12},{1,17},{... | collective-permute-start | bytes 122888 | tf_op jit(solution)/shard_map/ppermute | solution.py:113
  442.3 8.7 %collective-permute-start.41 = (f32[80,128]{1,0:T(8,128)S(1)}, f32[80,128]{1,0:T(8,128)S(1)}, u32[]{:S(2)}, u32[]{:S(2)}) collective-permute-start(f32[80,128]{1,0:T(8,128)S(1)} %fusion.25.refs_0_), channel_id=1, source_target_pairs={{0,24},{4,28},{8,0},{12,4},{16,8},{20,12},{24,16},{28,20},{1,25},{... | collective-permute-start | bytes 122888 | tf_op jit(solution)/shard_map/ppermute | solution.py:113
  (71 other events, 413.0 us)
Sparse Core Ops, SparseCore 0:
  9.6 84.7 all-gather.11
  96.0 80.5 all-gather.13
  200.4 87.2 reduce-scatter.2
  289.2 76.0 all-gather.9
  377.6 108.6 all-gather.15
  488.9 74.9 reduce-scatter.4
  565.7 65.2 all-gather.17

commit v3 on v2

--- a/solution.py
+++ b/solution.py
@@ -156,10 +156,8 @@
         return [scatter_rows(part, "fsdp", list(range(bits_of(lax.axis_size("fsdp"))))) for part in sides]
     me = lax.axis_index("fsdp")
     return [
-        flip(fsdp_block(sides[1], me ^ 3), "fsdp", 0),
-        flip(fsdp_block(sides[0], me ^ 3), "fsdp", 1),
-        flip(fsdp_block(sides[1], me ^ 1), "fsdp", 0),
-        flip(fsdp_block(sides[0], me ^ 2), "fsdp", 1),
+        flip(jnp.stack([fsdp_block(sides[1], me ^ 3), fsdp_block(sides[1], me ^ 1)]), "fsdp", 0),
+        flip(jnp.stack([fsdp_block(sides[0], me ^ 3), fsdp_block(sides[0], me ^ 2)]), "fsdp", 1),
     ]
 
 
@@ -167,8 +165,8 @@
     if lax.axis_size("fsdp") != 4:
         return []
     me = lax.axis_index("fsdp")
-    across = fsdp_block(sides[0], me ^ 1).astype(F32) + first[1].astype(F32)
-    along = fsdp_block(sides[1], me ^ 2).astype(F32) + first[0].astype(F32)
+    across = fsdp_block(sides[0], me ^ 1).astype(F32) + first[1][0].astype(F32)
+    along = fsdp_block(sides[1], me ^ 2).astype(F32) + first[0][0].astype(F32)
     return [flip(across.astype(BF), "fsdp", 0), flip(along.astype(BF), "fsdp", 1)]
 
 
@@ -176,17 +174,13 @@
     if lax.axis_size("fsdp") != 4:
         return first[0].astype(BF), first[1].astype(BF)
     me = lax.axis_index("fsdp")
-    left = fsdp_block(sides[0], me).astype(F32) + first[3].astype(F32) + second[0].astype(F32)
-    right = fsdp_block(sides[1], me).astype(F32) + first[2].astype(F32) + second[1].astype(F32)
+    left = fsdp_block(sides[0], me).astype(F32) + first[1][1].astype(F32) + second[0].astype(F32)
+    right = fsdp_block(sides[1], me).astype(F32) + first[0][1].astype(F32) + second[1].astype(F32)
     return left.astype(BF), right.astype(BF)
 
 
 def gather_ctx(values):
     return lax.all_gather(values, "ctx", axis=0, tiled=True)
-
-
-def scatter_ctx(values):
-    return lax.psum_scatter(values, "ctx", scatter_dimension=0, tiled=True)
 
 
 def split_cores(part):
@@ -196,12 +190,33 @@
     return [lax.dynamic_index_in_dim(blocks, k, 1, keepdims=False) for k in (core, 1 - core)]
 
 
-def scatter_places(values):
-    places, rows, columns = values.shape
-    lines = [[2 * p + k for p in range(places)] for k in range(2)]
-    return lax.psum_scatter(
-        values.reshape(places * rows, columns), "ctx", scatter_dimension=0, axis_index_groups=lines, tiled=True
-    )
+def scatter_ctx(values):
+    return lax.psum_scatter(values, "ctx", scatter_dimension=0, tiled=True)
+
+
+def shift(values, by, keep):
+    places = lax.axis_size("ctx") // 2
+    pairs = [
+        (2 * p + k, 2 * (p + by) + k) for p in range(places) for k in range(2) if keep(p) and 0 <= p + by < places
+    ]
+    return lax.ppermute(values, "ctx", pairs)
+
+
+def line_block(blocks, s):
+    places = blocks.shape[0]
+    at = (lax.axis_index("ctx") // 2 + places - s) % places
+    return lax.dynamic_index_in_dim(blocks, at, 0, keepdims=False).astype(F32)
+
+
+def line_step(blocks, step, before):
+    places = blocks.shape[0]
+    up, down = line_block(blocks, step), line_block(blocks, places - step)
+    if before:
+        up, down = up + before[0].astype(F32), down + before[1].astype(F32)
+    return [
+        shift(up.astype(BF), 1, lambda p: p <= step - 1),
+        shift(down.astype(BF), -1, lambda p: p >= places - step),
+    ]
 
 
 def nothing_kernel(*refs):
@@ -576,55 +591,95 @@
     )(at, normed, *gates, *ups)
 
 
-def grad_kernel(grad_ref, slope_ref, silu_ref, lower_ref, proj_ref, gate_ref, up_ref, mixed_ref):
+def fetch_rest(spans, at_ref, refs, lower, proj, sems):
+    n = len(spans) // 2
+    units = lower.shape[0]
+    filled = sum(rows for _, rows in spans[:n])
+    if filled < units:
+        lower[filled:, :] = jnp.zeros((units - filled, lower.shape[1]), BF)
+    copies = fetch(at_ref.at[0], refs[:n], spans[:n], lower, sems[0])
+    copies += fetch(at_ref.at[1], refs[n:], spans[n:], proj, sems[1])
+    for copy in copies:
+        copy.wait()
+
+
+def grad_kernel(spans, at_ref, grad_ref, slope_ref, silu_ref, *refs):
+    n = len(spans)
+    gate_ref, up_ref, mixed_ref, lower, proj, *sems = refs[n:]
+
+    @pl.when(pl.program_id(0) == 0)
+    def _():
+        fetch_rest(spans, at_ref, refs[:n], lower, proj, sems)
+
     grad = grad_ref[...]
-    act = matmul_nt(grad, lower_ref[...])
-    mixed_ref[...] = matmul_nt(grad, proj_ref[...]).astype(BF)
+    act = matmul_nt(grad, lower[...])
+    mixed_ref[...] = matmul_nt(grad, proj[...]).astype(BF)
     gate_ref[...] = (act * slope_ref[...].astype(F32)).astype(BF)
     up_ref[...] = (act * silu_ref[...].astype(F32)).astype(BF)
 
 
-def grad_side(grad, slope, silu, lower, proj):
+def rest_scratch(units, width, model, n):
+    return [
+        pltpu.VMEM((units, model), BF),
+        pltpu.VMEM((width, model), BF),
+        pltpu.SemaphoreType.DMA((n,)),
+        pltpu.SemaphoreType.DMA((n,)),
+    ]
+
+
+def split_rest(lower_pieces, proj_pieces):
+    lower_at, lowers, lower_spans = split_pieces(lower_pieces)
+    proj_at, projs, proj_spans = split_pieces(proj_pieces)
+    return jnp.stack([lower_at, proj_at]), lowers + projs, lower_spans + proj_spans
+
+
+def grad_side(grad, slope, silu, width, lower_pieces, proj_pieces):
     tokens, model = grad.shape
-    units, width = slope.shape[1], proj.shape[0]
+    units = slope.shape[1]
+    at, arrays, spans = split_rest(lower_pieces, proj_pieces)
     return pl.pallas_call(
-        grad_kernel,
+        functools.partial(grad_kernel, spans),
         grid=(tokens // CHUNK,),
         out_shape=(
             jax.ShapeDtypeStruct((tokens, units), BF),
             jax.ShapeDtypeStruct((tokens, units), BF),
             jax.ShapeDtypeStruct((tokens, width), BF),
         ),
-        in_specs=[
-            row_block(model),
-            row_block(units),
-            row_block(units),
-            full_block(lower),
-            full_block(proj),
-        ],
+        in_specs=[SCALAR, row_block(model), row_block(units), row_block(units)] + [ANYWHERE] * len(arrays),
         out_specs=(row_block(units), row_block(units), row_block(width)),
+        scratch_shapes=rest_scratch(units, width, model, len(arrays) // 2),
         compiler_params=pltpu.CompilerParams(vmem_limit_bytes=56 * 1024 * 1024),
         cost_estimate=pl.CostEstimate(flops=18_000_000_000, transcendentals=0, bytes_accessed=0),
         name="grad_side",
-    )(grad, slope, silu, lower, proj)
-
-
-def out_kernel(mixed_ref, act_ref, proj_ref, lower_ref, out_ref):
-    out_ref[...] = (matmul(mixed_ref[...], proj_ref[...]) + matmul(act_ref[...], lower_ref[...])).astype(BF)
-
-
-def out_side(mixed, act, proj, lower):
-    tokens, model = mixed.shape[0], proj.shape[1]
+    )(at, grad, slope, silu, *arrays)
+
+
+def out_kernel(spans, at_ref, mixed_ref, act_ref, *refs):
+    n = len(spans)
+    out_ref, lower, proj, *sems = refs[n:]
+
+    @pl.when(pl.program_id(0) == 0)
+    def _():
+        fetch_rest(spans, at_ref, refs[:n], lower, proj, sems)
+
+    out_ref[...] = (matmul(mixed_ref[...], proj[...]) + matmul(act_ref[...], lower[...])).astype(BF)
+
+
+def out_side(mixed, act, model, lower_pieces, proj_pieces):
+    tokens, width = mixed.shape
+    units = act.shape[1]
+    at, arrays, spans = split_rest(lower_pieces, proj_pieces)
     return pl.pallas_call(
-        out_kernel,
+        functools.partial(out_kernel, spans),
         grid=(tokens // CHUNK,),
         out_shape=jax.ShapeDtypeStruct((tokens, model), BF),
-        in_specs=[row_block(mixed.shape[1]), row_block(act.shape[1]), full_block(proj), full_block(lower)],
+        in_specs=[SCALAR, row_block(width), row_block(units)] + [ANYWHERE] * len(arrays),
         out_specs=row_block(model),
+        scratch_shapes=rest_scratch(units, width, model, len(arrays) // 2),
         compiler_params=pltpu.CompilerParams(vmem_limit_bytes=56 * 1024 * 1024),
         cost_estimate=pl.CostEstimate(flops=15_000_000_000, transcendentals=0, bytes_accessed=0),
         name="out_side",
-    )(mixed, act, proj, lower)
+    )(at, mixed, act, *arrays)
 
 
 def input_kernel(spans, at_ref, gate_ref, up_ref, merged_ref, hidden_ref, *refs):
@@ -820,32 +875,34 @@
     lows = stream_starts[::CHUNK] // CHUNK
     stream_starts = stream_starts.reshape(tokens // CHUNK, 1, CHUNK)
 
-    normed, merged = attn_side(hidden_all, gain_full[None], bias_full[None], b_attn_own[None], attn_pieces)
-    merged, up_near, w_rest_own = stage(merged, up_near, w_rest_own)
+    up_near, gate_far, w_rest_own = stage(up_near, gate_far, w_rest_own)
     up_far = gather_second(w_up_own, up_near)
     rest_near = gather_first(w_rest_own)
+    normed, merged = attn_side(hidden_all, gain_full[None], bias_full[None], b_attn_own[None], attn_pieces)
     mixed, *kept = attention_forward(heads, slots, lows, merged, tables, stream_starts)
-    mixed, gate_far, up_far, rest_near = stage(mixed, gate_far, up_far, rest_near)
+    mixed, up_far, rest_near = stage(mixed, up_far, rest_near)
+    rest_far = gather_second(w_rest_own, rest_near)
     gate_pieces = gathered_pieces(w_gate_own, gate_near, gate_far, shard_rows)
     up_pieces = gathered_pieces(w_up_own, up_near, up_far, shard_rows)
-    rest_far = gather_second(w_rest_own, rest_near)
     act, slope, silu = pair_side(normed, gate_pieces, up_pieces)
-    if spread:
+    if spread and shard_count == 4:
         me = lax.axis_index("fsdp")
-        if shard_count == 4:
-            rest_pieces = [w_rest_own, rest_near[0], rest_near[1], jnp.concatenate(rest_far, axis=0)]
-            origin = [me, me ^ 1, me ^ 2, me ^ 3]
+        corner = jnp.concatenate(rest_far, axis=0)
+        held = list(zip([w_rest_own, rest_near[0], rest_near[1], corner], [me, me ^ 1, me ^ 2, me ^ 3]))
+        lower_pieces = [(array, 0, unit_width, at * unit_width) for array, at in held]
+        proj_pieces = [(array, unit_width, head_width, at * head_width) for array, at in held]
+    else:
+        w_rest = rest_near[0].reshape(shard_count, -1, model)
+        w_lower = jnp.pad(w_rest[:, :unit_width].reshape(units, model), ((0, spare), (0, 0)))
+        if spread:
+            w_proj = w_rest[:, unit_width:].reshape(width, model)
         else:
-            rest_pieces = [rest_near[0].reshape(shard_count, -1, model)[i] for i in range(shard_count)]
-            origin = list(range(shard_count))
-        w_lower = placed([p[:unit_width] for p in rest_pieces], [o * unit_width for o in origin], units + spare)
-        w_proj = placed([p[unit_width:] for p in rest_pieces], [o * head_width for o in origin], width)
-    else:
-        w_lower = placed(rest_near, [0], units + spare)
-        w_proj = lax.dynamic_slice_in_dim(
-            lax.all_gather(w_out, "fsdp", axis=0, tiled=True), ctx_at * width, width, 0
-        )
-    out_part = out_side(mixed, act, w_proj, w_lower)
+            w_proj = lax.dynamic_slice_in_dim(
+                lax.all_gather(w_out, "fsdp", axis=0, tiled=True), ctx_at * width, width, 0
+            )
+        lower_pieces = [(w_lower, 0, units + spare, 0)]
+        proj_pieces = [(w_proj, 0, width, 0)]
+    out_part = out_side(mixed, act, model, lower_pieces, proj_pieces)
     out_rows = scatter_ctx(out_part)
 
     (grad_all,) = tie([grad_all], [out_part])
@@ -859,7 +916,7 @@
         rest_part = down_part[:units]
     rest_part, grad_all = stage(rest_part, grad_all)
     rest_first = scatter_first(halves(rest_part))
-    grad_gate, grad_up, grad_mixed = grad_side(grad_all, slope, silu, w_lower, w_proj)
+    grad_gate, grad_up, grad_mixed = grad_side(grad_all, slope, silu, width, lower_pieces, proj_pieces)
     grad_gate, grad_up, grad_mixed, rest_first = stage(grad_gate, grad_up, grad_mixed, rest_first)
 
     rest_second = scatter_second(halves(rest_part), rest_first)
@@ -874,6 +931,14 @@
     grad_merged, pair_first = stage(grad_merged, pair_first)
 
     pair_second = scatter_second((gate_part, up_part), pair_first)
+    attn_part = matmul_tn(normed, grad_merged).astype(BF)
+    pair_sum = jnp.concatenate(
+        [p[:, :units] for p in scatter_last((gate_part, up_part), pair_first, pair_second)], axis=1
+    )
+    attn_part, pair_sum, grad_merged = stage(attn_part, pair_sum, grad_merged)
+    pair_all = gather_ctx(pair_sum[None])
+
+    attn_first = scatter_first(halves(attn_part))
     grad_part, terms = input_side(
         grad_gate, grad_up, grad_merged, hidden_all, gate_pieces, up_pieces, attn_pieces
     )
@@ -882,48 +947,18 @@
         lax.broadcasted_iota(jnp.int32, (3, pieces, parts, head_width), 2) == ctx_at, merged_term, 0.0
     )
     terms = jnp.concatenate([terms.reshape(-1), merged_term.reshape(-1)]).reshape(-1, 128)
-    pair_sum = jnp.concatenate(
-        [p[:, :units] for p in scatter_last((gate_part, up_part), pair_first, pair_second)], axis=1
-    )
-    grad_part, terms, pair_sum, grad_merged = stage(grad_part, terms, pair_sum, grad_merged)
-    pair_all = gather_ctx(pair_sum[None])
-
+    grad_part, terms, attn_first = stage(grad_part, terms, attn_first)
+
+    attn_second = scatter_second(halves(attn_part), attn_first)
     part_own, part_other = split_cores(grad_part)
     part_other = flip(part_other, "ctx", 0)
     other_terms = others_of(terms, "ctx", 1, 2)
-    attn_part = matmul_tn(normed, grad_merged).astype(BF)
-    attn_part, part_other, terms, others = stage(attn_part, part_other, terms, other_terms[0])
+    attn_sum = jnp.concatenate(scatter_last(halves(attn_part), attn_first, attn_second), axis=1)
+    attn_sum, part_other, terms, others = stage(attn_sum, part_other, terms, other_terms[0])
+    attn_all = gather_ctx(attn_sum[None])
     terms = sum_of(terms, others, other_terms[1])
+
     part_places = (part_own.astype(F32) + part_other.astype(F32)).astype(BF)
-
-    attn_first = scatter_first(halves(attn_part))
-    other_terms = others_of(terms, "fsdp", 1, shard_count)
-    attn_first, terms, others, part_places = stage(attn_first, terms, other_terms[0], part_places)
-    terms = sum_of(terms, others, other_terms[1])
-    grad_normed = scatter_places(part_places)
-
-    attn_second = scatter_second(halves(attn_part), attn_first)
-    attn_sum = jnp.concatenate(scatter_last(halves(attn_part), attn_first, attn_second), axis=1)
-    attn_all = gather_ctx(attn_sum[None])
-    other_terms = others_of(terms, "ctx", 2, parts // 2)
-    terms, others = stage(terms, other_terms[0])
-    terms = sum_of(terms, others, other_terms[1]).reshape(-1)
-
-    float_in = hidden_in[0].astype(F32)
-    (out_rows,) = tie([out_rows], [attn_sum, terms])
-    output = (float_in + out_rows.astype(F32)).astype(BF)[None]
-    (rest_all,) = tie([rest_all], [output])
-    rest_blocks = rest_all.reshape(parts, -1, model)
-    grad_down_w = rest_blocks[:, :unit_width].reshape(-1, model).astype(F32)
-    if spread:
-        grad_proj_w = rest_blocks[:, unit_width:].reshape(-1, model).astype(F32)
-    else:
-        grad_proj_w = lax.dynamic_slice_in_dim(
-            gather_ctx(lax.psum(proj_part.astype(F32), "fsdp")), fsdp_at * shard_rows, shard_rows, 0
-        )
-    grad_down_w, grad_proj_w = stage(grad_down_w, grad_proj_w)
-    (pair_all,) = tie([pair_all], [grad_down_w])
-
     pair_plan = [
         [
             (c, side * units + p * unit_width, unit_width)
@@ -940,9 +975,37 @@
             for c in range(parts)
         ]
     ]
+    places = parts // 2
+    grad_step = line_step(part_places, 1, None)
+    other_terms = others_of(terms, "fsdp", 1, shard_count)
+    float_in = hidden_in[0].astype(F32)
+    output = (float_in + out_rows.astype(F32)).astype(BF)[None]
+    terms, others, part_places, grad_step, output = stage(terms, other_terms[0], part_places, grad_step, output)
+    terms = sum_of(terms, others, other_terms[1])
+
+    if places > 2:
+        grad_step = line_step(part_places, 2, grad_step)
+    other_terms = others_of(terms, "ctx", 2, places)
+    (rest_all,) = tie([rest_all], [output])
+    rest_blocks = rest_all.reshape(parts, -1, model)
+    grad_down_w = rest_blocks[:, :unit_width].reshape(-1, model).astype(F32)
+    if spread:
+        grad_proj_w = rest_blocks[:, unit_width:].reshape(-1, model).astype(F32)
+    else:
+        grad_proj_w = lax.dynamic_slice_in_dim(
+            gather_ctx(lax.psum(proj_part.astype(F32), "fsdp")), fsdp_at * shard_rows, shard_rows, 0
+        )
+    terms, others, grad_step, grad_down_w, grad_proj_w = stage(
+        terms, other_terms[0], grad_step, grad_down_w, grad_proj_w
+    )
+    (pair_all,) = tie([pair_all], [grad_down_w])
+    terms = sum_of(terms, others, other_terms[1]).reshape(-1)
+
+    for step in range(3, places):
+        grad_step = line_step(part_places, step, grad_step)
     grad_gate_w, grad_up_w = assemble(pair_all, pair_plan)
-    (grad_normed,) = tie([grad_normed], [grad_gate_w])
-    grad_normed = grad_normed.astype(F32)
+    part_places, grad_step, grad_gate_w, grad_up_w = stage(part_places, grad_step, grad_gate_w, grad_up_w)
+    grad_normed = line_block(part_places, 0) + grad_step[0].astype(F32) + grad_step[1].astype(F32)
 
     normal_hat, inverse_std = normalise(float_in)
     b_rows = b_qkv.shape[0]

time: 659 us -> 619 us (0.939)
  waiting for transfers between devices: 213 us -> 165 us
  starting transfers between devices: 48.1 us -> 55.7 us
    ppermute x0 -> x6, waiting for transfers between devices: none -> 122 us  [shift(): return lax.ppermute(values, 'ctx', pairs)]
    all_gather x5, waiting for transfers between devices: 93.5 us -> 0.02 us  [gather_ctx(): return lax.all_gather(values, 'ctx', axis=0, tiled=True)]
    reduce_scatter x1 -> x0, waiting for transfers between devices: 64.1 us -> none  [scatter_places(): lax.psum_scatter(values.reshape(places * rows, columns), 'ctx', scatter_d...]
    ppermute x0 -> x6, starting transfers between devices: none -> 12.5 us  [shift(): return lax.ppermute(values, 'ctx', pairs)]
    ppermute x35 -> x29, waiting for transfers between devices: 49 us -> 40.8 us  [flip(): return lax.ppermute(values, axis, [(i, i ^ 1 << bit) for i in range(count)])]
    ppermute x35 -> x29, starting transfers between devices: 39.4 us -> 32.4 us  [flip(): return lax.ppermute(values, axis, [(i, i ^ 1 << bit) for i in range(count)])]
    unnamed x145 -> x128, local copies, waits for them, and re-layouts: 24.5 us -> 27.7 us
  transfers between devices with their start and end apart: 49 -> 48, of which waited for: 19 -> 13; matrix products, arithmetic and copies ran while one was open for 26% -> 28% of each run, Pallas kernels for 27% -> 29%
where the time goes in v3:
time: 619 us; the launch traced here: 608 us
  Pallas kernels  180 us (29%)
  waiting for transfers between devices  165 us (27%)
  local copies, waits for them, and re-layouts  80.4 us (13%)
  other arithmetic  65.4 us (11%)
  starting transfers between devices  55.7 us (9%)
  matrix products  45.4 us (7%)
  between operations  16 us (3%)
    ppermute x6, waiting for transfers between devices, shift(): return lax.ppermute(values, 'ctx', pairs)  122 us
    dot_general x5, matrix products, matmul_tn(): lax.dot_general(left, right, (((0,), (0,)), ((), ())), preferred_element_...  45.4 us
    pallas_call x1, Pallas kernels, attention_backward(): pl.pallas_call(functools.partial(backward_kernel, heads), out_shape=jax.S...  41.8 us
    ppermute x29, waiting for transfers between devices, flip(): return lax.ppermute(values, axis, [(i, i ^ 1 << bit) for i in range(count)])  40.8 us
    ppermute x29, starting transfers between devices, flip(): return lax.ppermute(values, axis, [(i, i ^ 1 << bit) for i in range(count)])  32.4 us
    pallas_call x1, Pallas kernels, input_side(): pl.pallas_call(functools.partial(input_kernel, spans), grid=(tokens // CH...  30.5 us
    unnamed x128, local copies, waits for them, and re-layouts  27.7 us
    pallas_call x1, Pallas kernels, attention_forward(): pl.pallas_call(functools.partial(forward_kernel, heads), out_shape=(rows,...  22.6 us
  transfers between devices with their start and end apart: 48, of which 13 were waited for; matrix products, arithmetic and copies ran while one was open for 28% of the time, Pallas kernels for 29%

profile of v3, /device:TPU:0, one launch (start us, length us, event | category | flops | bytes accessed | tf_op | source)
XLA Modules:
  0.0 608.1 jit_solution(14541741097171153693)
XLA Ops:
  10.1 2.9 constant_dynamic-slice_fusion.10
  13.0 2.8 concatenate.40
  17.5 2.9 collective-permute-start
  22.0 4.2 constant_dynamic-slice_fusion.2
  26.3 2.4 concatenate.43.refs_0_
  30.3 2.3 concatenate.42.refs_2_
  34.8 5.6 fusion.26
  50.6 5.9 collective-permute-done.2.refs_0_
  58.6 8.4 %collective-permute-done.4.refs_2_ = bf16[256,768]{1,0:T(8,128)(2,1)} collective-permute-done((bf16[256,768]{1,0:T(8,128)(2,1)S(1)}, bf16[256,768]{1,0:T(8,128)(2,1)}, u32[]{:S(2)}, u32[]{:S(2)}) %collective-permute-start.4) | collective-permute-done | bytes 393248 | tf_op jit(solution)/shard_map/ppermute | solution.py:33
  76.9 5.4 collective-permute-done.6.refs_0_
  83.8 7.0 %collective-permute-done.8.refs_2_ = bf16[256,768]{1,0:T(8,128)(2,1)S(1)} collective-permute-done((bf16[256,768]{1,0:T(8,128)(2,1)}, bf16[256,768]{1,0:T(8,128)(2,1)S(1)}, u32[]{:S(2)}, u32[]{:S(2)}) %collective-permute-start.8) | collective-permute-done | bytes 393248 | tf_op jit(solution)/shard_map/ppermute | solution.py:33
  99.1 17.2 %attn_side.1 = (bf16[2048,2048]{1,0:T(8,128)(2,1)}, f32[2048,768]{1,0:T(8,128)}) custom-call(s32[5]{0:T(128)} %stack.141.at_ref, bf16[2048,2048]{1,0:T(8,128)(2,1)} %bitcast.252, f32[1,2048]{1,0:T(1,128)} %bitcast.250, f32[1,2048]{1,0:T(1,128)} %bitcast.251, f32[1,768]{1,0:T(1,128)} %broadcast_in_dim.150.shift_ref, ...), custom_call_target="tpu_custom_call" | custom-call | flops 17999998976 | tf_op jit(solution)/shard_map/attn_side/pallas_call | solution.py:557
  116.3 22.6 %attention_forward.1 = (bf16[2048,256]{1,0:T(8,128)(2,1)S(1)}, bf16[2048,256]{1,0:T(8,128)(2,1)S(1)}, bf16[2048,256]{1,0:T(8,128)(2,1)S(1)}, bf16[2048,256]{1,0:...) custom-call(s32[16]{0:T(128)S(1)} %select_reduce_fusion.slot_ref, s32[8]{0:T(128)S(1)} %and_select_fusion.1.low_ref, ...), custom_call_target="tpu_custom_call" | custom-call | flops 24999999488 | tf_op jit(solution)/shard_map/attention_forward/pallas_call | solution.py:446
  145.1 20.6 %pair_side.1 = (bf16[2048,768]{1,0:T(8,128)(2,1)}, bf16[2048,768]{1,0:T(8,128)(2,1)}, bf16[2048,768]{1,0:T(8,128)(2,1)}) custom-call(s32[5]{0:T(128)} %stack.141.at_ref, bf16[2048,2048]{1,0:T(8,128)(2,1)} %get-tuple-element.95.normed_ref, bf16[512,768]{1,0:T(8,128)(2,1)} %concatenate.43.refs_0_, bf16[512,768]{1,0:T(8,128)(2,1)} %get-tuple-element.102.refs_1_, ...), custom_call_target="tpu_custom_call" | custom-call | flops 28000000000 | tf_op jit(solution)/shard_map/pair_side/pallas_call | solution.py:576
  166.8 15.0 %out_side.1.refs_1_ = bf16[2048,2048]{1,0:T(8,128)(2,1)} custom-call(s32[2,4]{1,0:T(2,128)} %pad_add_fusion.at_ref, bf16[2048,256]{1,0:T(8,128)(2,1)} %get-tuple-element.114.mixed_ref, bf16[2048,768]{1,0:T(8,128)(2,1)} %get-tuple-element.113.act_ref, bf16[240,2048]{1,0:T(8,128)(2,1)} %get-tuple-element.110.refs_0_.refs_4_, ...), custom_call_target="tpu_custom_call" | custom-call | flops 15000000512 | tf_op jit(solution)/shard_map/out_side/pallas_call | solution.py:672
  182.4 10.3 %fusion.59 = bf16[768,2048]{1,0:T(8,128)(2,1)S(1)} fusion(bf16[2048,768]{1,0:T(8,128)(2,1)} %get-tuple-element.113.act_ref, bf16[2048,2048]{1,0:T(8,128)(2,1)} %tie.22.refs_1_), kind=kOutput, calls=%fused_computation.195 | convolution fusion | flops 6442450944 | bytes 14680064 | tf_op jit(solution)/shard_map/dot_general | solution.py:28
  193.9 2.4 convolution_convert_fusion.3
  196.2 2.5 pad_maximum_fusion
  198.7 2.6 fusion.55
  205.1 17.0 %grad_side.1 = (bf16[2048,768]{1,0:T(8,128)(2,1)}, bf16[2048,768]{1,0:T(8,128)(2,1)}, bf16[2048,256]{1,0:T(8,128)(2,1)}) custom-call(s32[2,4]{1,0:T(2,128)} %pad_add_fusion.at_ref, bf16[2048,2048]{1,0:T(8,128)(2,1)} %get-tuple-element.117.grad_ref, bf16[2048,768]{1,0:T(8,128)(2,1)} %get-tuple-element.118.slope_ref, ...), custom_call_target="tpu_custom_call" | custom-call | flops 17999998976 | tf_op jit(solution)/shard_map/grad_side/pallas_call | solution.py:640
  229.5 11.6 %convolution_convert_fusion.1.refs_1_ = bf16[2048,768]{1,0:T(8,128)(2,1)} fusion(bf16[2048,2048]{1,0:T(8,128)(2,1)} %get-tuple-element.95.normed_ref, bf16[2048,768]{1,0:T(8,128)(2,1)} %get-tuple-element.125.up_ref), kind=kOutput, calls=%fused_computation.8 | convolution fusion | flops 6444023808 | bytes 14680064 | tf_op jit(solution)/shard_map/dot_general | solution.py:28
  241.1 10.7 %convolution_convert_fusion.2.refs_0_ = bf16[2048,768]{1,0:T(8,128)(2,1)} fusion(bf16[2048,2048]{1,0:T(8,128)(2,1)} %get-tuple-element.95.normed_ref, bf16[2048,768]{1,0:T(8,128)(2,1)S(1)} %copy-done.32), kind=kOutput, calls=%fused_computation.9 | convolution fusion | flops 6444023808 | bytes 14680064 | tf_op jit(solution)/shard_map/dot_general | solution.py:28
  260.5 41.8 %attention_backward.1.refs_0_ = bf16[2048,768]{1,0:T(8,128)(2,1)} custom-call(s32[16]{0:T(128)S(1)} %select_reduce_fusion.slot_ref, s32[8]{0:T(128)S(1)} %and_select_fusion.1.low_ref, bf16[2048,256]{1,0:T(8,128)(2,1)S(1)} %get-tuple-element.97.q_ref, bf16[2048,256]{1,0:T(8,128)(2,1)S(1)} %get-tuple-element.98.k_ref, bf16[2048,256]{1,0:T(8,128)(2,1)S(1)} %copy-done.8, ...), custom_call_target="tpu_custom_call" | custom-call | flops 40000000000 | tf_op jit(solution)/shard_map/attention_backward/pallas_call | solution.py:471
  307.4 10.6 %convolution_convert_fusion.refs_0_ = bf16[2048,768]{1,0:T(8,128)(2,1)} fusion(bf16[2048,2048]{1,0:T(8,128)(2,1)} %get-tuple-element.95.normed_ref, bf16[2048,768]{1,0:T(8,128)(2,1)S(1)} %copy-done.11), kind=kOutput, calls=%fused_computation.7 | convolution fusion | flops 6444023808 | bytes 14680064 | tf_op jit(solution)/shard_map/dot_general | solution.py:28
  325.2 2.2 fusion.56
  332.2 30.5 %input_side.1 = (bf16[2048,2048]{1,0:T(8,128)(2,1)}, f32[2,2048]{1,0:T(2,128)}) custom-call(s32[5]{0:T(128)} %stack.141.at_ref, bf16[2048,768]{1,0:T(8,128)(2,1)} %get-tuple-element.124.gate_ref, bf16[2048,768]{1,0:T(8,128)(2,1)} %get-tuple-element.125.up_ref, bf16[2048,768]{1,0:T(8,128)(2,1)} %get-tuple-element.136.merged_ref, ...), custom_call_target="tpu_custom_call" | custom-call | flops 30000001024 | tf_op jit(solution)/shard_map/input_side/pallas_call | solution.py:713
  365.7 2.7 dynamic-slice_bitcast_fusion
  371.5 8.6 %collective-permute-done.26 = bf16[512,384]{1,0:T(8,128)(2,1)S(1)} collective-permute-done((bf16[512,384]{1,0:T(8,128)(2,1)S(1)}, bf16[512,384]{1,0:T(8,128)(2,1)S(1)}, u32[]{:S(2)}, u32[]{:S(2)}) %collective-permute-start.26) | collective-permute-done | bytes 393248 | tf_op jit(solution)/shard_map/ppermute | solution.py:33
  385.4 5.5 fusion.refs_4_
  394.4 3.7 collective-permute-start.33
  402.3 2.7 fusion.12
  405.1 38.6 %collective-permute-done.33.refs_5_ = bf16[256,2048]{1,0:T(8,128)(2,1)S(1)} collective-permute-done((bf16[256,2048]{1,0:T(8,128)(2,1)}, bf16[256,2048]{1,0:T(8,128)(2,1)S(1)}, u32[]{:S(2)}, u32[]{:S(2)}) %collective-permute-start.33) | collective-permute-done | bytes 1048608 | tf_op jit(solution)/shard_map/ppermute | solution.py:202
  448.2 2.4 collective-permute-start.35
  451.9 2.8 collective-permute-start.37
  454.7 3.3 slice.206
  462.3 6.4 %bitcast_convert_fusion.refs_6_ = f32[1408,2048]{1,0:T(8,128)} fusion(bf16[8,176,2048]{2,1,0:T(8,128)(2,1)S(1)} %slice.206), kind=kLoop, calls=%fused_computation.4 | loop fusion | flops 2883584 | bytes 17301504 | tf_op jit(solution)/shard_map/convert_element_type | solution.py:991
  470.4 2.7 bitcast_convert_fusion.1.refs_7_
  473.1 26.6 %collective-permute-done.38.refs_4_ = bf16[256,2048]{1,0:T(8,128)(2,1)S(1)} collective-permute-done((bf16[256,2048]{1,0:T(8,128)(2,1)S(1)}, bf16[256,2048]{1,0:T(8,128)(2,1)S(1)}, u32[]{:S(2)}, u32[]{:S(2)}) %collective-permute-start.38) | collective-permute-done | bytes 1048608 | tf_op jit(solution)/shard_map/ppermute | solution.py:202
  501.7 4.4 fusion.18
  506.1 4.4 collective-permute-start.40
  513.3 4.3 copy-done.2
  517.6 9.0 %assemble.2 = (f32[512,5632]{1,0:T(8,128)}, f32[512,5632]{1,0:T(8,128)}) custom-call(bf16[8,512,1408]{2,1,0:T(8,128)(2,1)S(1)} %copy-done.2), custom_call_target="tpu_custom_call" | custom-call | tf_op jit(solution)/shard_map/assemble/pallas_call | solution.py:746
  526.6 29.0 %collective-permute-done.40.refs_1_ = bf16[256,2048]{1,0:T(8,128)(2,1)S(1)} collective-permute-done((bf16[256,2048]{1,0:T(8,128)(2,1)}, bf16[256,2048]{1,0:T(8,128)(2,1)S(1)}, u32[]{:S(2)}, u32[]{:S(2)}) %collective-permute-start.40) | collective-permute-done | bytes 1048608 | tf_op jit(solution)/shard_map/ppermute | solution.py:202
  555.6 28.2 %collective-permute-done.41.refs_2_ = bf16[256,2048]{1,0:T(8,128)(2,1)S(1)} collective-permute-done((bf16[256,2048]{1,0:T(8,128)(2,1)}, bf16[256,2048]{1,0:T(8,128)(2,1)S(1)}, u32[]{:S(2)}, u32[]{:S(2)}) %collective-permute-start.41) | collective-permute-done | bytes 1048608 | tf_op jit(solution)/shard_map/ppermute | solution.py:202
  584.7 2.9 fusion.46
  587.7 3.5 fusion.30.refs_1_
  591.2 2.8 copy-done.3
  594.0 6.8 %assemble.3 = f32[512,6144]{1,0:T(8,128)} custom-call(bf16[8,512,768]{2,1,0:T(8,128)(2,1)S(1)} %copy-done.3), custom_call_target="tpu_custom_call" | custom-call | tf_op jit(solution)/shard_map/assemble/pallas_call | solution.py:746
  (334 shorter events, 123.6 us)
Async XLA Ops:
  7.2 91.9 %all-gather.12.cloned.1.call-start = ((), (), s32[]{:S(2)}) async-start(), calls=%async_computation.3 | async-start | bytes 9437184 | tf_op jit(solution)/shard_map/all_gather | solution.py:183
  7.9 174.4 %all-gather.14.cloned.1.call-start = ((), (), s32[]{:S(2)}) async-start(), calls=%async_computation.4 | async-start | bytes 9437184 | tf_op jit(solution)/shard_map/all_gather | solution.py:183
  8.7 393.6 %reduce-scatter.2.cloned.1.call-start = ((), (), s32[]{:S(2)}) async-start(), calls=%async_computation.1 | async-start | bytes 9437184 | tf_op jit(solution)/shard_map/reduce_scatter | solution.py:194
  17.5 24.5 %collective-permute-start = (bf16[528,768]{1,0:T(8,128)(2,1)}, bf16[528,768]{1,0:T(8,128)(2,1)}, u32[]{:S(2)}, u32[]{:S(2)}) collective-permute-start(bf16[528,768]{1,0:T(8,128)(2,1)} %pad_maximum_fusion.8.refs_0_.refs_10_), channel_id=1, source_target_pairs={{0,1},{1,0},{2,3},{3,2},{4,5},{5,4},{6,7},{7,6},{8,9},{9,8},{10,11... | collective-permute-start | bytes 2433032 | tf_op jit(solution)/shard_map/ppermute | solution.py:33
  20.5 21.6 %collective-permute-start.1 = (bf16[528,768]{1,0:T(8,128)(2,1)}, bf16[528,768]{1,0:T(8,128)(2,1)S(1)}, u32[]{:S(2)}, u32[]{:S(2)}) collective-permute-start(bf16[528,768]{1,0:T(8,128)(2,1)} %pad_maximum_fusion.8.refs_0_.refs_10_), channel_id=1, source_target_pairs={{0,2},{1,3},{2,0},{3,1},{4,6},{5,7},{6,4},{7,5},{8,10},{9,11},{10,... | collective-permute-start | bytes 2433032 | tf_op jit(solution)/shard_map/ppermute | solution.py:33
  28.6 27.9 %collective-permute-start.2 = (bf16[512,768]{1,0:T(8,128)(2,1)}, bf16[512,768]{1,0:T(8,128)(2,1)}, u32[]{:S(2)}, u32[]{:S(2)}) collective-permute-start(bf16[512,768]{1,0:T(8,128)(2,1)} %concatenate.43.refs_0_), channel_id=1, source_target_pairs={{0,1},{1,0},{2,3},{3,2},{4,5},{5,4},{6,7},{7,6},{8,9},{9,8},{10,11... | collective-permute-start | bytes 2359304 | tf_op jit(solution)/shard_map/ppermute | solution.py:33
  29.7 28.9 %collective-permute-start.3 = (bf16[512,768]{1,0:T(8,128)(2,1)}, bf16[512,768]{1,0:T(8,128)(2,1)}, u32[]{:S(2)}, u32[]{:S(2)}) collective-permute-start(bf16[512,768]{1,0:T(8,128)(2,1)} %concatenate.43.refs_0_), channel_id=1, source_target_pairs={{0,2},{1,3},{2,0},{3,1},{4,6},{5,7},{6,4},{7,5},{8,10},{9,11},{10,... | collective-permute-start | bytes 2359304 | tf_op jit(solution)/shard_map/ppermute | solution.py:33
  44.0 23.1 %collective-permute-start.5 = (bf16[272,768]{1,0:T(8,128)(2,1)S(1)}, bf16[272,768]{1,0:T(8,128)(2,1)S(1)}, u32[]{:S(2)}, u32[]{:S(2)}) collective-permute-start(bf16[272,768]{1,0:T(8,128)(2,1)S(1)} %slice.149), channel_id=1, source_target_pairs={{0,1},{1,0},{2,3},{3,2},{4,5},{5,4},{6,7},{7,6},{8,9},{9,8},{10,11... | collective-permute-start | bytes 1253384 | tf_op jit(solution)/shard_map/ppermute | solution.py:33
  47.0 20.0 %collective-permute-start.4 = (bf16[256,768]{1,0:T(8,128)(2,1)S(1)}, bf16[256,768]{1,0:T(8,128)(2,1)}, u32[]{:S(2)}, u32[]{:S(2)}) collective-permute-start(bf16[256,768]{1,0:T(8,128)(2,1)S(1)} %slice.148), channel_id=1, source_target_pairs={{0,2},{1,3},{2,0},{3,1},{4,6},{5,7},{6,4},{7,5},{8,10},{9,11},{10,... | collective-permute-start | bytes 1179656 | tf_op jit(solution)/shard_map/ppermute | solution.py:33
  48.1 34.2 %collective-permute-start.6 = (bf16[512,768]{1,0:T(8,128)(2,1)}, bf16[512,768]{1,0:T(8,128)(2,1)S(1)}, u32[]{:S(2)}, u32[]{:S(2)}) collective-permute-start(bf16[512,768]{1,0:T(8,128)(2,1)} %get-tuple-element.104.refs_5_), channel_id=1, source_target_pairs={{0,1},{1,0},{2,3},{3,2},{4,5},{5,4},{6,7},{7,6},{8,9},{9,8},{10,11... | collective-permute-start | bytes 2359304 | tf_op jit(solution)/shard_map/ppermute | solution.py:33
  56.5 27.3 %collective-permute-start.7 = (bf16[512,768]{1,0:T(8,128)(2,1)}, bf16[512,768]{1,0:T(8,128)(2,1)S(1)}, u32[]{:S(2)}, u32[]{:S(2)}) collective-permute-start(bf16[512,768]{1,0:T(8,128)(2,1)} %get-tuple-element.104.refs_5_), channel_id=1, source_target_pairs={{0,2},{1,3},{2,0},{3,1},{4,6},{5,7},{6,4},{7,5},{8,10},{9,11},{10,... | collective-permute-start | bytes 2359304 | tf_op jit(solution)/shard_map/ppermute | solution.py:33
  69.6 21.2 %collective-permute-start.8 = (bf16[256,768]{1,0:T(8,128)(2,1)}, bf16[256,768]{1,0:T(8,128)(2,1)S(1)}, u32[]{:S(2)}, u32[]{:S(2)}) collective-permute-start(bf16[256,768]{1,0:T(8,128)(2,1)} %slice.155), channel_id=1, source_target_pairs={{0,2},{1,3},{2,0},{3,1},{4,6},{5,7},{6,4},{7,5},{8,10},{9,11},{10,... | collective-permute-start | bytes 1179656 | tf_op jit(solution)/shard_map/ppermute | solution.py:33
  72.9 17.9 %collective-permute-start.9 = (bf16[256,768]{1,0:T(8,128)(2,1)}, bf16[256,768]{1,0:T(8,128)(2,1)}, u32[]{:S(2)}, u32[]{:S(2)}) collective-permute-start(bf16[256,768]{1,0:T(8,128)(2,1)} %slice.156), channel_id=1, source_target_pairs={{0,1},{1,0},{2,3},{3,2},{4,5},{5,4},{6,7},{7,6},{8,9},{9,8},{10,11... | collective-permute-start | bytes 1179656 | tf_op jit(solution)/shard_map/ppermute | solution.py:33
  91.5 49.4 %collective-permute-start.12 = (bf16[240,2048]{1,0:T(8,128)(2,1)}, bf16[240,2048]{1,0:T(8,128)(2,1)}, u32[]{:S(2)}, u32[]{:S(2)}) collective-permute-start(bf16[240,2048]{1,0:T(8,128)(2,1)} %get-tuple-element.110.refs_0_.refs_4_), channel_id=1, source_target_pairs={{0,1},{1,0},{2,3},{3,2},{4,5},{5,4},{6,7},{7,6},{8,9},{9,8},{10,11... | collective-permute-start | bytes 2949128 | tf_op jit(solution)/shard_map/ppermute | solution.py:33
  91.9 49.0 %collective-permute-start.13 = (bf16[240,2048]{1,0:T(8,128)(2,1)}, bf16[240,2048]{1,0:T(8,128)(2,1)}, u32[]{:S(2)}, u32[]{:S(2)}) collective-permute-start(bf16[240,2048]{1,0:T(8,128)(2,1)} %get-tuple-element.110.refs_0_.refs_4_), channel_id=1, source_target_pairs={{0,2},{1,3},{2,0},{3,1},{4,6},{5,7},{6,4},{7,5},{8,10},{9,11},{10,... | collective-permute-start | bytes 2949128 | tf_op jit(solution)/shard_map/ppermute | solution.py:33
  95.4 45.5 %collective-permute-start.10 = (bf16[256,768]{1,0:T(8,128)(2,1)}, bf16[256,768]{1,0:T(8,128)(2,1)}, u32[]{:S(2)}, u32[]{:S(2)}) collective-permute-start(bf16[256,768]{1,0:T(8,128)(2,1)} %slice.157), channel_id=1, source_target_pairs={{0,2},{1,3},{2,0},{3,1},{4,6},{5,7},{6,4},{7,5},{8,10},{9,11},{10,... | collective-permute-start | bytes 1179656 | tf_op jit(solution)/shard_map/ppermute | solution.py:33
  97.4 43.5 %collective-permute-start.11 = (bf16[256,768]{1,0:T(8,128)(2,1)}, bf16[256,768]{1,0:T(8,128)(2,1)}, u32[]{:S(2)}, u32[]{:S(2)}) collective-permute-start(bf16[256,768]{1,0:T(8,128)(2,1)} %slice.158), channel_id=1, source_target_pairs={{0,1},{1,0},{2,3},{3,2},{4,5},{5,4},{6,7},{7,6},{8,9},{9,8},{10,11... | collective-permute-start | bytes 1179656 | tf_op jit(solution)/shard_map/ppermute | solution.py:33
  142.0 23.7 %collective-permute-start.14 = (bf16[112,2048]{1,0:T(8,128)(2,1)S(1)}, bf16[112,2048]{1,0:T(8,128)(2,1)S(1)}, u32[]{:S(2)}, u32[]{:S(2)}) collective-permute-start(bf16[112,2048]{1,0:T(8,128)(2,1)S(1)} %slice.159), channel_id=1, source_target_pairs={{0,2},{1,3},{2,0},{3,1},{4,6},{5,7},{6,4},{7,5},{8,10},{9,11},{10,... | collective-permute-start | bytes 1376264 | tf_op jit(solution)/shard_map/ppermute | solution.py:33
  144.7 21.1 %collective-permute-start.15 = (bf16[128,2048]{1,0:T(8,128)(2,1)S(1)}, bf16[128,2048]{1,0:T(8,128)(2,1)S(1)}, u32[]{:S(2)}, u32[]{:S(2)}) collective-permute-start(bf16[128,2048]{1,0:T(8,128)(2,1)S(1)} %slice.160), channel_id=1, source_target_pairs={{0,1},{1,0},{2,3},{3,2},{4,5},{5,4},{6,7},{7,6},{8,9},{9,8},{10,11... | collective-permute-start | bytes 1572872 | tf_op jit(solution)/shard_map/ppermute | solution.py:33
  181.8 272.9 %all-gather.10.cloned.1.call-start = ((), (), s32[]{:S(2)}) async-start(), calls=%async_computation.2 | async-start | bytes 8847360 | tf_op jit(solution)/shard_map/all_gather | solution.py:183
  201.5 21.2 %collective-permute-start.17 = (bf16[2,240,1024]{2,1,0:T(8,128)(2,1)S(1)}, bf16[2,240,1024]{2,1,0:T(8,128)(2,1)}, u32[]{:S(2)}, u32[]{:S(2)}) collective-permute-start(bf16[2,240,1024]{2,1,0:T(8,128)(2,1)S(1)} %pad_maximum_fusion.6), channel_id=1, source_target_pairs={{0,2},{1,3},{2,0},{3,1},{4,6},{5,7},{6,4},{7,5},{8,10},{9,11},{10,... | collective-permute-start | bytes 2949128 | tf_op jit(solution)/shard_map/ppermute | solution.py:33
  203.4 21.2 %collective-permute-start.16 = (bf16[2,240,1024]{2,1,0:T(8,128)(2,1)S(1)}, bf16[2,240,1024]{2,1,0:T(8,128)(2,1)}, u32[]{:S(2)}, u32[]{:S(2)}) collective-permute-start(bf16[2,240,1024]{2,1,0:T(8,128)(2,1)S(1)} %pad_maximum_fusion.5), channel_id=1, source_target_pairs={{0,1},{1,0},{2,3},{3,2},{4,5},{5,4},{6,7},{7,6},{8,9},{9,8},{10,11... | collective-permute-start | bytes 2949128 | tf_op jit(solution)/shard_map/ppermute | solution.py:33
  226.0 25.8 %collective-permute-start.18 = (bf16[240,1024]{1,0:T(8,128)(2,1)S(1)}, bf16[240,1024]{1,0:T(8,128)(2,1)S(1)}, u32[]{:S(2)}, u32[]{:S(2)}) collective-permute-start(bf16[240,1024]{1,0:T(8,128)(2,1)S(1)} %fusion.34), channel_id=1, source_target_pairs={{0,1},{1,0},{2,3},{3,2},{4,5},{5,4},{6,7},{7,6},{8,9},{9,8},{10,11... | collective-permute-start | bytes 1474568 | tf_op jit(solution)/shard_map/ppermute | solution.py:33
  228.7 24.5 %collective-permute-start.19 = (bf16[240,1024]{1,0:T(8,128)(2,1)S(1)}, bf16[240,1024]{1,0:T(8,128)(2,1)S(1)}, u32[]{:S(2)}, u32[]{:S(2)}) collective-permute-start(bf16[240,1024]{1,0:T(8,128)(2,1)S(1)} %fusion.31), channel_id=1, source_target_pairs={{0,2},{1,3},{2,0},{3,1},{4,6},{5,7},{6,4},{7,5},{8,10},{9,11},{10,... | collective-permute-start | bytes 1474568 | tf_op jit(solution)/shard_map/ppermute | solution.py:33
  255.7 257.6 %all-gather.16.cloned.1.call-start = ((), (), s32[]{:S(2)}) async-start(), calls=%async_computation.5 | async-start | bytes 12976128 | tf_op jit(solution)/shard_map/all_gather | solution.py:183
  257.6 44.7 %collective-permute-start.21 = (bf16[2,512,768]{2,1,0:T(8,128)(2,1)S(1)}, bf16[2,512,768]{2,1,0:T(8,128)(2,1)}, u32[]{:S(2)}, u32[]{:S(2)}) collective-permute-start(bf16[2,512,768]{2,1,0:T(8,128)(2,1)S(1)} %pad_maximum_fusion.2), channel_id=1, source_target_pairs={{0,2},{1,3},{2,0},{3,1},{4,6},{5,7},{6,4},{7,5},{8,10},{9,11},{10,... | collective-permute-start | bytes 4718600 | tf_op jit(solution)/shard_map/ppermute | solution.py:33
  259.2 43.1 %collective-permute-start.20 = (bf16[2,512,768]{2,1,0:T(8,128)(2,1)S(1)}, bf16[2,512,768]{2,1,0:T(8,128)(2,1)}, u32[]{:S(2)}, u32[]{:S(2)}) collective-permute-start(bf16[2,512,768]{2,1,0:T(8,128)(2,1)S(1)} %pad_maximum_fusion.1), channel_id=1, source_target_pairs={{0,1},{1,0},{2,3},{3,2},{4,5},{5,4},{6,7},{7,6},{8,9},{9,8},{10,11... | collective-permute-start | bytes 4718600 | tf_op jit(solution)/shard_map/ppermute | solution.py:33
  304.1 16.3 %collective-permute-start.22 = (bf16[512,768]{1,0:T(8,128)(2,1)S(1)}, bf16[512,768]{1,0:T(8,128)(2,1)S(1)}, u32[]{:S(2)}, u32[]{:S(2)}) collective-permute-start(bf16[512,768]{1,0:T(8,128)(2,1)S(1)} %fusion.23), channel_id=1, source_target_pairs={{0,1},{1,0},{2,3},{3,2},{4,5},{5,4},{6,7},{7,6},{8,9},{9,8},{10,11... | collective-permute-start | bytes 2359304 | tf_op jit(solution)/shard_map/ppermute | solution.py:33
  306.5 15.3 %collective-permute-start.23 = (bf16[512,768]{1,0:T(8,128)(2,1)S(1)}, bf16[512,768]{1,0:T(8,128)(2,1)S(1)}, u32[]{:S(2)}, u32[]{:S(2)}) collective-permute-start(bf16[512,768]{1,0:T(8,128)(2,1)S(1)} %fusion.20), channel_id=1, source_target_pairs={{0,2},{1,3},{2,0},{3,1},{4,6},{5,7},{6,4},{7,5},{8,10},{9,11},{10,... | collective-permute-start | bytes 2359304 | tf_op jit(solution)/shard_map/ppermute | solution.py:33
  324.9 266.3 %all-gather.18.cloned.1.call-start = ((), (), s32[]{:S(2)}) async-start(), calls=%async_computation.6 | async-start | bytes 7077888 | tf_op jit(solution)/shard_map/all_gather | solution.py:183
  328.7 36.1 %collective-permute-start.25 = (bf16[2,512,384]{2,1,0:T(8,128)(2,1)}, bf16[2,512,384]{2,1,0:T(8,128)(2,1)S(1)}, u32[]{:S(2)}, u32[]{:S(2)}) collective-permute-start(bf16[2,512,384]{2,1,0:T(8,128)(2,1)} %pad_maximum_fusion.10), channel_id=1, source_target_pairs={{0,2},{1,3},{2,0},{3,1},{4,6},{5,7},{6,4},{7,5},{8,10},{9,11},{10,... | collective-permute-start | bytes 2359304 | tf_op jit(solution)/shard_map/ppermute | solution.py:33
  331.0 33.8 %collective-permute-start.24 = (bf16[2,512,384]{2,1,0:T(8,128)(2,1)}, bf16[2,512,384]{2,1,0:T(8,128)(2,1)}, u32[]{:S(2)}, u32[]{:S(2)}) collective-permute-start(bf16[2,512,384]{2,1,0:T(8,128)(2,1)} %pad_maximum_fusion.9), channel_id=1, source_target_pairs={{0,1},{1,0},{2,3},{3,2},{4,5},{5,4},{6,7},{7,6},{8,9},{9,8},{10,11... | collective-permute-start | bytes 2359304 | tf_op jit(solution)/shard_map/ppermute | solution.py:33
  368.4 15.5 %collective-permute-start.28 = (bf16[4,256,2048]{2,1,0:T(8,128)(2,1)S(1)}, bf16[4,256,2048]{2,1,0:T(8,128)(2,1)}, u32[]{:S(2)}, u32[]{:S(2)}) collective-permute-start(bf16[4,256,2048]{2,1,0:T(8,128)(2,1)S(1)} %dynamic-slice_bitcast_fusion), channel_id=1, source_target_pairs={{0,4},{4,0},{8,12},{12,8},{16,20},{20,16},{24,28},{28,24},{1,5},{5... | collective-permute-start | bytes 12582920 | tf_op jit(solution)/shard_map/ppermute | solution.py:33
  368.7 11.4 %collective-permute-start.26 = (bf16[512,384]{1,0:T(8,128)(2,1)S(1)}, bf16[512,384]{1,0:T(8,128)(2,1)S(1)}, u32[]{:S(2)}, u32[]{:S(2)}) collective-permute-start(bf16[512,384]{1,0:T(8,128)(2,1)S(1)} %fusion.40), channel_id=1, source_target_pairs={{0,1},{1,0},{2,3},{3,2},{4,5},{5,4},{6,7},{7,6},{8,9},{9,8},{10,11... | collective-permute-start | bytes 1179656 | tf_op jit(solution)/shard_map/ppermute | solution.py:33
  370.7 11.2 %collective-permute-start.27 = (bf16[512,384]{1,0:T(8,128)(2,1)S(1)}, bf16[512,384]{1,0:T(8,128)(2,1)S(1)}, u32[]{:S(2)}, u32[]{:S(2)}) collective-permute-start(bf16[512,384]{1,0:T(8,128)(2,1)S(1)} %fusion.37), channel_id=1, source_target_pairs={{0,2},{1,3},{2,0},{3,1},{4,6},{5,7},{6,4},{7,5},{8,10},{9,11},{10,... | collective-permute-start | bytes 1179656 | tf_op jit(solution)/shard_map/ppermute | solution.py:33
  371.5 12.4 %collective-permute-start.29 = (f32[80,128]{1,0:T(8,128)S(1)}, f32[80,128]{1,0:T(8,128)S(1)}, u32[]{:S(2)}, u32[]{:S(2)}) collective-permute-start(f32[80,128]{1,0:T(8,128)S(1)} %copy-done.36), channel_id=1, source_target_pairs={{0,4},{4,0},{8,12},{12,8},{16,20},{20,16},{24,28},{28,24},{1,5},{5... | collective-permute-start | bytes 122888 | tf_op jit(solution)/shard_map/ppermute | solution.py:113
  394.4 49.3 %collective-permute-start.33 = (bf16[256,2048]{1,0:T(8,128)(2,1)}, bf16[256,2048]{1,0:T(8,128)(2,1)S(1)}, u32[]{:S(2)}, u32[]{:S(2)}) collective-permute-start(bf16[256,2048]{1,0:T(8,128)(2,1)} %get-tuple-element.201), channel_id=1, source_target_pairs={{0,8},{4,12},{1,9},{5,13},{2,10},{6,14},{3,11},{7,15}} | collective-permute-start | bytes 3145736 | tf_op jit(solution)/shard_map/ppermute | solution.py:202
  398.0 45.7 %collective-permute-start.34 = (bf16[256,2048]{1,0:T(8,128)(2,1)}, bf16[256,2048]{1,0:T(8,128)(2,1)S(1)}, u32[]{:S(2)}, u32[]{:S(2)}) collective-permute-start(bf16[256,2048]{1,0:T(8,128)(2,1)} %get-tuple-element.200), channel_id=1, source_target_pairs={{24,16},{28,20},{25,17},{29,21},{26,18},{30,22},{27,19},{31,23}} | collective-permute-start | bytes 3145736 | tf_op jit(solution)/shard_map/ppermute | solution.py:202
  398.9 6.2 %collective-permute-start.30 = (f32[80,128]{1,0:T(8,128)S(1)}, f32[80,128]{1,0:T(8,128)S(1)}, u32[]{:S(2)}, u32[]{:S(2)}) collective-permute-start(f32[80,128]{1,0:T(8,128)S(1)} %fusion.49.refs_0_), channel_id=1, source_target_pairs={{0,1},{1,2},{2,3},{3,0},{4,5},{5,6},{6,7},{7,4},{8,9},{9,10},{10,1... | collective-permute-start | bytes 122888 | tf_op jit(solution)/shard_map/ppermute | solution.py:113
  400.1 4.9 collective-permute-start.31
  400.7 4.4 collective-permute-start.32
  448.2 24.9 %collective-permute-start.35 = (f32[80,128]{1,0:T(8,128)S(1)}, f32[80,128]{1,0:T(8,128)S(1)}, u32[]{:S(2)}, u32[]{:S(2)}) collective-permute-start(f32[80,128]{1,0:T(8,128)S(1)} %fusion.48.refs_0_), channel_id=1, source_target_pairs={{0,8},{4,12},{8,16},{12,20},{16,24},{20,28},{24,0},{28,4},{1,9},{5... | collective-permute-start | bytes 122888 | tf_op jit(solution)/shard_map/ppermute | solution.py:113
  450.6 22.5 %collective-permute-start.36 = (f32[80,128]{1,0:T(8,128)S(1)}, f32[80,128]{1,0:T(8,128)S(1)}, u32[]{:S(2)}, u32[]{:S(2)}) collective-permute-start(f32[80,128]{1,0:T(8,128)S(1)} %fusion.48.refs_0_), channel_id=1, source_target_pairs={{0,16},{4,20},{8,24},{12,28},{16,0},{20,4},{24,8},{28,12},{1,17},{... | collective-permute-start | bytes 122888 | tf_op jit(solution)/shard_map/ppermute | solution.py:113
  451.9 21.3 %collective-permute-start.37 = (f32[80,128]{1,0:T(8,128)S(1)}, f32[80,128]{1,0:T(8,128)S(1)}, u32[]{:S(2)}, u32[]{:S(2)}) collective-permute-start(f32[80,128]{1,0:T(8,128)S(1)} %fusion.48.refs_0_), channel_id=1, source_target_pairs={{0,24},{4,28},{8,0},{12,4},{16,8},{20,12},{24,16},{28,20},{1,25},{... | collective-permute-start | bytes 122888 | tf_op jit(solution)/shard_map/ppermute | solution.py:113
  459.9 39.8 %collective-permute-start.38 = (bf16[256,2048]{1,0:T(8,128)(2,1)S(1)}, bf16[256,2048]{1,0:T(8,128)(2,1)S(1)}, u32[]{:S(2)}, u32[]{:S(2)}) collective-permute-start(bf16[256,2048]{1,0:T(8,128)(2,1)S(1)} %get-tuple-element.199), channel_id=1, source_target_pairs={{0,8},{4,12},{8,16},{12,20},{1,9},{5,13},{9,17},{13,21},{2,10},{6,... | collective-permute-start | bytes 3145736 | tf_op jit(solution)/shard_map/ppermute | solution.py:202
  461.3 38.4 %collective-permute-start.39 = (bf16[256,2048]{1,0:T(8,128)(2,1)S(1)}, bf16[256,2048]{1,0:T(8,128)(2,1)S(1)}, u32[]{:S(2)}, u32[]{:S(2)}) collective-permute-start(bf16[256,2048]{1,0:T(8,128)(2,1)S(1)} %get-tuple-element.198), channel_id=1, source_target_pairs={{16,8},{20,12},{24,16},{28,20},{17,9},{21,13},{25,17},{29,21},{18,... | collective-permute-start | bytes 3145736 | tf_op jit(solution)/shard_map/ppermute | solution.py:202
  506.1 49.5 %collective-permute-start.40 = (bf16[256,2048]{1,0:T(8,128)(2,1)}, bf16[256,2048]{1,0:T(8,128)(2,1)S(1)}, u32[]{:S(2)}, u32[]{:S(2)}) collective-permute-start(bf16[256,2048]{1,0:T(8,128)(2,1)} %get-tuple-element.197), channel_id=1, source_target_pairs={{0,8},{4,12},{8,16},{12,20},{16,24},{20,28},{1,9},{5,13},{9,17},{1... | collective-permute-start | bytes 3145736 | tf_op jit(solution)/shard_map/ppermute | solution.py:202
  510.5 73.2 %collective-permute-start.41 = (bf16[256,2048]{1,0:T(8,128)(2,1)}, bf16[256,2048]{1,0:T(8,128)(2,1)S(1)}, u32[]{:S(2)}, u32[]{:S(2)}) collective-permute-start(bf16[256,2048]{1,0:T(8,128)(2,1)} %get-tuple-element.196), channel_id=1, source_target_pairs={{8,0},{12,4},{16,8},{20,12},{24,16},{28,20},{9,1},{13,5},{17,9},{2... | collective-permute-start | bytes 3145736 | tf_op jit(solution)/shard_map/ppermute | solution.py:202
  (60 other events, 531.9 us)
Sparse Core Ops, SparseCore 0:
  9.6 84.7 all-gather.11
  96.0 80.5 all-gather.13
  181.9 90.2 reduce-scatter.1
  273.7 76.0 all-gather.9
  351.3 143.0 all-gather.15
  495.9 92.6 all-gather.17

commit v4 on v3

--- a/solution.py
+++ b/solution.py
@@ -208,6 +208,11 @@
     return lax.dynamic_index_in_dim(blocks, at, 0, keepdims=False).astype(F32)
 
 
+def line_start(ends):
+    last = lax.axis_size("ctx") // 2 - 1
+    return [shift(ends[0], 1, lambda p: p <= 0), shift(ends[1], -1, lambda p: p >= last)]
+
+
 def line_step(blocks, step, before):
     places = blocks.shape[0]
     up, down = line_block(blocks, step), line_block(blocks, places - step)
@@ -217,6 +222,26 @@
         shift(up.astype(BF), 1, lambda p: p <= step - 1),
         shift(down.astype(BF), -1, lambda p: p >= places - step),
     ]
+
+
+def gather_step(step, before):
+    places = lax.axis_size("ctx") // 2
+    return [
+        shift(before[0], 1, lambda p: p >= step - 1),
+        shift(before[1], -1, lambda p: p <= places - step),
+    ]
+
+
+def line_origins():
+    me = lax.axis_index("ctx")
+    places = lax.axis_size("ctx") // 2
+    at, core = me // 2, me % 2
+    out = [me, me ^ 1]
+    for s in range(1, places):
+        ends = (jnp.where(at >= s, at - s, -1), jnp.where(at + s < places, at + s, -1))
+        for j in range(2):
+            out += [jnp.where(p < 0, -1, 2 * p + (core ^ j)) for p in ends]
+    return jnp.stack(out).astype(jnp.int32)
 
 
 def nothing_kernel(*refs):
@@ -752,6 +777,44 @@
         compiler_params=pltpu.CompilerParams(vmem_limit_bytes=40 * 1024 * 1024),
         name="assemble",
     )(gathered)
+
+
+def assemble_line_kernel(plan, count, at_ref, *refs):
+    target, held = refs[count], refs[count + 1]
+    for n in range(count):
+
+        @pl.when(at_ref[n] >= 0)
+        def _():
+            held[jnp.maximum(at_ref[n], 0)] = refs[n][0]
+
+    at = 0
+    for part, offset, width in plan:
+        target[:, at : at + width] = held[part, :, offset : offset + width].astype(F32)
+        at += width
+
+
+def assemble_line(sources, origins, plan):
+    parts = lax.axis_size("ctx")
+    rows, columns = sources[0][0].shape[1:]
+    step = 64
+    width = sum(piece[2] for piece in plan)
+
+    def block(n, index):
+        return pl.BlockSpec((1, step, columns), lambda i, at: (index, jnp.where(at[n] >= 0, i, 0), 0))
+
+    return pl.pallas_call(
+        functools.partial(assemble_line_kernel, plan, len(sources)),
+        out_shape=jax.ShapeDtypeStruct((rows, width), F32),
+        grid_spec=pltpu.PrefetchScalarGridSpec(
+            num_scalar_prefetch=1,
+            grid=(rows // step,),
+            in_specs=[block(n, index) for n, (_, index) in enumerate(sources)],
+            out_specs=pl.BlockSpec((step, width), lambda i, at: (i, 0)),
+            scratch_shapes=[pltpu.VMEM((parts, step, columns), BF)],
+        ),
+        compiler_params=pltpu.CompilerParams(vmem_limit_bytes=40 * 1024 * 1024),
+        name="assemble_line",
+    )(origins, *[array for array, _ in sources])
 
 
 def stream_places(order_row, length_row):
@@ -950,15 +1013,9 @@
     grad_part, terms, attn_first = stage(grad_part, terms, attn_first)
 
     attn_second = scatter_second(halves(attn_part), attn_first)
-    part_own, part_other = split_cores(grad_part)
-    part_other = flip(part_other, "ctx", 0)
-    other_terms = others_of(terms, "ctx", 1, 2)
     attn_sum = jnp.concatenate(scatter_last(halves(attn_part), attn_first, attn_second), axis=1)
-    attn_sum, part_other, terms, others = stage(attn_sum, part_other, terms, other_terms[0])
-    attn_all = gather_ctx(attn_sum[None])
-    terms = sum_of(terms, others, other_terms[1])
-
-    part_places = (part_own.astype(F32) + part_other.astype(F32)).astype(BF)
+    attn_sum, grad_part, terms = stage(attn_sum, grad_part, terms)
+
     pair_plan = [
         [
             (c, side * units + p * unit_width, unit_width)
@@ -976,16 +1033,15 @@
         ]
     ]
     places = parts // 2
-    grad_step = line_step(part_places, 1, None)
+    attn_got = gather_step(1, [attn_sum, attn_sum])
+    attn_held, attn_other = [attn_sum[None]], []
     other_terms = others_of(terms, "fsdp", 1, shard_count)
+    part_own, part_other = split_cores(grad_part)
+    part_other = flip(part_other, "ctx", 0)
+    part_places = (part_own.astype(F32) + part_other.astype(F32)).astype(BF)
+    part_ends = [line_block(part_places, 1).astype(BF), line_block(part_places, places - 1).astype(BF)]
     float_in = hidden_in[0].astype(F32)
     output = (float_in + out_rows.astype(F32)).astype(BF)[None]
-    terms, others, part_places, grad_step, output = stage(terms, other_terms[0], part_places, grad_step, output)
-    terms = sum_of(terms, others, other_terms[1])
-
-    if places > 2:
-        grad_step = line_step(part_places, 2, grad_step)
-    other_terms = others_of(terms, "ctx", 2, places)
     (rest_all,) = tie([rest_all], [output])
     rest_blocks = rest_all.reshape(parts, -1, model)
     grad_down_w = rest_blocks[:, :unit_width].reshape(-1, model).astype(F32)
@@ -995,16 +1051,44 @@
         grad_proj_w = lax.dynamic_slice_in_dim(
             gather_ctx(lax.psum(proj_part.astype(F32), "fsdp")), fsdp_at * shard_rows, shard_rows, 0
         )
-    terms, others, grad_step, grad_down_w, grad_proj_w = stage(
-        terms, other_terms[0], grad_step, grad_down_w, grad_proj_w
+    terms, others, part_places, part_ends, attn_got, output, grad_down_w, grad_proj_w = stage(
+        terms, other_terms[0], part_places, part_ends, attn_got, output, grad_down_w, grad_proj_w
     )
-    (pair_all,) = tie([pair_all], [grad_down_w])
-    terms = sum_of(terms, others, other_terms[1]).reshape(-1)
-
-    for step in range(3, places):
-        grad_step = line_step(part_places, step, grad_step)
-    grad_gate_w, grad_up_w = assemble(pair_all, pair_plan)
-    part_places, grad_step, grad_gate_w, grad_up_w = stage(part_places, grad_step, grad_gate_w, grad_up_w)
+    terms = sum_of(terms, others, other_terms[1])
+
+    waiting = jnp.stack([attn_sum, *attn_got])
+    grad_step = None
+    for step in range(2, places):
+        attn_held += [block[None] for block in attn_got]
+        attn_got = gather_step(step, attn_got)
+        grad_step = line_step(part_places, step - 1, grad_step) if grad_step else line_start(part_ends)
+        attn_other.append(flip(waiting, "ctx", 0))
+        late = []
+        if step == 3:
+            (pair_all,) = tie([pair_all], [grad_down_w])
+            late = list(assemble(pair_all, pair_plan))
+        grad_step, attn_got, attn_other, late, part_places = stage(
+            grad_step, attn_got, attn_other, late, part_places
+        )
+        if step == 3:
+            grad_gate_w, grad_up_w = late
+        waiting = jnp.stack(attn_got)
+    attn_held += [block[None] for block in attn_got]
+    grad_step = line_step(part_places, places - 1, grad_step) if grad_step else line_start(part_ends)
+    attn_other.append(flip(waiting, "ctx", 0))
+    sources = [(attn_held[0], 0), (attn_other[0], 0)]
+    for step in range(1, places):
+        sources += [(attn_held[2 * step - 1], 0), (attn_held[2 * step], 0)]
+        first = 1 if step == 1 else 0
+        sources += [(attn_other[step - 1], first), (attn_other[step - 1], first + 1)]
+    grad_attn_w = assemble_line(sources, line_origins(), attn_plan[0])
+    terms = terms + flip(terms, "ctx", 0)
+    other_terms = flip(terms, "ctx", 1)
+    grad_attn_w, other_terms, grad_step, part_places = stage(grad_attn_w, other_terms, grad_step, part_places)
+    terms = terms + other_terms
+    for bit in range(2, bits_of(parts)):
+        terms = terms + flip(terms, "ctx", bit)
+    terms = terms.reshape(-1)
     grad_normed = line_block(part_places, 0) + grad_step[0].astype(F32) + grad_step[1].astype(F32)
 
     normal_hat, inverse_std = normalise(float_in)
@@ -1020,8 +1104,6 @@
         - normal_hat * jnp.mean(grad_hat * normal_hat, axis=1, keepdims=True)
     )
     grad_in = grad_in.astype(BF)[None]
-    (attn_all,) = tie([attn_all], [grad_in])
-    (grad_attn_w,) = assemble(attn_all, attn_plan)
     return (
         output,
         grad_in,

time: 619 us -> 608 us (0.982)
  waiting for transfers between devices: 165 us -> 109 us
  starting transfers between devices: 55.7 us -> 71.9 us
  other arithmetic: 65.4 us -> 80.2 us
  matrix products: 45.4 us -> 56.8 us
    ppermute x6 -> x12, waiting for transfers between devices: 122 us -> 48.9 us  [shift(): return lax.ppermute(values, 'ctx', pairs)]
    ppermute x6 -> x12, starting transfers between devices: 12.5 us -> 30.9 us  [shift(): return lax.ppermute(values, 'ctx', pairs)]
    ppermute x29 -> x35, waiting for transfers between devices: 40.8 us -> 58.8 us  [flip(): return lax.ppermute(values, axis, [(i, i ^ 1 << bit) for i in range(count)])]
    dot_general x5, matrix products: 45.4 us -> 56.8 us  [matmul_tn(): lax.dot_general(left, right, (((0,), (0,)), ((), ())), preferred_element_...]
    pallas_call x0 -> x1, Pallas kernels: none -> 10.8 us  [assemble_line(): pl.pallas_call(functools.partial(assemble_line_kernel, plan, len(sources)...]
    another operation x1 -> x4, other arithmetic: 0.18 us -> 8.59 us  [the longest x2 5.38 us: shards(): waiting = jnp.stack(attn_got)]
    pallas_call x2 -> x1, Pallas kernels: 15.8 us -> 8.95 us  [assemble(): pl.pallas_call(functools.partial(assemble_kernel, plan), grid=(rows // st...]
    ppermute x29 -> x35, starting transfers between devices: 32.4 us -> 36.4 us  [flip(): return lax.ppermute(values, axis, [(i, i ^ 1 << bit) for i in range(count)])]
  transfers between devices with their start and end apart: 48 -> 55, of which waited for: 13 -> 18; matrix products, arithmetic and copies ran while one was open for 28% -> 31% of each run, Pallas kernels for 29% -> 31%
where the time goes in v4:
time: 608 us; the launch traced here: 597 us
  Pallas kernels  186 us (31%)
  waiting for transfers between devices  109 us (18%)
  other arithmetic  80.2 us (13%)
  local copies, waits for them, and re-layouts  77.9 us (13%)
  starting transfers between devices  71.9 us (12%)
  matrix products  56.8 us (9%)
  between operations  15.4 us (3%)
    ppermute x35, waiting for transfers between devices, flip(): return lax.ppermute(values, axis, [(i, i ^ 1 << bit) for i in range(count)])  58.8 us
    dot_general x5, matrix products, matmul_tn(): lax.dot_general(left, right, (((0,), (0,)), ((), ())), preferred_element_...  56.8 us
    ppermute x12, waiting for transfers between devices, shift(): return lax.ppermute(values, 'ctx', pairs)  48.9 us
    pallas_call x1, Pallas kernels, attention_backward(): pl.pallas_call(functools.partial(backward_kernel, heads), out_shape=jax.S...  41.9 us
    ppermute x35, starting transfers between devices, flip(): return lax.ppermute(values, axis, [(i, i ^ 1 << bit) for i in range(count)])  36.4 us
    pallas_call x1, Pallas kernels, input_side(): pl.pallas_call(functools.partial(input_kernel, spans), grid=(tokens // CH...  31.6 us
    ppermute x12, starting transfers between devices, shift(): return lax.ppermute(values, 'ctx', pairs)  30.9 us
    unnamed x96, local copies, waits for them, and re-layouts  24.5 us
  transfers between devices with their start and end apart: 55, of which 18 were waited for; matrix products, arithmetic and copies ran while one was open for 31% of the time, Pallas kernels for 31%

profile of v4, /device:TPU:0, one launch (start us, length us, event | category | flops | bytes accessed | tf_op | source)
XLA Modules:
  0.0 596.9 jit_solution(4142025744652556115)
XLA Ops:
  10.1 2.9 constant_dynamic-slice_fusion.10
  13.0 2.8 concatenate.40
  17.5 3.0 collective-permute-start.1
  22.0 4.2 constant_dynamic-slice_fusion.2
  34.8 5.6 fusion.26
  50.7 5.9 collective-permute-done.3.refs_1_
  58.7 6.3 %collective-permute-done.4.refs_2_ = bf16[256,768]{1,0:T(8,128)(2,1)} collective-permute-done((bf16[256,768]{1,0:T(8,128)(2,1)S(1)}, bf16[256,768]{1,0:T(8,128)(2,1)}, u32[]{:S(2)}, u32[]{:S(2)}) %collective-permute-start.4) | collective-permute-done | bytes 393248 | tf_op jit(solution)/shard_map/ppermute | solution.py:33
  77.3 4.5 collective-permute-done.7.refs_1_
  84.4 7.0 %collective-permute-done.9.refs_3_ = bf16[256,768]{1,0:T(8,128)(2,1)S(1)} collective-permute-done((bf16[256,768]{1,0:T(8,128)(2,1)}, bf16[256,768]{1,0:T(8,128)(2,1)S(1)}, u32[]{:S(2)}, u32[]{:S(2)}) %collective-permute-start.9) | collective-permute-done | bytes 393248 | tf_op jit(solution)/shard_map/ppermute | solution.py:33
  99.7 17.2 %attn_side.1 = (bf16[2048,2048]{1,0:T(8,128)(2,1)}, f32[2048,768]{1,0:T(8,128)}) custom-call(s32[5]{0:T(128)} %stack.210.at_ref, bf16[2048,2048]{1,0:T(8,128)(2,1)} %bitcast.261, f32[1,2048]{1,0:T(1,128)} %bitcast.260, f32[1,2048]{1,0:T(1,128)} %bitcast.259, f32[1,768]{1,0:T(1,128)} %broadcast_in_dim.141.shift_ref, ...), custom_call_target="tpu_custom_call" | custom-call | flops 17999998976 | tf_op jit(solution)/shard_map/attn_side/pallas_call | solution.py:582
  116.9 22.6 %attention_forward.1 = (bf16[2048,256]{1,0:T(8,128)(2,1)S(1)}, bf16[2048,256]{1,0:T(8,128)(2,1)S(1)}, bf16[2048,256]{1,0:T(8,128)(2,1)S(1)}, bf16[2048,256]{1,0:...) custom-call(s32[16]{0:T(128)S(1)} %select_reduce_fusion.slot_ref, s32[8]{0:T(128)S(1)} %and_select_fusion.1.low_ref, ...), custom_call_target="tpu_custom_call" | custom-call | flops 24999999488 | tf_op jit(solution)/shard_map/attention_forward/pallas_call | solution.py:471
  145.8 20.7 %pair_side.1 = (bf16[2048,768]{1,0:T(8,128)(2,1)}, bf16[2048,768]{1,0:T(8,128)(2,1)}, bf16[2048,768]{1,0:T(8,128)(2,1)}) custom-call(s32[5]{0:T(128)} %stack.210.at_ref, bf16[2048,2048]{1,0:T(8,128)(2,1)} %get-tuple-element.105.normed_ref, bf16[512,768]{1,0:T(8,128)(2,1)} %concatenate.43.refs_0_, bf16[512,768]{1,0:T(8,128)(2,1)} %get-tuple-element.112.refs_1_, ...), custom_call_target="tpu_custom_call" | custom-call | flops 28000000000 | tf_op jit(solution)/shard_map/pair_side/pallas_call | solution.py:601
  167.5 15.0 %out_side.1.refs_1_ = bf16[2048,2048]{1,0:T(8,128)(2,1)} custom-call(s32[2,4]{1,0:T(2,128)} %pad_add_fusion.at_ref, bf16[2048,256]{1,0:T(8,128)(2,1)} %get-tuple-element.124.mixed_ref, bf16[2048,768]{1,0:T(8,128)(2,1)} %get-tuple-element.123.act_ref, bf16[240,2048]{1,0:T(8,128)(2,1)} %get-tuple-element.120.refs_0_.refs_4_, ...), custom_call_target="tpu_custom_call" | custom-call | flops 15000000512 | tf_op jit(solution)/shard_map/out_side/pallas_call | solution.py:697
  182.9 10.3 %fusion.57 = bf16[768,2048]{1,0:T(8,128)(2,1)S(1)} fusion(bf16[2048,768]{1,0:T(8,128)(2,1)} %get-tuple-element.123.act_ref, bf16[2048,2048]{1,0:T(8,128)(2,1)} %tie.22.refs_1_), kind=kOutput, calls=%fused_computation.187 | convolution fusion | flops 6442450944 | bytes 14680064 | tf_op jit(solution)/shard_map/dot_general | solution.py:28
  205.6 17.0 %grad_side.1 = (bf16[2048,768]{1,0:T(8,128)(2,1)}, bf16[2048,768]{1,0:T(8,128)(2,1)}, bf16[2048,256]{1,0:T(8,128)(2,1)}) custom-call(s32[2,4]{1,0:T(2,128)} %pad_add_fusion.at_ref, bf16[2048,2048]{1,0:T(8,128)(2,1)} %get-tuple-element.127.grad_ref, bf16[2048,768]{1,0:T(8,128)(2,1)} %get-tuple-element.128.slope_ref, ...), custom_call_target="tpu_custom_call" | custom-call | flops 17999998976 | tf_op jit(solution)/shard_map/grad_side/pallas_call | solution.py:665
  229.8 11.6 %convolution_convert_fusion.2.refs_0_ = bf16[2048,768]{1,0:T(8,128)(2,1)} fusion(bf16[2048,2048]{1,0:T(8,128)(2,1)} %get-tuple-element.105.normed_ref, bf16[2048,768]{1,0:T(8,128)(2,1)} %get-tuple-element.134.gate_ref), kind=kOutput, calls=%fused_computation.9 | convolution fusion | flops 6444023808 | bytes 14680064 | tf_op jit(solution)/shard_map/dot_general | solution.py:28
  241.3 20.9 %convolution_convert_fusion.1.refs_1_ = bf16[2048,768]{1,0:T(8,128)(2,1)} fusion(bf16[2048,2048]{1,0:T(8,128)(2,1)} %get-tuple-element.105.normed_ref, bf16[2048,768]{1,0:T(8,128)(2,1)S(1)} %copy-done.23), kind=kOutput, calls=%fused_computation.8 | convolution fusion | flops 6444023808 | bytes 14680064 | tf_op jit(solution)/shard_map/dot_general | solution.py:28
  271.5 41.9 %attention_backward.1.refs_0_ = bf16[2048,768]{1,0:T(8,128)(2,1)} custom-call(s32[16]{0:T(128)S(1)} %select_reduce_fusion.slot_ref, s32[8]{0:T(128)S(1)} %and_select_fusion.1.low_ref, bf16[2048,256]{1,0:T(8,128)(2,1)S(1)} %get-tuple-element.107.q_ref, bf16[2048,256]{1,0:T(8,128)(2,1)S(1)} %get-tuple-element.108.k_ref, bf16[2048,256]{1,0:T(8,128)(2,1)S(1)} %copy-done.12, ...), custom_call_target="tpu_custom_call" | custom-call | flops 40000000000 | tf_op jit(solution)/shard_map/attention_backward/pallas_call | solution.py:496
  317.0 11.6 %convolution_convert_fusion.refs_0_ = bf16[2048,768]{1,0:T(8,128)(2,1)} fusion(bf16[2048,2048]{1,0:T(8,128)(2,1)} %get-tuple-element.105.normed_ref, bf16[2048,768]{1,0:T(8,128)(2,1)} %get-tuple-element.142.refs_2_), kind=kOutput, calls=%fused_computation.7 | convolution fusion | flops 6444023808 | bytes 14680064 | tf_op jit(solution)/shard_map/dot_general | solution.py:28
  334.2 10.7 %collective-permute-done.22 = bf16[512,768]{1,0:T(8,128)(2,1)S(1)} collective-permute-done((bf16[512,768]{1,0:T(8,128)(2,1)S(1)}, bf16[512,768]{1,0:T(8,128)(2,1)S(1)}, u32[]{:S(2)}, u32[]{:S(2)}) %collective-permute-start.22) | collective-permute-done | bytes 786464 | tf_op jit(solution)/shard_map/ppermute | solution.py:33
  353.8 31.6 %input_side.1 = (bf16[2048,2048]{1,0:T(8,128)(2,1)}, f32[2,2048]{1,0:T(2,128)}) custom-call(s32[5]{0:T(128)} %stack.210.at_ref, bf16[2048,768]{1,0:T(8,128)(2,1)} %get-tuple-element.134.gate_ref, bf16[2048,768]{1,0:T(8,128)(2,1)} %get-tuple-element.135.up_ref, bf16[2048,768]{1,0:T(8,128)(2,1)} %get-tuple-element.146.merged_ref, ...), custom_call_target="tpu_custom_call" | custom-call | flops 30000001024 | tf_op jit(solution)/shard_map/input_side/pallas_call | solution.py:738
  391.8 5.7 collective-permute-done.27
  401.3 4.9 dynamic-slice_bitcast_fusion
  413.7 5.0 collective-permute-start.32
  418.8 7.8 %fusion.refs_4_ = bf16[4,256,2048]{2,1,0:T(8,128)(2,1)} fusion(bf16[4,256,2048]{2,1,0:T(8,128)(2,1)} %collective-permute-done.31, bf16[4,2,256,2048]{3,2,1,0:T(8,128)(2,1)} %bitcast.246, s32[]{:T(128)S(6)} %select_n.394), kind=kLoop, calls=%fused_computation.1 | loop fusion | flops 8388608 | bytes 12582916 | tf_op jit(solution)/shard_map/convert_element_type | solution.py:1041
  426.5 3.1 dynamic-slice_bitcast_fusion.1
  429.7 2.7 fusion.12
  432.3 3.2 slice.176
  435.5 6.4 %bitcast_convert_fusion.refs_10_ = f32[1408,2048]{1,0:T(8,128)} fusion(bf16[8,176,2048]{2,1,0:T(8,128)(2,1)S(1)} %slice.176), kind=kLoop, calls=%fused_computation.4 | loop fusion | flops 2883584 | bytes 17301504 | tf_op jit(solution)/shard_map/convert_element_type | solution.py:1047
  443.6 2.7 bitcast_convert_fusion.1.refs_11_
  446.4 21.2 %collective-permute-done.33.refs_8_ = bf16[512,768]{1,0:T(8,128)(2,1)} collective-permute-done((bf16[512,768]{1,0:T(8,128)(2,1)S(1)}, bf16[512,768]{1,0:T(8,128)(2,1)}, u32[]{:S(2)}, u32[]{:S(2)}) %collective-permute-start.33) | collective-permute-done | bytes 786464 | tf_op jit(solution)/shard_map/ppermute | solution.py:202
  467.5 3.0 pad_maximum_fusion.1
  470.7 5.7 collective-permute-start.34
  481.0 20.5 %collective-permute-done.37.refs_3_ = bf16[512,768]{1,0:T(8,128)(2,1)} collective-permute-done((bf16[512,768]{1,0:T(8,128)(2,1)}, bf16[512,768]{1,0:T(8,128)(2,1)}, u32[]{:S(2)}, u32[]{:S(2)}) %collective-permute-start.37) | collective-permute-done | bytes 786464 | tf_op jit(solution)/shard_map/ppermute | solution.py:202
  502.9 2.7 pad_maximum_fusion.4
  505.6 4.0 fusion.15
  511.2 2.9 collective-permute-start.39
  517.2 4.3 copy-done.4
  521.5 9.0 %assemble.1 = (f32[512,5632]{1,0:T(8,128)}, f32[512,5632]{1,0:T(8,128)}) custom-call(bf16[8,512,1408]{2,1,0:T(8,128)(2,1)S(1)} %copy-done.4), custom_call_target="tpu_custom_call" | custom-call | tf_op jit(solution)/shard_map/assemble/pallas_call | solution.py:771
  530.4 7.1 %collective-permute-done.42.refs_3_ = bf16[512,768]{1,0:T(8,128)(2,1)} collective-permute-done((bf16[512,768]{1,0:T(8,128)(2,1)}, bf16[512,768]{1,0:T(8,128)(2,1)}, u32[]{:S(2)}, u32[]{:S(2)}) %collective-permute-start.42) | collective-permute-done | bytes 786464 | tf_op jit(solution)/shard_map/ppermute | solution.py:202
  538.8 2.7 pad_maximum_fusion.5
  541.5 4.7 fusion.18
  547.4 5.7 collective-permute-start.47
  556.9 10.8 %assemble_line.1.refs_0_ = f32[512,6144]{1,0:T(8,128)} custom-call(s32[14]{0:T(128)S(1)} %stack.256.at_ref, bf16[1,512,768]{2,1,0:T(8,128)(2,1)S(1)} %bitcast.241, bf16[3,512,768]{2,1,0:T(8,128)(2,1)S(1)} %copy-done.3, bf16[1,512,768]{2,1,0:T(8,128)(2,1)} %bitcast.78.refs_2_, bf16[1,512,768]{2,1,0:T(8,128)(2,1)} %bitcast.79.refs_3_, ...), custom_call_target="tpu_custom_call" | custom-call | tf_op jit(solution)/shard_map/assemble_line/pallas_call | solution.py:805
  567.7 8.2 %collective-permute-done.46.refs_1_ = f32[80,128]{1,0:T(8,128)S(1)} collective-permute-done((f32[80,128]{1,0:T(8,128)S(1)}, f32[80,128]{1,0:T(8,128)S(1)}, u32[]{:S(2)}, u32[]{:S(2)}) %collective-permute-start.46) | collective-permute-done | bytes 40992 | tf_op jit(solution)/shard_map/ppermute | solution.py:33
  577.3 2.8 fusion.46
  580.2 4.4 collective-permute-start.49
  584.5 4.1 fusion.30
  (312 shorter events, 143.2 us)
Async XLA Ops:
  7.2 92.5 %all-gather.10.cloned.1.call-start = ((), (), s32[]{:S(2)}) async-start(), calls=%async_computation.3 | async-start | bytes 9437184 | tf_op jit(solution)/shard_map/all_gather | solution.py:183
  7.9 175.0 %all-gather.12.cloned.1.call-start = ((), (), s32[]{:S(2)}) async-start(), calls=%async_computation.4 | async-start | bytes 9437184 | tf_op jit(solution)/shard_map/all_gather | solution.py:183
  8.7 421.0 %reduce-scatter.2.cloned.1.call-start = ((), (), s32[]{:S(2)}) async-start(), calls=%async_computation.1 | async-start | bytes 9437184 | tf_op jit(solution)/shard_map/reduce_scatter | solution.py:194
  17.5 24.5 %collective-permute-start.1 = (bf16[528,768]{1,0:T(8,128)(2,1)}, bf16[528,768]{1,0:T(8,128)(2,1)S(1)}, u32[]{:S(2)}, u32[]{:S(2)}) collective-permute-start(bf16[528,768]{1,0:T(8,128)(2,1)} %pad_maximum_fusion.11.refs_0_.refs_10_), channel_id=1, source_target_pairs={{0,2},{1,3},{2,0},{3,1},{4,6},{5,7},{6,4},{7,5},{8,10},{9,11},{10,... | collective-permute-start | bytes 2433032 | tf_op jit(solution)/shard_map/ppermute | solution.py:33
  20.5 21.6 %collective-permute-start = (bf16[528,768]{1,0:T(8,128)(2,1)}, bf16[528,768]{1,0:T(8,128)(2,1)}, u32[]{:S(2)}, u32[]{:S(2)}) collective-permute-start(bf16[528,768]{1,0:T(8,128)(2,1)} %pad_maximum_fusion.11.refs_0_.refs_10_), channel_id=1, source_target_pairs={{0,1},{1,0},{2,3},{3,2},{4,5},{5,4},{6,7},{7,6},{8,9},{9,8},{10,11... | collective-permute-start | bytes 2433032 | tf_op jit(solution)/shard_map/ppermute | solution.py:33
  28.6 27.9 %collective-permute-start.3 = (bf16[512,768]{1,0:T(8,128)(2,1)}, bf16[512,768]{1,0:T(8,128)(2,1)}, u32[]{:S(2)}, u32[]{:S(2)}) collective-permute-start(bf16[512,768]{1,0:T(8,128)(2,1)} %concatenate.43.refs_0_), channel_id=1, source_target_pairs={{0,2},{1,3},{2,0},{3,1},{4,6},{5,7},{6,4},{7,5},{8,10},{9,11},{10,... | collective-permute-start | bytes 2359304 | tf_op jit(solution)/shard_map/ppermute | solution.py:33
  29.7 29.0 %collective-permute-start.2 = (bf16[512,768]{1,0:T(8,128)(2,1)}, bf16[512,768]{1,0:T(8,128)(2,1)}, u32[]{:S(2)}, u32[]{:S(2)}) collective-permute-start(bf16[512,768]{1,0:T(8,128)(2,1)} %concatenate.43.refs_0_), channel_id=1, source_target_pairs={{0,1},{1,0},{2,3},{3,2},{4,5},{5,4},{6,7},{7,6},{8,9},{9,8},{10,11... | collective-permute-start | bytes 2359304 | tf_op jit(solution)/shard_map/ppermute | solution.py:33
  44.0 21.0 %collective-permute-start.4 = (bf16[256,768]{1,0:T(8,128)(2,1)S(1)}, bf16[256,768]{1,0:T(8,128)(2,1)}, u32[]{:S(2)}, u32[]{:S(2)}) collective-permute-start(bf16[256,768]{1,0:T(8,128)(2,1)S(1)} %slice.130), channel_id=1, source_target_pairs={{0,2},{1,3},{2,0},{3,1},{4,6},{5,7},{6,4},{7,5},{8,10},{9,11},{10,... | collective-permute-start | bytes 1179656 | tf_op jit(solution)/shard_map/ppermute | solution.py:33
  47.1 20.4 %collective-permute-start.5 = (bf16[272,768]{1,0:T(8,128)(2,1)S(1)}, bf16[272,768]{1,0:T(8,128)(2,1)S(1)}, u32[]{:S(2)}, u32[]{:S(2)}) collective-permute-start(bf16[272,768]{1,0:T(8,128)(2,1)S(1)} %slice.131), channel_id=1, source_target_pairs={{0,1},{1,0},{2,3},{3,2},{4,5},{5,4},{6,7},{7,6},{8,9},{9,8},{10,11... | collective-permute-start | bytes 1253384 | tf_op jit(solution)/shard_map/ppermute | solution.py:33
  48.1 33.6 %collective-permute-start.7 = (bf16[512,768]{1,0:T(8,128)(2,1)}, bf16[512,768]{1,0:T(8,128)(2,1)S(1)}, u32[]{:S(2)}, u32[]{:S(2)}) collective-permute-start(bf16[512,768]{1,0:T(8,128)(2,1)} %get-tuple-element.114.refs_5_), channel_id=1, source_target_pairs={{0,2},{1,3},{2,0},{3,1},{4,6},{5,7},{6,4},{7,5},{8,10},{9,11},{10,... | collective-permute-start | bytes 2359304 | tf_op jit(solution)/shard_map/ppermute | solution.py:33
  56.6 27.8 %collective-permute-start.6 = (bf16[512,768]{1,0:T(8,128)(2,1)}, bf16[512,768]{1,0:T(8,128)(2,1)S(1)}, u32[]{:S(2)}, u32[]{:S(2)}) collective-permute-start(bf16[512,768]{1,0:T(8,128)(2,1)} %get-tuple-element.114.refs_5_), channel_id=1, source_target_pairs={{0,1},{1,0},{2,3},{3,2},{4,5},{5,4},{6,7},{7,6},{8,9},{9,8},{10,11... | collective-permute-start | bytes 2359304 | tf_op jit(solution)/shard_map/ppermute | solution.py:33
  72.6 18.7 %collective-permute-start.9 = (bf16[256,768]{1,0:T(8,128)(2,1)}, bf16[256,768]{1,0:T(8,128)(2,1)S(1)}, u32[]{:S(2)}, u32[]{:S(2)}) collective-permute-start(bf16[256,768]{1,0:T(8,128)(2,1)} %slice.138), channel_id=1, source_target_pairs={{0,1},{1,0},{2,3},{3,2},{4,5},{5,4},{6,7},{7,6},{8,9},{9,8},{10,11... | collective-permute-start | bytes 1179656 | tf_op jit(solution)/shard_map/ppermute | solution.py:33
  74.1 17.2 %collective-permute-start.8 = (bf16[256,768]{1,0:T(8,128)(2,1)}, bf16[256,768]{1,0:T(8,128)(2,1)}, u32[]{:S(2)}, u32[]{:S(2)}) collective-permute-start(bf16[256,768]{1,0:T(8,128)(2,1)} %slice.137), channel_id=1, source_target_pairs={{0,2},{1,3},{2,0},{3,1},{4,6},{5,7},{6,4},{7,5},{8,10},{9,11},{10,... | collective-permute-start | bytes 1179656 | tf_op jit(solution)/shard_map/ppermute | solution.py:33
  92.1 49.4 %collective-permute-start.13 = (bf16[240,2048]{1,0:T(8,128)(2,1)}, bf16[240,2048]{1,0:T(8,128)(2,1)}, u32[]{:S(2)}, u32[]{:S(2)}) collective-permute-start(bf16[240,2048]{1,0:T(8,128)(2,1)} %get-tuple-element.120.refs_0_.refs_4_), channel_id=1, source_target_pairs={{0,2},{1,3},{2,0},{3,1},{4,6},{5,7},{6,4},{7,5},{8,10},{9,11},{10,... | collective-permute-start | bytes 2949128 | tf_op jit(solution)/shard_map/ppermute | solution.py:33
  92.4 49.2 %collective-permute-start.12 = (bf16[240,2048]{1,0:T(8,128)(2,1)}, bf16[240,2048]{1,0:T(8,128)(2,1)}, u32[]{:S(2)}, u32[]{:S(2)}) collective-permute-start(bf16[240,2048]{1,0:T(8,128)(2,1)} %get-tuple-element.120.refs_0_.refs_4_), channel_id=1, source_target_pairs={{0,1},{1,0},{2,3},{3,2},{4,5},{5,4},{6,7},{7,6},{8,9},{9,8},{10,11... | collective-permute-start | bytes 2949128 | tf_op jit(solution)/shard_map/ppermute | solution.py:33
  97.6 43.9 %collective-permute-start.11 = (bf16[256,768]{1,0:T(8,128)(2,1)}, bf16[256,768]{1,0:T(8,128)(2,1)}, u32[]{:S(2)}, u32[]{:S(2)}) collective-permute-start(bf16[256,768]{1,0:T(8,128)(2,1)} %slice.140), channel_id=1, source_target_pairs={{0,1},{1,0},{2,3},{3,2},{4,5},{5,4},{6,7},{7,6},{8,9},{9,8},{10,11... | collective-permute-start | bytes 1179656 | tf_op jit(solution)/shard_map/ppermute | solution.py:33
  97.9 43.6 %collective-permute-start.10 = (bf16[256,768]{1,0:T(8,128)(2,1)}, bf16[256,768]{1,0:T(8,128)(2,1)}, u32[]{:S(2)}, u32[]{:S(2)}) collective-permute-start(bf16[256,768]{1,0:T(8,128)(2,1)} %slice.139), channel_id=1, source_target_pairs={{0,2},{1,3},{2,0},{3,1},{4,6},{5,7},{6,4},{7,5},{8,10},{9,11},{10,... | collective-permute-start | bytes 1179656 | tf_op jit(solution)/shard_map/ppermute | solution.py:33
  142.6 23.9 %collective-permute-start.14 = (bf16[112,2048]{1,0:T(8,128)(2,1)S(1)}, bf16[112,2048]{1,0:T(8,128)(2,1)S(1)}, u32[]{:S(2)}, u32[]{:S(2)}) collective-permute-start(bf16[112,2048]{1,0:T(8,128)(2,1)S(1)} %slice.141), channel_id=1, source_target_pairs={{0,2},{1,3},{2,0},{3,1},{4,6},{5,7},{6,4},{7,5},{8,10},{9,11},{10,... | collective-permute-start | bytes 1376264 | tf_op jit(solution)/shard_map/ppermute | solution.py:33
  143.9 22.7 %collective-permute-start.15 = (bf16[128,2048]{1,0:T(8,128)(2,1)S(1)}, bf16[128,2048]{1,0:T(8,128)(2,1)S(1)}, u32[]{:S(2)}, u32[]{:S(2)}) collective-permute-start(bf16[128,2048]{1,0:T(8,128)(2,1)S(1)} %slice.142), channel_id=1, source_target_pairs={{0,1},{1,0},{2,3},{3,2},{4,5},{5,4},{6,7},{7,6},{8,9},{9,8},{10,11... | collective-permute-start | bytes 1572872 | tf_op jit(solution)/shard_map/ppermute | solution.py:33
  182.6 249.8 %all-gather.8.cloned.1.call-start = ((), (), s32[]{:S(2)}) async-start(), calls=%async_computation.2 | async-start | bytes 8847360 | tf_op jit(solution)/shard_map/all_gather | solution.py:183
  202.1 20.6 %collective-permute-start.16 = (bf16[2,240,1024]{2,1,0:T(8,128)(2,1)S(1)}, bf16[2,240,1024]{2,1,0:T(8,128)(2,1)}, u32[]{:S(2)}, u32[]{:S(2)}) collective-permute-start(bf16[2,240,1024]{2,1,0:T(8,128)(2,1)S(1)} %pad_maximum_fusion.8), channel_id=1, source_target_pairs={{0,1},{1,0},{2,3},{3,2},{4,5},{5,4},{6,7},{7,6},{8,9},{9,8},{10,11... | collective-permute-start | bytes 2949128 | tf_op jit(solution)/shard_map/ppermute | solution.py:33
  204.0 20.6 %collective-permute-start.17 = (bf16[2,240,1024]{2,1,0:T(8,128)(2,1)S(1)}, bf16[2,240,1024]{2,1,0:T(8,128)(2,1)}, u32[]{:S(2)}, u32[]{:S(2)}) collective-permute-start(bf16[2,240,1024]{2,1,0:T(8,128)(2,1)S(1)} %pad_maximum_fusion.9), channel_id=1, source_target_pairs={{0,2},{1,3},{2,0},{3,1},{4,6},{5,7},{6,4},{7,5},{8,10},{9,11},{10,... | collective-permute-start | bytes 2949128 | tf_op jit(solution)/shard_map/ppermute | solution.py:33
  226.0 36.3 %collective-permute-start.19 = (bf16[240,1024]{1,0:T(8,128)(2,1)S(1)}, bf16[240,1024]{1,0:T(8,128)(2,1)S(1)}, u32[]{:S(2)}, u32[]{:S(2)}) collective-permute-start(bf16[240,1024]{1,0:T(8,128)(2,1)S(1)} %fusion.31), channel_id=1, source_target_pairs={{0,2},{1,3},{2,0},{3,1},{4,6},{5,7},{6,4},{7,5},{8,10},{9,11},{10,... | collective-permute-start | bytes 1474568 | tf_op jit(solution)/shard_map/ppermute | solution.py:33
  229.1 34.7 %collective-permute-start.18 = (bf16[240,1024]{1,0:T(8,128)(2,1)S(1)}, bf16[240,1024]{1,0:T(8,128)(2,1)S(1)}, u32[]{:S(2)}, u32[]{:S(2)}) collective-permute-start(bf16[240,1024]{1,0:T(8,128)(2,1)S(1)} %fusion.34), channel_id=1, source_target_pairs={{0,1},{1,0},{2,3},{3,2},{4,5},{5,4},{6,7},{7,6},{8,9},{9,8},{10,11... | collective-permute-start | bytes 1474568 | tf_op jit(solution)/shard_map/ppermute | solution.py:33
  266.3 250.9 %all-gather.14.cloned.1.call-start = ((), (), s32[]{:S(2)}) async-start(), calls=%async_computation.5 | async-start | bytes 12976128 | tf_op jit(solution)/shard_map/all_gather | solution.py:183
  268.1 45.3 %collective-permute-start.21 = (bf16[2,512,768]{2,1,0:T(8,128)(2,1)S(1)}, bf16[2,512,768]{2,1,0:T(8,128)(2,1)}, u32[]{:S(2)}, u32[]{:S(2)}) collective-permute-start(bf16[2,512,768]{2,1,0:T(8,128)(2,1)S(1)} %pad_maximum_fusion.3), channel_id=1, source_target_pairs={{0,2},{1,3},{2,0},{3,1},{4,6},{5,7},{6,4},{7,5},{8,10},{9,11},{10,... | collective-permute-start | bytes 4718600 | tf_op jit(solution)/shard_map/ppermute | solution.py:33
  270.1 43.3 %collective-permute-start.20 = (bf16[2,512,768]{2,1,0:T(8,128)(2,1)S(1)}, bf16[2,512,768]{2,1,0:T(8,128)(2,1)}, u32[]{:S(2)}, u32[]{:S(2)}) collective-permute-start(bf16[2,512,768]{2,1,0:T(8,128)(2,1)S(1)} %pad_maximum_fusion.2), channel_id=1, source_target_pairs={{0,1},{1,0},{2,3},{3,2},{4,5},{5,4},{6,7},{7,6},{8,9},{9,8},{10,11... | collective-permute-start | bytes 4718600 | tf_op jit(solution)/shard_map/ppermute | solution.py:33
  316.7 17.2 %collective-permute-start.23 = (bf16[512,768]{1,0:T(8,128)(2,1)S(1)}, bf16[512,768]{1,0:T(8,128)(2,1)S(1)}, u32[]{:S(2)}, u32[]{:S(2)}) collective-permute-start(bf16[512,768]{1,0:T(8,128)(2,1)S(1)} %fusion.20), channel_id=1, source_target_pairs={{0,2},{1,3},{2,0},{3,1},{4,6},{5,7},{6,4},{7,5},{8,10},{9,11},{10,... | collective-permute-start | bytes 2359304 | tf_op jit(solution)/shard_map/ppermute | solution.py:33
  330.0 14.8 %collective-permute-start.22 = (bf16[512,768]{1,0:T(8,128)(2,1)S(1)}, bf16[512,768]{1,0:T(8,128)(2,1)S(1)}, u32[]{:S(2)}, u32[]{:S(2)}) collective-permute-start(bf16[512,768]{1,0:T(8,128)(2,1)S(1)} %fusion.23), channel_id=1, source_target_pairs={{0,1},{1,0},{2,3},{3,2},{4,5},{5,4},{6,7},{7,6},{8,9},{9,8},{10,11... | collective-permute-start | bytes 2359304 | tf_op jit(solution)/shard_map/ppermute | solution.py:33
  350.1 37.5 %collective-permute-start.24 = (bf16[2,512,384]{2,1,0:T(8,128)(2,1)}, bf16[2,512,384]{2,1,0:T(8,128)(2,1)}, u32[]{:S(2)}, u32[]{:S(2)}) collective-permute-start(bf16[2,512,384]{2,1,0:T(8,128)(2,1)} %pad_maximum_fusion.12), channel_id=1, source_target_pairs={{0,1},{1,0},{2,3},{3,2},{4,5},{5,4},{6,7},{7,6},{8,9},{9,8},{10,11... | collective-permute-start | bytes 2359304 | tf_op jit(solution)/shard_map/ppermute | solution.py:33
  352.1 35.4 %collective-permute-start.25 = (bf16[2,512,384]{2,1,0:T(8,128)(2,1)}, bf16[2,512,384]{2,1,0:T(8,128)(2,1)}, u32[]{:S(2)}, u32[]{:S(2)}) collective-permute-start(bf16[2,512,384]{2,1,0:T(8,128)(2,1)} %pad_maximum_fusion.13), channel_id=1, source_target_pairs={{0,2},{1,3},{2,0},{3,1},{4,6},{5,7},{6,4},{7,5},{8,10},{9,11},{10,... | collective-permute-start | bytes 2359304 | tf_op jit(solution)/shard_map/ppermute | solution.py:33
  406.5 39.8 %collective-permute-start.30 = (f32[80,128]{1,0:T(8,128)S(1)}, f32[80,128]{1,0:T(8,128)S(1)}, u32[]{:S(2)}, u32[]{:S(2)}) collective-permute-start(f32[80,128]{1,0:T(8,128)S(1)} %copy-done.27), channel_id=1, source_target_pairs={{0,3},{1,0},{2,1},{3,2},{4,7},{5,4},{6,5},{7,6},{8,11},{9,8},{10,9... | collective-permute-start | bytes 122888 | tf_op jit(solution)/shard_map/ppermute | solution.py:113
  408.2 38.1 %collective-permute-start.29 = (f32[80,128]{1,0:T(8,128)S(1)}, f32[80,128]{1,0:T(8,128)S(1)}, u32[]{:S(2)}, u32[]{:S(2)}) collective-permute-start(f32[80,128]{1,0:T(8,128)S(1)} %copy-done.27), channel_id=1, source_target_pairs={{0,2},{1,3},{2,0},{3,1},{4,6},{5,7},{6,4},{7,5},{8,10},{9,11},{10,... | collective-permute-start | bytes 122888 | tf_op jit(solution)/shard_map/ppermute | solution.py:113
  408.7 37.6 %collective-permute-start.28 = (f32[80,128]{1,0:T(8,128)S(1)}, f32[80,128]{1,0:T(8,128)S(1)}, u32[]{:S(2)}, u32[]{:S(2)}) collective-permute-start(f32[80,128]{1,0:T(8,128)S(1)} %copy-done.27), channel_id=1, source_target_pairs={{0,1},{1,2},{2,3},{3,0},{4,5},{5,6},{6,7},{7,4},{8,9},{9,10},{10,1... | collective-permute-start | bytes 122888 | tf_op jit(solution)/shard_map/ppermute | solution.py:113
  410.7 56.8 %collective-permute-start.33 = (bf16[512,768]{1,0:T(8,128)(2,1)S(1)}, bf16[512,768]{1,0:T(8,128)(2,1)}, u32[]{:S(2)}, u32[]{:S(2)}) collective-permute-start(bf16[512,768]{1,0:T(8,128)(2,1)S(1)} %copy-done.7), channel_id=1, source_target_pairs={{8,0},{12,4},{16,8},{20,12},{24,16},{28,20},{9,1},{13,5},{17,9},{2... | collective-permute-start | bytes 2359304 | tf_op jit(solution)/shard_map/ppermute | solution.py:202
  413.7 53.8 %collective-permute-start.32 = (bf16[512,768]{1,0:T(8,128)(2,1)S(1)}, bf16[512,768]{1,0:T(8,128)(2,1)}, u32[]{:S(2)}, u32[]{:S(2)}) collective-permute-start(bf16[512,768]{1,0:T(8,128)(2,1)S(1)} %copy-done.7), channel_id=1, source_target_pairs={{0,8},{4,12},{8,16},{12,20},{16,24},{20,28},{1,9},{5,13},{9,17},{1... | collective-permute-start | bytes 2359304 | tf_op jit(solution)/shard_map/ppermute | solution.py:202
  470.6 30.9 %collective-permute-start.38 = (bf16[3,512,768]{2,1,0:T(8,128)(2,1)}, bf16[3,512,768]{2,1,0:T(8,128)(2,1)S(1)}, u32[]{:S(2)}, u32[]{:S(2)}) collective-permute-start(bf16[3,512,768]{2,1,0:T(8,128)(2,1)} %pad_maximum_fusion.1), channel_id=1, source_target_pairs={{0,4},{4,0},{8,12},{12,8},{16,20},{20,16},{24,28},{28,24},{1,5},{5... | collective-permute-start | bytes 7077896 | tf_op jit(solution)/shard_map/ppermute | solution.py:33
  470.7 30.8 %collective-permute-start.34 = (bf16[256,2048]{1,0:T(8,128)(2,1)}, bf16[256,2048]{1,0:T(8,128)(2,1)}, u32[]{:S(2)}, u32[]{:S(2)}) collective-permute-start(bf16[256,2048]{1,0:T(8,128)(2,1)} %get-tuple-element.158), channel_id=1, source_target_pairs={{0,8},{4,12},{1,9},{5,13},{2,10},{6,14},{3,11},{7,15}} | collective-permute-start | bytes 3145736 | tf_op jit(solution)/shard_map/ppermute | solution.py:202
  476.5 25.1 %collective-permute-start.35 = (bf16[256,2048]{1,0:T(8,128)(2,1)}, bf16[256,2048]{1,0:T(8,128)(2,1)}, u32[]{:S(2)}, u32[]{:S(2)}) collective-permute-start(bf16[256,2048]{1,0:T(8,128)(2,1)} %get-tuple-element.159), channel_id=1, source_target_pairs={{24,16},{28,20},{25,17},{29,21},{26,18},{30,22},{27,19},{31,23}} | collective-permute-start | bytes 3145736 | tf_op jit(solution)/shard_map/ppermute | solution.py:202
  479.6 21.9 %collective-permute-start.37 = (bf16[512,768]{1,0:T(8,128)(2,1)}, bf16[512,768]{1,0:T(8,128)(2,1)}, u32[]{:S(2)}, u32[]{:S(2)}) collective-permute-start(bf16[512,768]{1,0:T(8,128)(2,1)} %get-tuple-element.161), channel_id=1, source_target_pairs={{8,0},{12,4},{16,8},{20,12},{9,1},{13,5},{17,9},{21,13},{10,2},{14... | collective-permute-start | bytes 2359304 | tf_op jit(solution)/shard_map/ppermute | solution.py:202
  505.6 31.9 %collective-permute-start.43 = (bf16[2,512,768]{2,1,0:T(8,128)(2,1)}, bf16[2,512,768]{2,1,0:T(8,128)(2,1)S(1)}, u32[]{:S(2)}, u32[]{:S(2)}) collective-permute-start(bf16[2,512,768]{2,1,0:T(8,128)(2,1)} %pad_maximum_fusion.4), channel_id=1, source_target_pairs={{0,4},{4,0},{8,12},{12,8},{16,20},{20,16},{24,28},{28,24},{1,5},{5... | collective-permute-start | bytes 4718600 | tf_op jit(solution)/shard_map/ppermute | solution.py:33
  509.6 27.9 %collective-permute-start.40 = (bf16[256,2048]{1,0:T(8,128)(2,1)}, bf16[256,2048]{1,0:T(8,128)(2,1)}, u32[]{:S(2)}, u32[]{:S(2)}) collective-permute-start(bf16[256,2048]{1,0:T(8,128)(2,1)} %get-tuple-element.218), channel_id=1, source_target_pairs={{16,8},{20,12},{24,16},{28,20},{17,9},{21,13},{25,17},{29,21},{18,... | collective-permute-start | bytes 3145736 | tf_op jit(solution)/shard_map/ppermute | solution.py:202
  511.2 26.3 %collective-permute-start.39 = (bf16[256,2048]{1,0:T(8,128)(2,1)}, bf16[256,2048]{1,0:T(8,128)(2,1)}, u32[]{:S(2)}, u32[]{:S(2)}) collective-permute-start(bf16[256,2048]{1,0:T(8,128)(2,1)} %get-tuple-element.219), channel_id=1, source_target_pairs={{0,8},{4,12},{8,16},{12,20},{1,9},{5,13},{9,17},{13,21},{2,10},{6,... | collective-permute-start | bytes 3145736 | tf_op jit(solution)/shard_map/ppermute | solution.py:202
  514.1 16.3 %collective-permute-start.41 = (bf16[512,768]{1,0:T(8,128)(2,1)}, bf16[512,768]{1,0:T(8,128)(2,1)}, u32[]{:S(2)}, u32[]{:S(2)}) collective-permute-start(bf16[512,768]{1,0:T(8,128)(2,1)} %get-tuple-element.166), channel_id=1, source_target_pairs={{16,24},{20,28},{17,25},{21,29},{18,26},{22,30},{19,27},{23,31}} | collective-permute-start | bytes 2359304 | tf_op jit(solution)/shard_map/ppermute | solution.py:202
  515.7 21.8 %collective-permute-start.42 = (bf16[512,768]{1,0:T(8,128)(2,1)}, bf16[512,768]{1,0:T(8,128)(2,1)}, u32[]{:S(2)}, u32[]{:S(2)}) collective-permute-start(bf16[512,768]{1,0:T(8,128)(2,1)} %get-tuple-element.167), channel_id=1, source_target_pairs={{8,0},{12,4},{9,1},{13,5},{10,2},{14,6},{11,3},{15,7}} | collective-permute-start | bytes 2359304 | tf_op jit(solution)/shard_map/ppermute | solution.py:202
  546.1 29.7 %collective-permute-start.48 = (bf16[256,2048]{1,0:T(8,128)(2,1)}, bf16[256,2048]{1,0:T(8,128)(2,1)}, u32[]{:S(2)}, u32[]{:S(2)}) collective-permute-start(bf16[256,2048]{1,0:T(8,128)(2,1)} %get-tuple-element.216), channel_id=1, source_target_pairs={{8,0},{12,4},{16,8},{20,12},{24,16},{28,20},{9,1},{13,5},{17,9},{2... | collective-permute-start | bytes 3145736 | tf_op jit(solution)/shard_map/ppermute | solution.py:202
  547.4 28.4 %collective-permute-start.47 = (bf16[256,2048]{1,0:T(8,128)(2,1)}, bf16[256,2048]{1,0:T(8,128)(2,1)}, u32[]{:S(2)}, u32[]{:S(2)}) collective-permute-start(bf16[256,2048]{1,0:T(8,128)(2,1)} %get-tuple-element.217), channel_id=1, source_target_pairs={{0,8},{4,12},{8,16},{12,20},{16,24},{20,28},{1,9},{5,13},{9,17},{1... | collective-permute-start | bytes 3145736 | tf_op jit(solution)/shard_map/ppermute | solution.py:202
  554.6 21.3 %collective-permute-start.46 = (f32[80,128]{1,0:T(8,128)S(1)}, f32[80,128]{1,0:T(8,128)S(1)}, u32[]{:S(2)}, u32[]{:S(2)}) collective-permute-start(f32[80,128]{1,0:T(8,128)S(1)} %fusion.68), channel_id=1, source_target_pairs={{0,8},{4,12},{8,0},{12,4},{16,24},{20,28},{24,16},{28,20},{1,9},{5... | collective-permute-start | bytes 122888 | tf_op jit(solution)/shard_map/ppermute | solution.py:33
  (51 other events, 395.7 us)
Sparse Core Ops, SparseCore 0:
  9.6 84.7 all-gather.9
  96.0 80.5 all-gather.11
  182.7 89.9 reduce-scatter.1
  274.1 76.0 all-gather.7
  351.8 123.7 all-gather.13

commit v5 on v4

--- a/solution.py
+++ b/solution.py
@@ -1056,33 +1056,41 @@
     )
     terms = sum_of(terms, others, other_terms[1])
 
-    waiting = jnp.stack([attn_sum, *attn_got])
+    waiting = None
     grad_step = None
     for step in range(2, places):
         attn_held += [block[None] for block in attn_got]
+        attn_before = attn_got
         attn_got = gather_step(step, attn_got)
         grad_step = line_step(part_places, step - 1, grad_step) if grad_step else line_start(part_ends)
-        attn_other.append(flip(waiting, "ctx", 0))
+        if waiting is not None:
+            attn_other.append(flip(waiting, "ctx", 0))
+        waiting = jnp.stack([attn_sum, *attn_before] if step == 2 else attn_before)
+        other_terms = flip(terms, "ctx", 0) if step == 2 else terms
         late = []
         if step == 3:
             (pair_all,) = tie([pair_all], [grad_down_w])
             late = list(assemble(pair_all, pair_plan))
-        grad_step, attn_got, attn_other, late, part_places = stage(
-            grad_step, attn_got, attn_other, late, part_places
+        grad_step, attn_got, attn_other, late, part_places, waiting, terms, other_terms = stage(
+            grad_step, attn_got, attn_other, late, part_places, waiting, terms, other_terms
         )
+        if step == 2:
+            terms = terms + other_terms
         if step == 3:
             grad_gate_w, grad_up_w = late
-        waiting = jnp.stack(attn_got)
     attn_held += [block[None] for block in attn_got]
     grad_step = line_step(part_places, places - 1, grad_step) if grad_step else line_start(part_ends)
     attn_other.append(flip(waiting, "ctx", 0))
+    attn_last = [flip(block[None], "ctx", 0) for block in attn_got]
     sources = [(attn_held[0], 0), (attn_other[0], 0)]
     for step in range(1, places):
         sources += [(attn_held[2 * step - 1], 0), (attn_held[2 * step], 0)]
         first = 1 if step == 1 else 0
-        sources += [(attn_other[step - 1], first), (attn_other[step - 1], first + 1)]
+        if step < places - 1:
+            sources += [(attn_other[step - 1], first), (attn_other[step - 1], first + 1)]
+        else:
+            sources += [(block, 0) for block in attn_last]
     grad_attn_w = assemble_line(sources, line_origins(), attn_plan[0])
-    terms = terms + flip(terms, "ctx", 0)
     other_terms = flip(terms, "ctx", 1)
     grad_attn_w, other_terms, grad_step, part_places = stage(grad_attn_w, other_terms, grad_step, part_places)
     terms = terms + other_terms

time: 608 us -> 606 us (level)
  waiting for transfers between devices: 109 us -> 100 us
    ppermute x12, waiting for transfers between devices: 48.9 us -> 41.5 us  [shift(): return lax.ppermute(values, 'ctx', pairs)]
    unnamed x96 -> x106, local copies, waits for them, and re-layouts: 24.5 us -> 26.7 us
    ppermute x35 -> x36, starting transfers between devices: 36.4 us -> 37.7 us  [flip(): return lax.ppermute(values, axis, [(i, i ^ 1 << bit) for i in range(count)])]
    ppermute x35 -> x36, waiting for transfers between devices: 58.8 us -> 57.5 us  [flip(): return lax.ppermute(values, axis, [(i, i ^ 1 << bit) for i in range(count)])]
  transfers between devices with their start and end apart: 55 -> 56, of which waited for: 18 -> 19; matrix products, arithmetic and copies ran while one was open for 31% -> 32% of each run, Pallas kernels for 31% -> 31%
where the time goes in v5:
time: 606 us; the launch traced here: 595 us
  Pallas kernels  186 us (31%)
  waiting for transfers between devices  100 us (17%)
  local copies, waits for them, and re-layouts  83.1 us (14%)
  other arithmetic  78.4 us (13%)
  starting transfers between devices  75.3 us (12%)
  matrix products  56.8 us (9%)
  between operations  15.1 us (2%)
    ppermute x36, waiting for transfers between devices, flip(): return lax.ppermute(values, axis, [(i, i ^ 1 << bit) for i in range(count)])  57.5 us
    dot_general x5, matrix products, matmul_tn(): lax.dot_general(left, right, (((0,), (0,)), ((), ())), preferred_element_...  56.8 us
    pallas_call x1, Pallas kernels, attention_backward(): pl.pallas_call(functools.partial(backward_kernel, heads), out_shape=jax.S...  41.9 us
    ppermute x12, waiting for transfers between devices, shift(): return lax.ppermute(values, 'ctx', pairs)  41.5 us
    ppermute x36, starting transfers between devices, flip(): return lax.ppermute(values, axis, [(i, i ^ 1 << bit) for i in range(count)])  37.7 us
    ppermute x12, starting transfers between devices, shift(): return lax.ppermute(values, 'ctx', pairs)  32.9 us
    pallas_call x1, Pallas kernels, input_side(): pl.pallas_call(functools.partial(input_kernel, spans), grid=(tokens // CH...  31.6 us
    unnamed x106, local copies, waits for them, and re-layouts  26.7 us
  transfers between devices with their start and end apart: 56, of which 19 were waited for; matrix products, arithmetic and copies ran while one was open for 32% of the time, Pallas kernels for 31%

profile of v5, /device:TPU:0, one launch (start us, length us, event | category | flops | bytes accessed | tf_op | source)
XLA Modules:
  0.0 594.9 jit_solution(11525503926727429239)
XLA Ops:
  10.1 2.9 constant_dynamic-slice_fusion.10
  13.0 2.8 concatenate.40
  17.5 3.0 collective-permute-start.1
  22.0 4.2 constant_dynamic-slice_fusion.2
  34.8 5.6 fusion.26
  50.7 5.9 collective-permute-done.3.refs_1_
  58.7 6.3 %collective-permute-done.4.refs_2_ = bf16[256,768]{1,0:T(8,128)(2,1)} collective-permute-done((bf16[256,768]{1,0:T(8,128)(2,1)S(1)}, bf16[256,768]{1,0:T(8,128)(2,1)}, u32[]{:S(2)}, u32[]{:S(2)}) %collective-permute-start.4) | collective-permute-done | bytes 393248 | tf_op jit(solution)/shard_map/ppermute | solution.py:33
  77.3 4.5 collective-permute-done.7.refs_1_
  84.4 7.0 %collective-permute-done.9.refs_3_ = bf16[256,768]{1,0:T(8,128)(2,1)S(1)} collective-permute-done((bf16[256,768]{1,0:T(8,128)(2,1)}, bf16[256,768]{1,0:T(8,128)(2,1)S(1)}, u32[]{:S(2)}, u32[]{:S(2)}) %collective-permute-start.9) | collective-permute-done | bytes 393248 | tf_op jit(solution)/shard_map/ppermute | solution.py:33
  99.7 17.2 %attn_side.1 = (bf16[2048,2048]{1,0:T(8,128)(2,1)}, f32[2048,768]{1,0:T(8,128)}) custom-call(s32[5]{0:T(128)} %stack.205.at_ref, bf16[2048,2048]{1,0:T(8,128)(2,1)} %bitcast.263, f32[1,2048]{1,0:T(1,128)} %bitcast.262, f32[1,2048]{1,0:T(1,128)} %bitcast.261, f32[1,768]{1,0:T(1,128)} %broadcast_in_dim.143.shift_ref, ...), custom_call_target="tpu_custom_call" | custom-call | flops 17999998976 | tf_op jit(solution)/shard_map/attn_side/pallas_call | solution.py:582
  116.9 22.6 %attention_forward.1 = (bf16[2048,256]{1,0:T(8,128)(2,1)S(1)}, bf16[2048,256]{1,0:T(8,128)(2,1)S(1)}, bf16[2048,256]{1,0:T(8,128)(2,1)S(1)}, bf16[2048,256]{1,0:...) custom-call(s32[16]{0:T(128)S(1)} %select_reduce_fusion.slot_ref, s32[8]{0:T(128)S(1)} %and_select_fusion.1.low_ref, ...), custom_call_target="tpu_custom_call" | custom-call | flops 24999999488 | tf_op jit(solution)/shard_map/attention_forward/pallas_call | solution.py:471
  145.8 20.7 %pair_side.1 = (bf16[2048,768]{1,0:T(8,128)(2,1)}, bf16[2048,768]{1,0:T(8,128)(2,1)}, bf16[2048,768]{1,0:T(8,128)(2,1)}) custom-call(s32[5]{0:T(128)} %stack.205.at_ref, bf16[2048,2048]{1,0:T(8,128)(2,1)} %get-tuple-element.108.normed_ref, bf16[512,768]{1,0:T(8,128)(2,1)} %concatenate.43.refs_0_, bf16[512,768]{1,0:T(8,128)(2,1)} %get-tuple-element.115.refs_1_, ...), custom_call_target="tpu_custom_call" | custom-call | flops 28000000000 | tf_op jit(solution)/shard_map/pair_side/pallas_call | solution.py:601
  167.6 15.0 %out_side.1.refs_1_ = bf16[2048,2048]{1,0:T(8,128)(2,1)} custom-call(s32[2,4]{1,0:T(2,128)} %pad_add_fusion.at_ref, bf16[2048,256]{1,0:T(8,128)(2,1)} %get-tuple-element.127.mixed_ref, bf16[2048,768]{1,0:T(8,128)(2,1)} %get-tuple-element.126.act_ref, bf16[240,2048]{1,0:T(8,128)(2,1)} %get-tuple-element.123.refs_0_.refs_4_, ...), custom_call_target="tpu_custom_call" | custom-call | flops 15000000512 | tf_op jit(solution)/shard_map/out_side/pallas_call | solution.py:697
  183.0 10.3 %fusion.57 = bf16[768,2048]{1,0:T(8,128)(2,1)S(1)} fusion(bf16[2048,768]{1,0:T(8,128)(2,1)} %get-tuple-element.126.act_ref, bf16[2048,2048]{1,0:T(8,128)(2,1)} %tie.22.refs_1_), kind=kOutput, calls=%fused_computation.186 | convolution fusion | flops 6442450944 | bytes 14680064 | tf_op jit(solution)/shard_map/dot_general | solution.py:28
  205.6 17.0 %grad_side.1 = (bf16[2048,768]{1,0:T(8,128)(2,1)}, bf16[2048,768]{1,0:T(8,128)(2,1)}, bf16[2048,256]{1,0:T(8,128)(2,1)}) custom-call(s32[2,4]{1,0:T(2,128)} %pad_add_fusion.at_ref, bf16[2048,2048]{1,0:T(8,128)(2,1)} %get-tuple-element.130.grad_ref, bf16[2048,768]{1,0:T(8,128)(2,1)} %get-tuple-element.131.slope_ref, ...), custom_call_target="tpu_custom_call" | custom-call | flops 17999998976 | tf_op jit(solution)/shard_map/grad_side/pallas_call | solution.py:665
  229.8 11.5 %convolution_convert_fusion.2.refs_0_ = bf16[2048,768]{1,0:T(8,128)(2,1)} fusion(bf16[2048,2048]{1,0:T(8,128)(2,1)} %get-tuple-element.108.normed_ref, bf16[2048,768]{1,0:T(8,128)(2,1)} %get-tuple-element.137.gate_ref), kind=kOutput, calls=%fused_computation.9 | convolution fusion | flops 6444023808 | bytes 14680064 | tf_op jit(solution)/shard_map/dot_general | solution.py:28
  241.4 20.9 %convolution_convert_fusion.1.refs_1_ = bf16[2048,768]{1,0:T(8,128)(2,1)} fusion(bf16[2048,2048]{1,0:T(8,128)(2,1)} %get-tuple-element.108.normed_ref, bf16[2048,768]{1,0:T(8,128)(2,1)S(1)} %copy-done.27), kind=kOutput, calls=%fused_computation.8 | convolution fusion | flops 6444023808 | bytes 14680064 | tf_op jit(solution)/shard_map/dot_general | solution.py:28
  271.5 41.9 %attention_backward.1.refs_0_ = bf16[2048,768]{1,0:T(8,128)(2,1)} custom-call(s32[16]{0:T(128)S(1)} %select_reduce_fusion.slot_ref, s32[8]{0:T(128)S(1)} %and_select_fusion.1.low_ref, bf16[2048,256]{1,0:T(8,128)(2,1)S(1)} %get-tuple-element.110.q_ref, bf16[2048,256]{1,0:T(8,128)(2,1)S(1)} %get-tuple-element.111.k_ref, bf16[2048,256]{1,0:T(8,128)(2,1)S(1)} %copy-done.14, ...), custom_call_target="tpu_custom_call" | custom-call | flops 40000000000 | tf_op jit(solution)/shard_map/attention_backward/pallas_call | solution.py:496
  317.0 11.6 %convolution_convert_fusion.refs_0_ = bf16[2048,768]{1,0:T(8,128)(2,1)} fusion(bf16[2048,2048]{1,0:T(8,128)(2,1)} %get-tuple-element.108.normed_ref, bf16[2048,768]{1,0:T(8,128)(2,1)} %get-tuple-element.145.refs_2_), kind=kOutput, calls=%fused_computation.7 | convolution fusion | flops 6444023808 | bytes 14680064 | tf_op jit(solution)/shard_map/dot_general | solution.py:28
  334.2 10.7 %collective-permute-done.22 = bf16[512,768]{1,0:T(8,128)(2,1)S(1)} collective-permute-done((bf16[512,768]{1,0:T(8,128)(2,1)S(1)}, bf16[512,768]{1,0:T(8,128)(2,1)S(1)}, u32[]{:S(2)}, u32[]{:S(2)}) %collective-permute-start.22) | collective-permute-done | bytes 786464 | tf_op jit(solution)/shard_map/ppermute | solution.py:33
  353.8 31.6 %input_side.1 = (bf16[2048,2048]{1,0:T(8,128)(2,1)}, f32[2,2048]{1,0:T(2,128)}) custom-call(s32[5]{0:T(128)} %stack.205.at_ref, bf16[2048,768]{1,0:T(8,128)(2,1)} %get-tuple-element.137.gate_ref, bf16[2048,768]{1,0:T(8,128)(2,1)} %get-tuple-element.138.up_ref, bf16[2048,768]{1,0:T(8,128)(2,1)} %get-tuple-element.149.merged_ref, ...), custom_call_target="tpu_custom_call" | custom-call | flops 30000001024 | tf_op jit(solution)/shard_map/input_side/pallas_call | solution.py:738
  391.8 5.7 collective-permute-done.27
  401.3 4.9 dynamic-slice_bitcast_fusion
  413.7 4.2 collective-permute-start.32
  417.9 7.8 %fusion.refs_4_ = bf16[4,256,2048]{2,1,0:T(8,128)(2,1)} fusion(bf16[4,256,2048]{2,1,0:T(8,128)(2,1)} %collective-permute-done.31, bf16[4,2,256,2048]{3,2,1,0:T(8,128)(2,1)} %bitcast.248, s32[]{:T(128)S(6)} %select_n.394), kind=kLoop, calls=%fused_computation.1 | loop fusion | flops 8388608 | bytes 12582916 | tf_op jit(solution)/shard_map/convert_element_type | solution.py:1041
  425.7 3.1 dynamic-slice_bitcast_fusion.1
  428.8 3.0 fusion.12
  431.8 3.2 slice.176
  435.0 6.4 %bitcast_convert_fusion.refs_10_ = f32[1408,2048]{1,0:T(8,128)} fusion(bf16[8,176,2048]{2,1,0:T(8,128)(2,1)S(1)} %slice.176), kind=kLoop, calls=%fused_computation.4 | loop fusion | flops 2883584 | bytes 17301504 | tf_op jit(solution)/shard_map/convert_element_type | solution.py:1047
  443.1 2.7 bitcast_convert_fusion.1.refs_11_
  445.8 21.6 %collective-permute-done.33.refs_8_ = bf16[512,768]{1,0:T(8,128)(2,1)S(1)} collective-permute-done((bf16[512,768]{1,0:T(8,128)(2,1)S(1)}, bf16[512,768]{1,0:T(8,128)(2,1)S(1)}, u32[]{:S(2)}, u32[]{:S(2)}) %collective-permute-start.33) | collective-permute-done | bytes 786464 | tf_op jit(solution)/shard_map/ppermute | solution.py:202
  471.6 7.1 %collective-permute-start.34 = (bf16[256,2048]{1,0:T(8,128)(2,1)}, bf16[256,2048]{1,0:T(8,128)(2,1)S(1)}, u32[]{:S(2)}, u32[]{:S(2)}) collective-permute-start(bf16[256,2048]{1,0:T(8,128)(2,1)} %get-tuple-element.161), channel_id=1, source_target_pairs={{0,8},{4,12},{1,9},{5,13},{2,10},{6,14},{3,11},{7,15}} | collective-permute-start | bytes 3145736 | tf_op jit(solution)/shard_map/ppermute | solution.py:202
  482.7 3.0 pad_maximum_fusion.1.refs_5_
  485.8 8.8 %collective-permute-done.37.refs_3_ = bf16[512,768]{1,0:T(8,128)(2,1)} collective-permute-done((bf16[512,768]{1,0:T(8,128)(2,1)}, bf16[512,768]{1,0:T(8,128)(2,1)}, u32[]{:S(2)}, u32[]{:S(2)}) %collective-permute-start.37) | collective-permute-done | bytes 786464 | tf_op jit(solution)/shard_map/ppermute | solution.py:202
  494.6 6.8 %collective-permute-done.34.refs_0_ = bf16[256,2048]{1,0:T(8,128)(2,1)S(1)} collective-permute-done((bf16[256,2048]{1,0:T(8,128)(2,1)}, bf16[256,2048]{1,0:T(8,128)(2,1)S(1)}, u32[]{:S(2)}, u32[]{:S(2)}) %collective-permute-start.34) | collective-permute-done | bytes 1048608 | tf_op jit(solution)/shard_map/ppermute | solution.py:202
  502.7 4.0 fusion.15
  508.3 4.9 collective-permute-start.39
  516.7 2.7 pad_maximum_fusion.4.refs_8_
  519.4 4.3 copy-done.2
  523.7 9.0 %assemble.1 = (f32[512,5632]{1,0:T(8,128)}, f32[512,5632]{1,0:T(8,128)}) custom-call(bf16[8,512,1408]{2,1,0:T(8,128)(2,1)S(1)} %copy-done.2), custom_call_target="tpu_custom_call" | custom-call | tf_op jit(solution)/shard_map/assemble/pallas_call | solution.py:771
  532.7 4.3 collective-permute-done.42.refs_3_
  538.4 4.6 fusion.18
  544.5 5.8 collective-permute-start.48
  556.8 10.8 %assemble_line.1.refs_0_ = f32[512,6144]{1,0:T(8,128)} custom-call(s32[14]{0:T(128)S(1)} %stack.251.at_ref, bf16[1,512,768]{2,1,0:T(8,128)(2,1)S(1)} %bitcast.239, bf16[3,512,768]{2,1,0:T(8,128)(2,1)S(1)} %copy-done.4, bf16[1,512,768]{2,1,0:T(8,128)(2,1)S(1)} %bitcast.243, bf16[1,512,768]{2,1,0:T(8,128)(2,1)S(1)} %bitcast.241, ...), custom_call_target="tpu_custom_call" | custom-call | tf_op jit(solution)/shard_map/assemble_line/pallas_call | solution.py:805
  567.5 5.9 collective-permute-done.47.refs_1_
  574.9 2.8 fusion.46
  577.8 4.7 collective-permute-start.50
  582.5 4.1 fusion.30
  (323 shorter events, 150.5 us)
Async XLA Ops:
  7.2 92.5 %all-gather.10.cloned.1.call-start = ((), (), s32[]{:S(2)}) async-start(), calls=%async_computation.3 | async-start | bytes 9437184 | tf_op jit(solution)/shard_map/all_gather | solution.py:183
  7.9 175.0 %all-gather.12.cloned.1.call-start = ((), (), s32[]{:S(2)}) async-start(), calls=%async_computation.4 | async-start | bytes 9437184 | tf_op jit(solution)/shard_map/all_gather | solution.py:183
  8.7 420.1 %reduce-scatter.2.cloned.1.call-start = ((), (), s32[]{:S(2)}) async-start(), calls=%async_computation.1 | async-start | bytes 9437184 | tf_op jit(solution)/shard_map/reduce_scatter | solution.py:194
  17.5 24.5 %collective-permute-start.1 = (bf16[528,768]{1,0:T(8,128)(2,1)}, bf16[528,768]{1,0:T(8,128)(2,1)S(1)}, u32[]{:S(2)}, u32[]{:S(2)}) collective-permute-start(bf16[528,768]{1,0:T(8,128)(2,1)} %pad_maximum_fusion.10.refs_0_.refs_10_), channel_id=1, source_target_pairs={{0,2},{1,3},{2,0},{3,1},{4,6},{5,7},{6,4},{7,5},{8,10},{9,11},{10,... | collective-permute-start | bytes 2433032 | tf_op jit(solution)/shard_map/ppermute | solution.py:33
  20.5 21.6 %collective-permute-start = (bf16[528,768]{1,0:T(8,128)(2,1)}, bf16[528,768]{1,0:T(8,128)(2,1)}, u32[]{:S(2)}, u32[]{:S(2)}) collective-permute-start(bf16[528,768]{1,0:T(8,128)(2,1)} %pad_maximum_fusion.10.refs_0_.refs_10_), channel_id=1, source_target_pairs={{0,1},{1,0},{2,3},{3,2},{4,5},{5,4},{6,7},{7,6},{8,9},{9,8},{10,11... | collective-permute-start | bytes 2433032 | tf_op jit(solution)/shard_map/ppermute | solution.py:33
  28.7 27.9 %collective-permute-start.3 = (bf16[512,768]{1,0:T(8,128)(2,1)}, bf16[512,768]{1,0:T(8,128)(2,1)}, u32[]{:S(2)}, u32[]{:S(2)}) collective-permute-start(bf16[512,768]{1,0:T(8,128)(2,1)} %concatenate.43.refs_0_), channel_id=1, source_target_pairs={{0,2},{1,3},{2,0},{3,1},{4,6},{5,7},{6,4},{7,5},{8,10},{9,11},{10,... | collective-permute-start | bytes 2359304 | tf_op jit(solution)/shard_map/ppermute | solution.py:33
  29.7 28.9 %collective-permute-start.2 = (bf16[512,768]{1,0:T(8,128)(2,1)}, bf16[512,768]{1,0:T(8,128)(2,1)}, u32[]{:S(2)}, u32[]{:S(2)}) collective-permute-start(bf16[512,768]{1,0:T(8,128)(2,1)} %concatenate.43.refs_0_), channel_id=1, source_target_pairs={{0,1},{1,0},{2,3},{3,2},{4,5},{5,4},{6,7},{7,6},{8,9},{9,8},{10,11... | collective-permute-start | bytes 2359304 | tf_op jit(solution)/shard_map/ppermute | solution.py:33
  44.0 21.0 %collective-permute-start.4 = (bf16[256,768]{1,0:T(8,128)(2,1)S(1)}, bf16[256,768]{1,0:T(8,128)(2,1)}, u32[]{:S(2)}, u32[]{:S(2)}) collective-permute-start(bf16[256,768]{1,0:T(8,128)(2,1)S(1)} %slice.130), channel_id=1, source_target_pairs={{0,2},{1,3},{2,0},{3,1},{4,6},{5,7},{6,4},{7,5},{8,10},{9,11},{10,... | collective-permute-start | bytes 1179656 | tf_op jit(solution)/shard_map/ppermute | solution.py:33
  47.1 20.4 %collective-permute-start.5 = (bf16[272,768]{1,0:T(8,128)(2,1)S(1)}, bf16[272,768]{1,0:T(8,128)(2,1)S(1)}, u32[]{:S(2)}, u32[]{:S(2)}) collective-permute-start(bf16[272,768]{1,0:T(8,128)(2,1)S(1)} %slice.131), channel_id=1, source_target_pairs={{0,1},{1,0},{2,3},{3,2},{4,5},{5,4},{6,7},{7,6},{8,9},{9,8},{10,11... | collective-permute-start | bytes 1253384 | tf_op jit(solution)/shard_map/ppermute | solution.py:33
  48.1 33.6 %collective-permute-start.7 = (bf16[512,768]{1,0:T(8,128)(2,1)}, bf16[512,768]{1,0:T(8,128)(2,1)S(1)}, u32[]{:S(2)}, u32[]{:S(2)}) collective-permute-start(bf16[512,768]{1,0:T(8,128)(2,1)} %get-tuple-element.117.refs_5_), channel_id=1, source_target_pairs={{0,2},{1,3},{2,0},{3,1},{4,6},{5,7},{6,4},{7,5},{8,10},{9,11},{10,... | collective-permute-start | bytes 2359304 | tf_op jit(solution)/shard_map/ppermute | solution.py:33
  56.6 27.8 %collective-permute-start.6 = (bf16[512,768]{1,0:T(8,128)(2,1)}, bf16[512,768]{1,0:T(8,128)(2,1)S(1)}, u32[]{:S(2)}, u32[]{:S(2)}) collective-permute-start(bf16[512,768]{1,0:T(8,128)(2,1)} %get-tuple-element.117.refs_5_), channel_id=1, source_target_pairs={{0,1},{1,0},{2,3},{3,2},{4,5},{5,4},{6,7},{7,6},{8,9},{9,8},{10,11... | collective-permute-start | bytes 2359304 | tf_op jit(solution)/shard_map/ppermute | solution.py:33
  72.6 18.7 %collective-permute-start.9 = (bf16[256,768]{1,0:T(8,128)(2,1)}, bf16[256,768]{1,0:T(8,128)(2,1)S(1)}, u32[]{:S(2)}, u32[]{:S(2)}) collective-permute-start(bf16[256,768]{1,0:T(8,128)(2,1)} %slice.138), channel_id=1, source_target_pairs={{0,1},{1,0},{2,3},{3,2},{4,5},{5,4},{6,7},{7,6},{8,9},{9,8},{10,11... | collective-permute-start | bytes 1179656 | tf_op jit(solution)/shard_map/ppermute | solution.py:33
  74.1 17.2 %collective-permute-start.8 = (bf16[256,768]{1,0:T(8,128)(2,1)}, bf16[256,768]{1,0:T(8,128)(2,1)}, u32[]{:S(2)}, u32[]{:S(2)}) collective-permute-start(bf16[256,768]{1,0:T(8,128)(2,1)} %slice.137), channel_id=1, source_target_pairs={{0,2},{1,3},{2,0},{3,1},{4,6},{5,7},{6,4},{7,5},{8,10},{9,11},{10,... | collective-permute-start | bytes 1179656 | tf_op jit(solution)/shard_map/ppermute | solution.py:33
  92.1 49.5 %collective-permute-start.13 = (bf16[240,2048]{1,0:T(8,128)(2,1)}, bf16[240,2048]{1,0:T(8,128)(2,1)}, u32[]{:S(2)}, u32[]{:S(2)}) collective-permute-start(bf16[240,2048]{1,0:T(8,128)(2,1)} %get-tuple-element.123.refs_0_.refs_4_), channel_id=1, source_target_pairs={{0,2},{1,3},{2,0},{3,1},{4,6},{5,7},{6,4},{7,5},{8,10},{9,11},{10,... | collective-permute-start | bytes 2949128 | tf_op jit(solution)/shard_map/ppermute | solution.py:33
  92.4 49.2 %collective-permute-start.12 = (bf16[240,2048]{1,0:T(8,128)(2,1)}, bf16[240,2048]{1,0:T(8,128)(2,1)}, u32[]{:S(2)}, u32[]{:S(2)}) collective-permute-start(bf16[240,2048]{1,0:T(8,128)(2,1)} %get-tuple-element.123.refs_0_.refs_4_), channel_id=1, source_target_pairs={{0,1},{1,0},{2,3},{3,2},{4,5},{5,4},{6,7},{7,6},{8,9},{9,8},{10,11... | collective-permute-start | bytes 2949128 | tf_op jit(solution)/shard_map/ppermute | solution.py:33
  97.6 43.9 %collective-permute-start.11 = (bf16[256,768]{1,0:T(8,128)(2,1)}, bf16[256,768]{1,0:T(8,128)(2,1)}, u32[]{:S(2)}, u32[]{:S(2)}) collective-permute-start(bf16[256,768]{1,0:T(8,128)(2,1)} %slice.140), channel_id=1, source_target_pairs={{0,1},{1,0},{2,3},{3,2},{4,5},{5,4},{6,7},{7,6},{8,9},{9,8},{10,11... | collective-permute-start | bytes 1179656 | tf_op jit(solution)/shard_map/ppermute | solution.py:33
  97.9 43.6 %collective-permute-start.10 = (bf16[256,768]{1,0:T(8,128)(2,1)}, bf16[256,768]{1,0:T(8,128)(2,1)}, u32[]{:S(2)}, u32[]{:S(2)}) collective-permute-start(bf16[256,768]{1,0:T(8,128)(2,1)} %slice.139), channel_id=1, source_target_pairs={{0,2},{1,3},{2,0},{3,1},{4,6},{5,7},{6,4},{7,5},{8,10},{9,11},{10,... | collective-permute-start | bytes 1179656 | tf_op jit(solution)/shard_map/ppermute | solution.py:33
  142.6 23.9 %collective-permute-start.14 = (bf16[112,2048]{1,0:T(8,128)(2,1)S(1)}, bf16[112,2048]{1,0:T(8,128)(2,1)S(1)}, u32[]{:S(2)}, u32[]{:S(2)}) collective-permute-start(bf16[112,2048]{1,0:T(8,128)(2,1)S(1)} %slice.141), channel_id=1, source_target_pairs={{0,2},{1,3},{2,0},{3,1},{4,6},{5,7},{6,4},{7,5},{8,10},{9,11},{10,... | collective-permute-start | bytes 1376264 | tf_op jit(solution)/shard_map/ppermute | solution.py:33
  143.9 22.6 %collective-permute-start.15 = (bf16[128,2048]{1,0:T(8,128)(2,1)S(1)}, bf16[128,2048]{1,0:T(8,128)(2,1)S(1)}, u32[]{:S(2)}, u32[]{:S(2)}) collective-permute-start(bf16[128,2048]{1,0:T(8,128)(2,1)S(1)} %slice.142), channel_id=1, source_target_pairs={{0,1},{1,0},{2,3},{3,2},{4,5},{5,4},{6,7},{7,6},{8,9},{9,8},{10,11... | collective-permute-start | bytes 1572872 | tf_op jit(solution)/shard_map/ppermute | solution.py:33
  182.6 249.2 %all-gather.8.cloned.1.call-start = ((), (), s32[]{:S(2)}) async-start(), calls=%async_computation.2 | async-start | bytes 8847360 | tf_op jit(solution)/shard_map/all_gather | solution.py:183
  202.1 20.7 %collective-permute-start.16 = (bf16[2,240,1024]{2,1,0:T(8,128)(2,1)S(1)}, bf16[2,240,1024]{2,1,0:T(8,128)(2,1)}, u32[]{:S(2)}, u32[]{:S(2)}) collective-permute-start(bf16[2,240,1024]{2,1,0:T(8,128)(2,1)S(1)} %pad_maximum_fusion.7), channel_id=1, source_target_pairs={{0,1},{1,0},{2,3},{3,2},{4,5},{5,4},{6,7},{7,6},{8,9},{9,8},{10,11... | collective-permute-start | bytes 2949128 | tf_op jit(solution)/shard_map/ppermute | solution.py:33
  204.0 20.7 %collective-permute-start.17 = (bf16[2,240,1024]{2,1,0:T(8,128)(2,1)S(1)}, bf16[2,240,1024]{2,1,0:T(8,128)(2,1)}, u32[]{:S(2)}, u32[]{:S(2)}) collective-permute-start(bf16[2,240,1024]{2,1,0:T(8,128)(2,1)S(1)} %pad_maximum_fusion.8), channel_id=1, source_target_pairs={{0,2},{1,3},{2,0},{3,1},{4,6},{5,7},{6,4},{7,5},{8,10},{9,11},{10,... | collective-permute-start | bytes 2949128 | tf_op jit(solution)/shard_map/ppermute | solution.py:33
  226.0 36.3 %collective-permute-start.19 = (bf16[240,1024]{1,0:T(8,128)(2,1)S(1)}, bf16[240,1024]{1,0:T(8,128)(2,1)S(1)}, u32[]{:S(2)}, u32[]{:S(2)}) collective-permute-start(bf16[240,1024]{1,0:T(8,128)(2,1)S(1)} %fusion.31), channel_id=1, source_target_pairs={{0,2},{1,3},{2,0},{3,1},{4,6},{5,7},{6,4},{7,5},{8,10},{9,11},{10,... | collective-permute-start | bytes 1474568 | tf_op jit(solution)/shard_map/ppermute | solution.py:33
  229.1 34.7 %collective-permute-start.18 = (bf16[240,1024]{1,0:T(8,128)(2,1)S(1)}, bf16[240,1024]{1,0:T(8,128)(2,1)S(1)}, u32[]{:S(2)}, u32[]{:S(2)}) collective-permute-start(bf16[240,1024]{1,0:T(8,128)(2,1)S(1)} %fusion.34), channel_id=1, source_target_pairs={{0,1},{1,0},{2,3},{3,2},{4,5},{5,4},{6,7},{7,6},{8,9},{9,8},{10,11... | collective-permute-start | bytes 1474568 | tf_op jit(solution)/shard_map/ppermute | solution.py:33
  266.3 253.1 %all-gather.14.cloned.1.call-start = ((), (), s32[]{:S(2)}) async-start(), calls=%async_computation.5 | async-start | bytes 12976128 | tf_op jit(solution)/shard_map/all_gather | solution.py:183
  268.1 45.3 %collective-permute-start.21 = (bf16[2,512,768]{2,1,0:T(8,128)(2,1)S(1)}, bf16[2,512,768]{2,1,0:T(8,128)(2,1)}, u32[]{:S(2)}, u32[]{:S(2)}) collective-permute-start(bf16[2,512,768]{2,1,0:T(8,128)(2,1)S(1)} %pad_maximum_fusion.3), channel_id=1, source_target_pairs={{0,2},{1,3},{2,0},{3,1},{4,6},{5,7},{6,4},{7,5},{8,10},{9,11},{10,... | collective-permute-start | bytes 4718600 | tf_op jit(solution)/shard_map/ppermute | solution.py:33
  270.1 43.3 %collective-permute-start.20 = (bf16[2,512,768]{2,1,0:T(8,128)(2,1)S(1)}, bf16[2,512,768]{2,1,0:T(8,128)(2,1)}, u32[]{:S(2)}, u32[]{:S(2)}) collective-permute-start(bf16[2,512,768]{2,1,0:T(8,128)(2,1)S(1)} %pad_maximum_fusion.2), channel_id=1, source_target_pairs={{0,1},{1,0},{2,3},{3,2},{4,5},{5,4},{6,7},{7,6},{8,9},{9,8},{10,11... | collective-permute-start | bytes 4718600 | tf_op jit(solution)/shard_map/ppermute | solution.py:33
  316.7 17.2 %collective-permute-start.23 = (bf16[512,768]{1,0:T(8,128)(2,1)S(1)}, bf16[512,768]{1,0:T(8,128)(2,1)S(1)}, u32[]{:S(2)}, u32[]{:S(2)}) collective-permute-start(bf16[512,768]{1,0:T(8,128)(2,1)S(1)} %fusion.20), channel_id=1, source_target_pairs={{0,2},{1,3},{2,0},{3,1},{4,6},{5,7},{6,4},{7,5},{8,10},{9,11},{10,... | collective-permute-start | bytes 2359304 | tf_op jit(solution)/shard_map/ppermute | solution.py:33
  350.1 37.4 %collective-permute-start.24 = (bf16[2,512,384]{2,1,0:T(8,128)(2,1)}, bf16[2,512,384]{2,1,0:T(8,128)(2,1)}, u32[]{:S(2)}, u32[]{:S(2)}) collective-permute-start(bf16[2,512,384]{2,1,0:T(8,128)(2,1)} %pad_maximum_fusion.11), channel_id=1, source_target_pairs={{0,1},{1,0},{2,3},{3,2},{4,5},{5,4},{6,7},{7,6},{8,9},{9,8},{10,11... | collective-permute-start | bytes 2359304 | tf_op jit(solution)/shard_map/ppermute | solution.py:33
  352.1 35.4 %collective-permute-start.25 = (bf16[2,512,384]{2,1,0:T(8,128)(2,1)}, bf16[2,512,384]{2,1,0:T(8,128)(2,1)}, u32[]{:S(2)}, u32[]{:S(2)}) collective-permute-start(bf16[2,512,384]{2,1,0:T(8,128)(2,1)} %pad_maximum_fusion.12), channel_id=1, source_target_pairs={{0,2},{1,3},{2,0},{3,1},{4,6},{5,7},{6,4},{7,5},{8,10},{9,11},{10,... | collective-permute-start | bytes 2359304 | tf_op jit(solution)/shard_map/ppermute | solution.py:33
  406.5 39.3 %collective-permute-start.30 = (f32[80,128]{1,0:T(8,128)S(1)}, f32[80,128]{1,0:T(8,128)S(1)}, u32[]{:S(2)}, u32[]{:S(2)}) collective-permute-start(f32[80,128]{1,0:T(8,128)S(1)} %copy-done.31), channel_id=1, source_target_pairs={{0,3},{1,0},{2,1},{3,2},{4,7},{5,4},{6,5},{7,6},{8,11},{9,8},{10,9... | collective-permute-start | bytes 122888 | tf_op jit(solution)/shard_map/ppermute | solution.py:113
  408.2 37.6 %collective-permute-start.29 = (f32[80,128]{1,0:T(8,128)S(1)}, f32[80,128]{1,0:T(8,128)S(1)}, u32[]{:S(2)}, u32[]{:S(2)}) collective-permute-start(f32[80,128]{1,0:T(8,128)S(1)} %copy-done.31), channel_id=1, source_target_pairs={{0,2},{1,3},{2,0},{3,1},{4,6},{5,7},{6,4},{7,5},{8,10},{9,11},{10,... | collective-permute-start | bytes 122888 | tf_op jit(solution)/shard_map/ppermute | solution.py:113
  408.7 37.1 %collective-permute-start.28 = (f32[80,128]{1,0:T(8,128)S(1)}, f32[80,128]{1,0:T(8,128)S(1)}, u32[]{:S(2)}, u32[]{:S(2)}) collective-permute-start(f32[80,128]{1,0:T(8,128)S(1)} %copy-done.31), channel_id=1, source_target_pairs={{0,1},{1,2},{2,3},{3,0},{4,5},{5,6},{6,7},{7,4},{8,9},{9,10},{10,1... | collective-permute-start | bytes 122888 | tf_op jit(solution)/shard_map/ppermute | solution.py:113
  410.7 56.8 %collective-permute-start.33 = (bf16[512,768]{1,0:T(8,128)(2,1)S(1)}, bf16[512,768]{1,0:T(8,128)(2,1)S(1)}, u32[]{:S(2)}, u32[]{:S(2)}) collective-permute-start(bf16[512,768]{1,0:T(8,128)(2,1)S(1)} %copy-done.5), channel_id=1, source_target_pairs={{8,0},{12,4},{16,8},{20,12},{24,16},{28,20},{9,1},{13,5},{17,9},{2... | collective-permute-start | bytes 2359304 | tf_op jit(solution)/shard_map/ppermute | solution.py:202
  413.7 53.7 %collective-permute-start.32 = (bf16[512,768]{1,0:T(8,128)(2,1)S(1)}, bf16[512,768]{1,0:T(8,128)(2,1)S(1)}, u32[]{:S(2)}, u32[]{:S(2)}) collective-permute-start(bf16[512,768]{1,0:T(8,128)(2,1)S(1)} %copy-done.5), channel_id=1, source_target_pairs={{0,8},{4,12},{8,16},{12,20},{16,24},{20,28},{1,9},{5,13},{9,17},{1... | collective-permute-start | bytes 2359304 | tf_op jit(solution)/shard_map/ppermute | solution.py:202
  468.7 17.1 %collective-permute-start.36 = (bf16[512,768]{1,0:T(8,128)(2,1)}, bf16[512,768]{1,0:T(8,128)(2,1)}, u32[]{:S(2)}, u32[]{:S(2)}) collective-permute-start(bf16[512,768]{1,0:T(8,128)(2,1)} %get-tuple-element.163), channel_id=1, source_target_pairs={{8,16},{12,20},{16,24},{20,28},{9,17},{13,21},{17,25},{21,29},{10,... | collective-permute-start | bytes 2359304 | tf_op jit(solution)/shard_map/ppermute | solution.py:202
  470.3 24.3 %collective-permute-start.37 = (bf16[512,768]{1,0:T(8,128)(2,1)}, bf16[512,768]{1,0:T(8,128)(2,1)}, u32[]{:S(2)}, u32[]{:S(2)}) collective-permute-start(bf16[512,768]{1,0:T(8,128)(2,1)} %get-tuple-element.164), channel_id=1, source_target_pairs={{8,0},{12,4},{16,8},{20,12},{9,1},{13,5},{17,9},{21,13},{10,2},{14... | collective-permute-start | bytes 2359304 | tf_op jit(solution)/shard_map/ppermute | solution.py:202
  471.6 29.8 %collective-permute-start.34 = (bf16[256,2048]{1,0:T(8,128)(2,1)}, bf16[256,2048]{1,0:T(8,128)(2,1)S(1)}, u32[]{:S(2)}, u32[]{:S(2)}) collective-permute-start(bf16[256,2048]{1,0:T(8,128)(2,1)} %get-tuple-element.161), channel_id=1, source_target_pairs={{0,8},{4,12},{1,9},{5,13},{2,10},{6,14},{3,11},{7,15}} | collective-permute-start | bytes 3145736 | tf_op jit(solution)/shard_map/ppermute | solution.py:202
  478.7 22.7 %collective-permute-start.35 = (bf16[256,2048]{1,0:T(8,128)(2,1)}, bf16[256,2048]{1,0:T(8,128)(2,1)S(1)}, u32[]{:S(2)}, u32[]{:S(2)}) collective-permute-start(bf16[256,2048]{1,0:T(8,128)(2,1)} %get-tuple-element.162), channel_id=1, source_target_pairs={{24,16},{28,20},{25,17},{29,21},{26,18},{30,22},{27,19},{31,23}} | collective-permute-start | bytes 3145736 | tf_op jit(solution)/shard_map/ppermute | solution.py:202
  502.7 34.3 %collective-permute-start.43 = (bf16[3,512,768]{2,1,0:T(8,128)(2,1)}, bf16[3,512,768]{2,1,0:T(8,128)(2,1)S(1)}, u32[]{:S(2)}, u32[]{:S(2)}) collective-permute-start(bf16[3,512,768]{2,1,0:T(8,128)(2,1)} %get-tuple-element.175), channel_id=1, source_target_pairs={{0,4},{4,0},{8,12},{12,8},{16,20},{20,16},{24,28},{28,24},{1,5},{5... | collective-permute-start | bytes 7077896 | tf_op jit(solution)/shard_map/ppermute | solution.py:33
  506.7 30.3 %collective-permute-start.40 = (bf16[256,2048]{1,0:T(8,128)(2,1)}, bf16[256,2048]{1,0:T(8,128)(2,1)}, u32[]{:S(2)}, u32[]{:S(2)}) collective-permute-start(bf16[256,2048]{1,0:T(8,128)(2,1)} %get-tuple-element.224), channel_id=1, source_target_pairs={{16,8},{20,12},{24,16},{28,20},{17,9},{21,13},{25,17},{29,21},{18,... | collective-permute-start | bytes 3145736 | tf_op jit(solution)/shard_map/ppermute | solution.py:202
  508.3 28.6 %collective-permute-start.39 = (bf16[256,2048]{1,0:T(8,128)(2,1)}, bf16[256,2048]{1,0:T(8,128)(2,1)}, u32[]{:S(2)}, u32[]{:S(2)}) collective-permute-start(bf16[256,2048]{1,0:T(8,128)(2,1)} %get-tuple-element.225), channel_id=1, source_target_pairs={{0,8},{4,12},{8,16},{12,20},{1,9},{5,13},{9,17},{13,21},{2,10},{6,... | collective-permute-start | bytes 3145736 | tf_op jit(solution)/shard_map/ppermute | solution.py:202
  513.2 19.4 %collective-permute-start.41 = (bf16[512,768]{1,0:T(8,128)(2,1)}, bf16[512,768]{1,0:T(8,128)(2,1)}, u32[]{:S(2)}, u32[]{:S(2)}) collective-permute-start(bf16[512,768]{1,0:T(8,128)(2,1)} %get-tuple-element.173), channel_id=1, source_target_pairs={{16,24},{20,28},{17,25},{21,29},{18,26},{22,30},{19,27},{23,31}} | collective-permute-start | bytes 2359304 | tf_op jit(solution)/shard_map/ppermute | solution.py:202
  514.8 22.1 %collective-permute-start.42 = (bf16[512,768]{1,0:T(8,128)(2,1)}, bf16[512,768]{1,0:T(8,128)(2,1)}, u32[]{:S(2)}, u32[]{:S(2)}) collective-permute-start(bf16[512,768]{1,0:T(8,128)(2,1)} %get-tuple-element.174), channel_id=1, source_target_pairs={{8,0},{12,4},{9,1},{13,5},{10,2},{14,6},{11,3},{15,7}} | collective-permute-start | bytes 2359304 | tf_op jit(solution)/shard_map/ppermute | solution.py:202
  538.3 16.2 %collective-permute-start.44 = (bf16[2,512,768]{2,1,0:T(8,128)(2,1)}, bf16[2,512,768]{2,1,0:T(8,128)(2,1)}, u32[]{:S(2)}, u32[]{:S(2)}) collective-permute-start(bf16[2,512,768]{2,1,0:T(8,128)(2,1)} %get-tuple-element.183), channel_id=1, source_target_pairs={{0,4},{4,0},{8,12},{12,8},{16,20},{20,16},{24,28},{28,24},{1,5},{5... | collective-permute-start | bytes 4718600 | tf_op jit(solution)/shard_map/ppermute | solution.py:33
  542.9 30.5 %collective-permute-start.49 = (bf16[256,2048]{1,0:T(8,128)(2,1)}, bf16[256,2048]{1,0:T(8,128)(2,1)}, u32[]{:S(2)}, u32[]{:S(2)}) collective-permute-start(bf16[256,2048]{1,0:T(8,128)(2,1)} %get-tuple-element.222), channel_id=1, source_target_pairs={{8,0},{12,4},{16,8},{20,12},{24,16},{28,20},{9,1},{13,5},{17,9},{2... | collective-permute-start | bytes 3145736 | tf_op jit(solution)/shard_map/ppermute | solution.py:202
  544.5 29.0 %collective-permute-start.48 = (bf16[256,2048]{1,0:T(8,128)(2,1)}, bf16[256,2048]{1,0:T(8,128)(2,1)}, u32[]{:S(2)}, u32[]{:S(2)}) collective-permute-start(bf16[256,2048]{1,0:T(8,128)(2,1)} %get-tuple-element.223), channel_id=1, source_target_pairs={{0,8},{4,12},{8,16},{12,20},{16,24},{20,28},{1,9},{5,13},{9,17},{1... | collective-permute-start | bytes 3145736 | tf_op jit(solution)/shard_map/ppermute | solution.py:202
  552.9 20.5 %collective-permute-start.47 = (f32[80,128]{1,0:T(8,128)S(1)}, f32[80,128]{1,0:T(8,128)S(1)}, u32[]{:S(2)}, u32[]{:S(2)}) collective-permute-start(f32[80,128]{1,0:T(8,128)S(1)} %copy-done.32), channel_id=1, source_target_pairs={{0,8},{4,12},{8,0},{12,4},{16,24},{20,28},{24,16},{28,20},{1,9},{5... | collective-permute-start | bytes 122888 | tf_op jit(solution)/shard_map/ppermute | solution.py:33
  (57 other events, 422.6 us)
Sparse Core Ops, SparseCore 0:
  9.6 84.7 all-gather.9
  96.0 80.5 all-gather.11
  182.7 89.9 reduce-scatter.1
  274.2 76.1 all-gather.7
  351.8 123.3 all-gather.13

commit v6 on v5

--- a/solution.py
+++ b/solution.py
@@ -1091,11 +1091,9 @@
         else:
             sources += [(block, 0) for block in attn_last]
     grad_attn_w = assemble_line(sources, line_origins(), attn_plan[0])
-    other_terms = flip(terms, "ctx", 1)
-    grad_attn_w, other_terms, grad_step, part_places = stage(grad_attn_w, other_terms, grad_step, part_places)
-    terms = terms + other_terms
-    for bit in range(2, bits_of(parts)):
-        terms = terms + flip(terms, "ctx", bit)
+    other_terms = others_of(terms, "ctx", 2, places)
+    grad_attn_w, others, grad_step, part_places = stage(grad_attn_w, other_terms[0], grad_step, part_places)
+    terms = sum_of(terms, others, other_terms[1])
     terms = terms.reshape(-1)
     grad_normed = line_block(part_places, 0) + grad_step[0].astype(F32) + grad_step[1].astype(F32)
 

time: 606 us -> 601 us (level)
    ppermute x3 -> x6, waiting for transfers between devices: 0.01 us -> 6.82 us  [others_of(): lax.ppermute(values, axis, [(i, moved(i, by)) for i in range(size)])]
    ppermute x3 -> x6, starting transfers between devices: 4.18 us -> 10.4 us  [others_of(): lax.ppermute(values, axis, [(i, moved(i, by)) for i in range(size)])]
    ppermute x36 -> x34, waiting for transfers between devices: 57.5 us -> 51.7 us  [flip(): return lax.ppermute(values, axis, [(i, i ^ 1 << bit) for i in range(count)])]
    ppermute x36 -> x34, starting transfers between devices: 37.7 us -> 32.6 us  [flip(): return lax.ppermute(values, axis, [(i, i ^ 1 << bit) for i in range(count)])]
    unnamed x106 -> x118, local copies, waits for them, and re-layouts: 26.7 us -> 23.7 us
  transfers between devices with their start and end apart: 56 -> 57, of which waited for: 19 -> 19; matrix products, arithmetic and copies ran while one was open for 32% -> 32% of each run, Pallas kernels for 31% -> 31%
where the time goes in v6:
time: 601 us; the launch traced here: 590 us
  Pallas kernels  185 us (31%)
  waiting for transfers between devices  103 us (17%)
  local copies, waits for them, and re-layouts  80.4 us (13%)
  other arithmetic  77.7 us (13%)
  starting transfers between devices  71 us (12%)
  matrix products  56.7 us (9%)
  between operations  15.3 us (3%)
    dot_general x5, matrix products, matmul_tn(): lax.dot_general(left, right, (((0,), (0,)), ((), ())), preferred_element_...  56.7 us
    ppermute x34, waiting for transfers between devices, flip(): return lax.ppermute(values, axis, [(i, i ^ 1 << bit) for i in range(count)])  51.7 us
    ppermute x12, waiting for transfers between devices, shift(): return lax.ppermute(values, 'ctx', pairs)  43.4 us
    pallas_call x1, Pallas kernels, attention_backward(): pl.pallas_call(functools.partial(backward_kernel, heads), out_shape=jax.S...  41.9 us
    ppermute x34, starting transfers between devices, flip(): return lax.ppermute(values, axis, [(i, i ^ 1 << bit) for i in range(count)])  32.6 us
    pallas_call x1, Pallas kernels, input_side(): pl.pallas_call(functools.partial(input_kernel, spans), grid=(tokens // CH...  31.6 us
    ppermute x12, starting transfers between devices, shift(): return lax.ppermute(values, 'ctx', pairs)  27.4 us
    unnamed x118, local copies, waits for them, and re-layouts  23.7 us
  transfers between devices with their start and end apart: 57, of which 19 were waited for; matrix products, arithmetic and copies ran while one was open for 32% of the time, Pallas kernels for 31%

profile of v6, /device:TPU:0, one launch (start us, length us, event | category | flops | bytes accessed | tf_op | source)
XLA Modules:
  0.0 589.8 jit_solution(12200343332502200135)
XLA Ops:
  10.1 2.9 constant_dynamic-slice_fusion.10
  13.0 2.8 concatenate.40
  17.5 2.9 collective-permute-start
  22.0 4.2 constant_dynamic-slice_fusion.2
  34.9 5.6 fusion.26
  50.8 5.8 collective-permute-done.2.refs_0_
  58.6 8.4 %collective-permute-done.4.refs_2_ = bf16[256,768]{1,0:T(8,128)(2,1)} collective-permute-done((bf16[256,768]{1,0:T(8,128)(2,1)S(1)}, bf16[256,768]{1,0:T(8,128)(2,1)}, u32[]{:S(2)}, u32[]{:S(2)}) %collective-permute-start.4) | collective-permute-done | bytes 393248 | tf_op jit(solution)/shard_map/ppermute | solution.py:33
  76.8 5.4 collective-permute-done.6.refs_0_
  83.8 7.0 %collective-permute-done.8.refs_2_ = bf16[256,768]{1,0:T(8,128)(2,1)S(1)} collective-permute-done((bf16[256,768]{1,0:T(8,128)(2,1)}, bf16[256,768]{1,0:T(8,128)(2,1)S(1)}, u32[]{:S(2)}, u32[]{:S(2)}) %collective-permute-start.8) | collective-permute-done | bytes 393248 | tf_op jit(solution)/shard_map/ppermute | solution.py:33
  99.1 17.2 %attn_side.1 = (bf16[2048,2048]{1,0:T(8,128)(2,1)}, f32[2048,768]{1,0:T(8,128)}) custom-call(s32[5]{0:T(128)} %stack.205.at_ref, bf16[2048,2048]{1,0:T(8,128)(2,1)} %bitcast.271, f32[1,2048]{1,0:T(1,128)} %bitcast.269, f32[1,2048]{1,0:T(1,128)} %bitcast.270, f32[1,768]{1,0:T(1,128)} %broadcast_in_dim.152.shift_ref, ...), custom_call_target="tpu_custom_call" | custom-call | flops 17999998976 | tf_op jit(solution)/shard_map/attn_side/pallas_call | solution.py:582
  116.3 22.6 %attention_forward.1 = (bf16[2048,256]{1,0:T(8,128)(2,1)S(1)}, bf16[2048,256]{1,0:T(8,128)(2,1)S(1)}, bf16[2048,256]{1,0:T(8,128)(2,1)S(1)}, bf16[2048,256]{1,0:...) custom-call(s32[16]{0:T(128)S(1)} %select_reduce_fusion.slot_ref, s32[8]{0:T(128)S(1)} %and_select_fusion.1.low_ref, ...), custom_call_target="tpu_custom_call" | custom-call | flops 24999999488 | tf_op jit(solution)/shard_map/attention_forward/pallas_call | solution.py:471
  145.1 20.6 %pair_side.1 = (bf16[2048,768]{1,0:T(8,128)(2,1)}, bf16[2048,768]{1,0:T(8,128)(2,1)}, bf16[2048,768]{1,0:T(8,128)(2,1)}) custom-call(s32[5]{0:T(128)} %stack.205.at_ref, bf16[2048,2048]{1,0:T(8,128)(2,1)} %get-tuple-element.110.normed_ref, bf16[512,768]{1,0:T(8,128)(2,1)} %concatenate.43.refs_0_, bf16[512,768]{1,0:T(8,128)(2,1)} %get-tuple-element.117.refs_1_, ...), custom_call_target="tpu_custom_call" | custom-call | flops 28000000000 | tf_op jit(solution)/shard_map/pair_side/pallas_call | solution.py:601
  166.8 15.0 %out_side.1.refs_1_ = bf16[2048,2048]{1,0:T(8,128)(2,1)} custom-call(s32[2,4]{1,0:T(2,128)} %pad_add_fusion.at_ref, bf16[2048,256]{1,0:T(8,128)(2,1)} %get-tuple-element.129.mixed_ref, bf16[2048,768]{1,0:T(8,128)(2,1)} %get-tuple-element.128.act_ref, bf16[240,2048]{1,0:T(8,128)(2,1)} %get-tuple-element.125.refs_0_.refs_4_, ...), custom_call_target="tpu_custom_call" | custom-call | flops 15000000512 | tf_op jit(solution)/shard_map/out_side/pallas_call | solution.py:697
  182.2 10.3 %fusion.58 = bf16[768,2048]{1,0:T(8,128)(2,1)S(1)} fusion(bf16[2048,768]{1,0:T(8,128)(2,1)} %get-tuple-element.128.act_ref, bf16[2048,2048]{1,0:T(8,128)(2,1)} %tie.22.refs_1_), kind=kOutput, calls=%fused_computation.193 | convolution fusion | flops 6442450944 | bytes 14680064 | tf_op jit(solution)/shard_map/dot_general | solution.py:28
  203.8 16.9 %grad_side.1 = (bf16[2048,768]{1,0:T(8,128)(2,1)}, bf16[2048,768]{1,0:T(8,128)(2,1)}, bf16[2048,256]{1,0:T(8,128)(2,1)}) custom-call(s32[2,4]{1,0:T(2,128)} %pad_add_fusion.at_ref, bf16[2048,2048]{1,0:T(8,128)(2,1)} %get-tuple-element.132.grad_ref, bf16[2048,768]{1,0:T(8,128)(2,1)} %get-tuple-element.133.slope_ref, ...), custom_call_target="tpu_custom_call" | custom-call | flops 17999998976 | tf_op jit(solution)/shard_map/grad_side/pallas_call | solution.py:665
  229.2 11.6 %convolution_convert_fusion.2.refs_0_ = bf16[2048,768]{1,0:T(8,128)(2,1)} fusion(bf16[2048,2048]{1,0:T(8,128)(2,1)} %get-tuple-element.110.normed_ref, bf16[2048,768]{1,0:T(8,128)(2,1)} %get-tuple-element.139.gate_ref), kind=kOutput, calls=%fused_computation.9 | convolution fusion | flops 6444023808 | bytes 14680064 | tf_op jit(solution)/shard_map/dot_general | solution.py:28
  240.8 20.9 %convolution_convert_fusion.1.refs_1_ = bf16[2048,768]{1,0:T(8,128)(2,1)} fusion(bf16[2048,2048]{1,0:T(8,128)(2,1)} %get-tuple-element.110.normed_ref, bf16[2048,768]{1,0:T(8,128)(2,1)S(1)} %copy-done.27), kind=kOutput, calls=%fused_computation.8 | convolution fusion | flops 6444023808 | bytes 14680064 | tf_op jit(solution)/shard_map/dot_general | solution.py:28
  271.0 41.9 %attention_backward.1.refs_0_ = bf16[2048,768]{1,0:T(8,128)(2,1)} custom-call(s32[16]{0:T(128)S(1)} %select_reduce_fusion.slot_ref, s32[8]{0:T(128)S(1)} %and_select_fusion.1.low_ref, bf16[2048,256]{1,0:T(8,128)(2,1)S(1)} %get-tuple-element.112.q_ref, bf16[2048,256]{1,0:T(8,128)(2,1)S(1)} %get-tuple-element.113.k_ref, bf16[2048,256]{1,0:T(8,128)(2,1)S(1)} %copy-done.14, ...), custom_call_target="tpu_custom_call" | custom-call | flops 40000000000 | tf_op jit(solution)/shard_map/attention_backward/pallas_call | solution.py:496
  317.5 11.6 %convolution_convert_fusion.refs_0_ = bf16[2048,768]{1,0:T(8,128)(2,1)} fusion(bf16[2048,2048]{1,0:T(8,128)(2,1)} %get-tuple-element.110.normed_ref, bf16[2048,768]{1,0:T(8,128)(2,1)} %get-tuple-element.147.refs_2_), kind=kOutput, calls=%fused_computation.7 | convolution fusion | flops 6444023808 | bytes 14680064 | tf_op jit(solution)/shard_map/dot_general | solution.py:28
  333.8 11.2 %collective-permute-done.22 = bf16[512,768]{1,0:T(8,128)(2,1)S(1)} collective-permute-done((bf16[512,768]{1,0:T(8,128)(2,1)S(1)}, bf16[512,768]{1,0:T(8,128)(2,1)S(1)}, u32[]{:S(2)}, u32[]{:S(2)}) %collective-permute-start.22) | collective-permute-done | bytes 786464 | tf_op jit(solution)/shard_map/ppermute | solution.py:33
  353.3 31.6 %input_side.1 = (bf16[2048,2048]{1,0:T(8,128)(2,1)}, f32[2,2048]{1,0:T(2,128)}) custom-call(s32[5]{0:T(128)} %stack.205.at_ref, bf16[2048,768]{1,0:T(8,128)(2,1)} %get-tuple-element.139.gate_ref, bf16[2048,768]{1,0:T(8,128)(2,1)} %get-tuple-element.140.up_ref, bf16[2048,768]{1,0:T(8,128)(2,1)} %get-tuple-element.151.merged_ref, ...), custom_call_target="tpu_custom_call" | custom-call | flops 30000001024 | tf_op jit(solution)/shard_map/input_side/pallas_call | solution.py:738
  391.4 4.8 collective-permute-done.27
  400.8 4.9 dynamic-slice_bitcast_fusion
  414.5 7.7 %fusion.refs_4_ = bf16[4,256,2048]{2,1,0:T(8,128)(2,1)} fusion(bf16[4,256,2048]{2,1,0:T(8,128)(2,1)} %collective-permute-done.31, bf16[4,2,256,2048]{3,2,1,0:T(8,128)(2,1)} %bitcast.256, s32[]{:T(128)S(6)} %select_n.427), kind=kLoop, calls=%fused_computation.1 | loop fusion | flops 8388608 | bytes 12582916 | tf_op jit(solution)/shard_map/convert_element_type | solution.py:1041
  422.2 3.2 dynamic-slice_bitcast_fusion.1
  425.4 3.0 fusion.12
  428.4 3.2 slice.192
  431.6 6.4 %bitcast_convert_fusion.refs_10_ = f32[1408,2048]{1,0:T(8,128)} fusion(bf16[8,176,2048]{2,1,0:T(8,128)(2,1)S(1)} %slice.192), kind=kLoop, calls=%fused_computation.4 | loop fusion | flops 2883584 | bytes 17301504 | tf_op jit(solution)/shard_map/convert_element_type | solution.py:1047
  439.7 2.7 bitcast_convert_fusion.1.refs_11_
  442.4 4.3 collective-permute-done.32.refs_7_
  446.7 21.2 %collective-permute-done.33.refs_8_ = bf16[512,768]{1,0:T(8,128)(2,1)S(1)} collective-permute-done((bf16[512,768]{1,0:T(8,128)(2,1)S(1)}, bf16[512,768]{1,0:T(8,128)(2,1)S(1)}, u32[]{:S(2)}, u32[]{:S(2)}) %collective-permute-start.33) | collective-permute-done | bytes 786464 | tf_op jit(solution)/shard_map/ppermute | solution.py:202
  468.9 5.3 collective-permute-start.34
  481.1 3.0 pad_maximum_fusion.1.refs_5_
  484.2 13.9 %collective-permute-done.37.refs_3_ = bf16[512,768]{1,0:T(8,128)(2,1)} collective-permute-done((bf16[512,768]{1,0:T(8,128)(2,1)}, bf16[512,768]{1,0:T(8,128)(2,1)}, u32[]{:S(2)}, u32[]{:S(2)}) %collective-permute-start.37) | collective-permute-done | bytes 786464 | tf_op jit(solution)/shard_map/ppermute | solution.py:202
  499.4 4.0 fusion.15
  503.3 4.4 collective-permute-start.39
  512.9 2.7 pad_maximum_fusion.4.refs_8_
  515.6 4.3 copy-done.2
  519.8 9.0 %assemble.1 = (f32[512,5632]{1,0:T(8,128)}, f32[512,5632]{1,0:T(8,128)}) custom-call(bf16[8,512,1408]{2,1,0:T(8,128)(2,1)S(1)} %copy-done.2), custom_call_target="tpu_custom_call" | custom-call | tf_op jit(solution)/shard_map/assemble/pallas_call | solution.py:771
  528.8 4.0 collective-permute-done.42.refs_3_
  534.2 4.6 fusion.18
  538.8 4.9 collective-permute-start.50
  550.3 3.5 collective-permute-start.49
  556.1 10.8 %assemble_line.1.refs_0_ = f32[512,6144]{1,0:T(8,128)} custom-call(s32[14]{0:T(128)S(1)} %stack.251.at_ref, bf16[1,512,768]{2,1,0:T(8,128)(2,1)S(1)} %bitcast.247, bf16[3,512,768]{2,1,0:T(8,128)(2,1)S(1)} %copy-done.4, bf16[1,512,768]{2,1,0:T(8,128)(2,1)S(1)} %bitcast.249, bf16[1,512,768]{2,1,0:T(8,128)(2,1)S(1)} %bitcast.251, ...), custom_call_target="tpu_custom_call" | custom-call | tf_op jit(solution)/shard_map/assemble_line/pallas_call | solution.py:805
  566.9 3.3 collective-permute-done.47.refs_1_
  570.2 2.7 collective-permute-done.48.refs_2_
  574.3 2.9 fusion.46
  577.3 4.2 fusion.30
  (341 shorter events, 149.6 us)
Async XLA Ops:
  7.2 91.9 %all-gather.10.cloned.1.call-start = ((), (), s32[]{:S(2)}) async-start(), calls=%async_computation.3 | async-start | bytes 9437184 | tf_op jit(solution)/shard_map/all_gather | solution.py:183
  7.9 174.2 %all-gather.12.cloned.1.call-start = ((), (), s32[]{:S(2)}) async-start(), calls=%async_computation.4 | async-start | bytes 9437184 | tf_op jit(solution)/shard_map/all_gather | solution.py:183
  8.7 416.7 %reduce-scatter.2.cloned.1.call-start = ((), (), s32[]{:S(2)}) async-start(), calls=%async_computation.1 | async-start | bytes 9437184 | tf_op jit(solution)/shard_map/reduce_scatter | solution.py:194
  17.5 24.5 %collective-permute-start = (bf16[528,768]{1,0:T(8,128)(2,1)}, bf16[528,768]{1,0:T(8,128)(2,1)}, u32[]{:S(2)}, u32[]{:S(2)}) collective-permute-start(bf16[528,768]{1,0:T(8,128)(2,1)} %pad_maximum_fusion.10.refs_0_.refs_10_), channel_id=1, source_target_pairs={{0,1},{1,0},{2,3},{3,2},{4,5},{5,4},{6,7},{7,6},{8,9},{9,8},{10,11... | collective-permute-start | bytes 2433032 | tf_op jit(solution)/shard_map/ppermute | solution.py:33
  20.5 21.6 %collective-permute-start.1 = (bf16[528,768]{1,0:T(8,128)(2,1)}, bf16[528,768]{1,0:T(8,128)(2,1)S(1)}, u32[]{:S(2)}, u32[]{:S(2)}) collective-permute-start(bf16[528,768]{1,0:T(8,128)(2,1)} %pad_maximum_fusion.10.refs_0_.refs_10_), channel_id=1, source_target_pairs={{0,2},{1,3},{2,0},{3,1},{4,6},{5,7},{6,4},{7,5},{8,10},{9,11},{10,... | collective-permute-start | bytes 2433032 | tf_op jit(solution)/shard_map/ppermute | solution.py:33
  28.7 27.9 %collective-permute-start.2 = (bf16[512,768]{1,0:T(8,128)(2,1)}, bf16[512,768]{1,0:T(8,128)(2,1)}, u32[]{:S(2)}, u32[]{:S(2)}) collective-permute-start(bf16[512,768]{1,0:T(8,128)(2,1)} %concatenate.43.refs_0_), channel_id=1, source_target_pairs={{0,1},{1,0},{2,3},{3,2},{4,5},{5,4},{6,7},{7,6},{8,9},{9,8},{10,11... | collective-permute-start | bytes 2359304 | tf_op jit(solution)/shard_map/ppermute | solution.py:33
  29.8 28.9 %collective-permute-start.3 = (bf16[512,768]{1,0:T(8,128)(2,1)}, bf16[512,768]{1,0:T(8,128)(2,1)}, u32[]{:S(2)}, u32[]{:S(2)}) collective-permute-start(bf16[512,768]{1,0:T(8,128)(2,1)} %concatenate.43.refs_0_), channel_id=1, source_target_pairs={{0,2},{1,3},{2,0},{3,1},{4,6},{5,7},{6,4},{7,5},{8,10},{9,11},{10,... | collective-permute-start | bytes 2359304 | tf_op jit(solution)/shard_map/ppermute | solution.py:33
  44.1 23.0 %collective-permute-start.4 = (bf16[256,768]{1,0:T(8,128)(2,1)S(1)}, bf16[256,768]{1,0:T(8,128)(2,1)}, u32[]{:S(2)}, u32[]{:S(2)}) collective-permute-start(bf16[256,768]{1,0:T(8,128)(2,1)S(1)} %slice.142), channel_id=1, source_target_pairs={{0,2},{1,3},{2,0},{3,1},{4,6},{5,7},{6,4},{7,5},{8,10},{9,11},{10,... | collective-permute-start | bytes 1179656 | tf_op jit(solution)/shard_map/ppermute | solution.py:33
  47.2 19.9 %collective-permute-start.5 = (bf16[272,768]{1,0:T(8,128)(2,1)S(1)}, bf16[272,768]{1,0:T(8,128)(2,1)S(1)}, u32[]{:S(2)}, u32[]{:S(2)}) collective-permute-start(bf16[272,768]{1,0:T(8,128)(2,1)S(1)} %slice.143), channel_id=1, source_target_pairs={{0,1},{1,0},{2,3},{3,2},{4,5},{5,4},{6,7},{7,6},{8,9},{9,8},{10,11... | collective-permute-start | bytes 1253384 | tf_op jit(solution)/shard_map/ppermute | solution.py:33
  48.2 34.0 %collective-permute-start.6 = (bf16[512,768]{1,0:T(8,128)(2,1)}, bf16[512,768]{1,0:T(8,128)(2,1)S(1)}, u32[]{:S(2)}, u32[]{:S(2)}) collective-permute-start(bf16[512,768]{1,0:T(8,128)(2,1)} %get-tuple-element.119.refs_5_), channel_id=1, source_target_pairs={{0,1},{1,0},{2,3},{3,2},{4,5},{5,4},{6,7},{7,6},{8,9},{9,8},{10,11... | collective-permute-start | bytes 2359304 | tf_op jit(solution)/shard_map/ppermute | solution.py:33
  56.5 27.3 %collective-permute-start.7 = (bf16[512,768]{1,0:T(8,128)(2,1)}, bf16[512,768]{1,0:T(8,128)(2,1)S(1)}, u32[]{:S(2)}, u32[]{:S(2)}) collective-permute-start(bf16[512,768]{1,0:T(8,128)(2,1)} %get-tuple-element.119.refs_5_), channel_id=1, source_target_pairs={{0,2},{1,3},{2,0},{3,1},{4,6},{5,7},{6,4},{7,5},{8,10},{9,11},{10,... | collective-permute-start | bytes 2359304 | tf_op jit(solution)/shard_map/ppermute | solution.py:33
  72.2 18.6 %collective-permute-start.8 = (bf16[256,768]{1,0:T(8,128)(2,1)}, bf16[256,768]{1,0:T(8,128)(2,1)S(1)}, u32[]{:S(2)}, u32[]{:S(2)}) collective-permute-start(bf16[256,768]{1,0:T(8,128)(2,1)} %slice.149), channel_id=1, source_target_pairs={{0,2},{1,3},{2,0},{3,1},{4,6},{5,7},{6,4},{7,5},{8,10},{9,11},{10,... | collective-permute-start | bytes 1179656 | tf_op jit(solution)/shard_map/ppermute | solution.py:33
  91.5 49.4 %collective-permute-start.12 = (bf16[240,2048]{1,0:T(8,128)(2,1)}, bf16[240,2048]{1,0:T(8,128)(2,1)}, u32[]{:S(2)}, u32[]{:S(2)}) collective-permute-start(bf16[240,2048]{1,0:T(8,128)(2,1)} %get-tuple-element.125.refs_0_.refs_4_), channel_id=1, source_target_pairs={{0,1},{1,0},{2,3},{3,2},{4,5},{5,4},{6,7},{7,6},{8,9},{9,8},{10,11... | collective-permute-start | bytes 2949128 | tf_op jit(solution)/shard_map/ppermute | solution.py:33
  91.9 49.1 %collective-permute-start.13 = (bf16[240,2048]{1,0:T(8,128)(2,1)}, bf16[240,2048]{1,0:T(8,128)(2,1)}, u32[]{:S(2)}, u32[]{:S(2)}) collective-permute-start(bf16[240,2048]{1,0:T(8,128)(2,1)} %get-tuple-element.125.refs_0_.refs_4_), channel_id=1, source_target_pairs={{0,2},{1,3},{2,0},{3,1},{4,6},{5,7},{6,4},{7,5},{8,10},{9,11},{10,... | collective-permute-start | bytes 2949128 | tf_op jit(solution)/shard_map/ppermute | solution.py:33
  95.3 45.6 %collective-permute-start.10 = (bf16[256,768]{1,0:T(8,128)(2,1)}, bf16[256,768]{1,0:T(8,128)(2,1)}, u32[]{:S(2)}, u32[]{:S(2)}) collective-permute-start(bf16[256,768]{1,0:T(8,128)(2,1)} %slice.151), channel_id=1, source_target_pairs={{0,2},{1,3},{2,0},{3,1},{4,6},{5,7},{6,4},{7,5},{8,10},{9,11},{10,... | collective-permute-start | bytes 1179656 | tf_op jit(solution)/shard_map/ppermute | solution.py:33
  97.4 43.5 %collective-permute-start.11 = (bf16[256,768]{1,0:T(8,128)(2,1)}, bf16[256,768]{1,0:T(8,128)(2,1)}, u32[]{:S(2)}, u32[]{:S(2)}) collective-permute-start(bf16[256,768]{1,0:T(8,128)(2,1)} %slice.152), channel_id=1, source_target_pairs={{0,1},{1,0},{2,3},{3,2},{4,5},{5,4},{6,7},{7,6},{8,9},{9,8},{10,11... | collective-permute-start | bytes 1179656 | tf_op jit(solution)/shard_map/ppermute | solution.py:33
  142.0 23.7 %collective-permute-start.14 = (bf16[112,2048]{1,0:T(8,128)(2,1)S(1)}, bf16[112,2048]{1,0:T(8,128)(2,1)S(1)}, u32[]{:S(2)}, u32[]{:S(2)}) collective-permute-start(bf16[112,2048]{1,0:T(8,128)(2,1)S(1)} %slice.153), channel_id=1, source_target_pairs={{0,2},{1,3},{2,0},{3,1},{4,6},{5,7},{6,4},{7,5},{8,10},{9,11},{10,... | collective-permute-start | bytes 1376264 | tf_op jit(solution)/shard_map/ppermute | solution.py:33
  144.7 21.1 %collective-permute-start.15 = (bf16[128,2048]{1,0:T(8,128)(2,1)S(1)}, bf16[128,2048]{1,0:T(8,128)(2,1)S(1)}, u32[]{:S(2)}, u32[]{:S(2)}) collective-permute-start(bf16[128,2048]{1,0:T(8,128)(2,1)S(1)} %slice.154), channel_id=1, source_target_pairs={{0,1},{1,0},{2,3},{3,2},{4,5},{5,4},{6,7},{7,6},{8,9},{9,8},{10,11... | collective-permute-start | bytes 1572872 | tf_op jit(solution)/shard_map/ppermute | solution.py:33
  181.8 246.6 %all-gather.8.cloned.1.call-start = ((), (), s32[]{:S(2)}) async-start(), calls=%async_computation.2 | async-start | bytes 8847360 | tf_op jit(solution)/shard_map/all_gather | solution.py:183
  201.3 21.2 %collective-permute-start.16 = (bf16[2,240,1024]{2,1,0:T(8,128)(2,1)S(1)}, bf16[2,240,1024]{2,1,0:T(8,128)(2,1)}, u32[]{:S(2)}, u32[]{:S(2)}) collective-permute-start(bf16[2,240,1024]{2,1,0:T(8,128)(2,1)S(1)} %pad_maximum_fusion.7), channel_id=1, source_target_pairs={{0,1},{1,0},{2,3},{3,2},{4,5},{5,4},{6,7},{7,6},{8,9},{9,8},{10,11... | collective-permute-start | bytes 2949128 | tf_op jit(solution)/shard_map/ppermute | solution.py:33
  203.2 21.1 %collective-permute-start.17 = (bf16[2,240,1024]{2,1,0:T(8,128)(2,1)S(1)}, bf16[2,240,1024]{2,1,0:T(8,128)(2,1)}, u32[]{:S(2)}, u32[]{:S(2)}) collective-permute-start(bf16[2,240,1024]{2,1,0:T(8,128)(2,1)S(1)} %pad_maximum_fusion.8), channel_id=1, source_target_pairs={{0,2},{1,3},{2,0},{3,1},{4,6},{5,7},{6,4},{7,5},{8,10},{9,11},{10,... | collective-permute-start | bytes 2949128 | tf_op jit(solution)/shard_map/ppermute | solution.py:33
  225.8 36.0 %collective-permute-start.19 = (bf16[240,1024]{1,0:T(8,128)(2,1)S(1)}, bf16[240,1024]{1,0:T(8,128)(2,1)S(1)}, u32[]{:S(2)}, u32[]{:S(2)}) collective-permute-start(bf16[240,1024]{1,0:T(8,128)(2,1)S(1)} %fusion.31), channel_id=1, source_target_pairs={{0,2},{1,3},{2,0},{3,1},{4,6},{5,7},{6,4},{7,5},{8,10},{9,11},{10,... | collective-permute-start | bytes 1474568 | tf_op jit(solution)/shard_map/ppermute | solution.py:33
  228.0 35.2 %collective-permute-start.18 = (bf16[240,1024]{1,0:T(8,128)(2,1)S(1)}, bf16[240,1024]{1,0:T(8,128)(2,1)S(1)}, u32[]{:S(2)}, u32[]{:S(2)}) collective-permute-start(bf16[240,1024]{1,0:T(8,128)(2,1)S(1)} %fusion.34), channel_id=1, source_target_pairs={{0,1},{1,0},{2,3},{3,2},{4,5},{5,4},{6,7},{7,6},{8,9},{9,8},{10,11... | collective-permute-start | bytes 1474568 | tf_op jit(solution)/shard_map/ppermute | solution.py:33
  265.7 249.9 %all-gather.14.cloned.1.call-start = ((), (), s32[]{:S(2)}) async-start(), calls=%async_computation.5 | async-start | bytes 12976128 | tf_op jit(solution)/shard_map/all_gather | solution.py:183
  267.5 45.4 %collective-permute-start.20 = (bf16[2,512,768]{2,1,0:T(8,128)(2,1)S(1)}, bf16[2,512,768]{2,1,0:T(8,128)(2,1)}, u32[]{:S(2)}, u32[]{:S(2)}) collective-permute-start(bf16[2,512,768]{2,1,0:T(8,128)(2,1)S(1)} %pad_maximum_fusion.2), channel_id=1, source_target_pairs={{0,1},{1,0},{2,3},{3,2},{4,5},{5,4},{6,7},{7,6},{8,9},{9,8},{10,11... | collective-permute-start | bytes 4718600 | tf_op jit(solution)/shard_map/ppermute | solution.py:33
  269.5 43.4 %collective-permute-start.21 = (bf16[2,512,768]{2,1,0:T(8,128)(2,1)S(1)}, bf16[2,512,768]{2,1,0:T(8,128)(2,1)}, u32[]{:S(2)}, u32[]{:S(2)}) collective-permute-start(bf16[2,512,768]{2,1,0:T(8,128)(2,1)S(1)} %pad_maximum_fusion.3), channel_id=1, source_target_pairs={{0,2},{1,3},{2,0},{3,1},{4,6},{5,7},{6,4},{7,5},{8,10},{9,11},{10,... | collective-permute-start | bytes 4718600 | tf_op jit(solution)/shard_map/ppermute | solution.py:33
  316.2 17.3 %collective-permute-start.23 = (bf16[512,768]{1,0:T(8,128)(2,1)S(1)}, bf16[512,768]{1,0:T(8,128)(2,1)S(1)}, u32[]{:S(2)}, u32[]{:S(2)}) collective-permute-start(bf16[512,768]{1,0:T(8,128)(2,1)S(1)} %fusion.20), channel_id=1, source_target_pairs={{0,2},{1,3},{2,0},{3,1},{4,6},{5,7},{6,4},{7,5},{8,10},{9,11},{10,... | collective-permute-start | bytes 2359304 | tf_op jit(solution)/shard_map/ppermute | solution.py:33
  350.2 36.1 %collective-permute-start.24 = (bf16[2,512,384]{2,1,0:T(8,128)(2,1)}, bf16[2,512,384]{2,1,0:T(8,128)(2,1)}, u32[]{:S(2)}, u32[]{:S(2)}) collective-permute-start(bf16[2,512,384]{2,1,0:T(8,128)(2,1)} %pad_maximum_fusion.11), channel_id=1, source_target_pairs={{0,1},{1,0},{2,3},{3,2},{4,5},{5,4},{6,7},{7,6},{8,9},{9,8},{10,11... | collective-permute-start | bytes 2359304 | tf_op jit(solution)/shard_map/ppermute | solution.py:33
  352.3 34.0 %collective-permute-start.25 = (bf16[2,512,384]{2,1,0:T(8,128)(2,1)}, bf16[2,512,384]{2,1,0:T(8,128)(2,1)}, u32[]{:S(2)}, u32[]{:S(2)}) collective-permute-start(bf16[2,512,384]{2,1,0:T(8,128)(2,1)} %pad_maximum_fusion.12), channel_id=1, source_target_pairs={{0,2},{1,3},{2,0},{3,1},{4,6},{5,7},{6,4},{7,5},{8,10},{9,11},{10,... | collective-permute-start | bytes 2359304 | tf_op jit(solution)/shard_map/ppermute | solution.py:33
  405.9 36.5 %collective-permute-start.28 = (f32[80,128]{1,0:T(8,128)S(1)}, f32[80,128]{1,0:T(8,128)S(1)}, u32[]{:S(2)}, u32[]{:S(2)}) collective-permute-start(f32[80,128]{1,0:T(8,128)S(1)} %copy-done.31), channel_id=1, source_target_pairs={{0,1},{1,2},{2,3},{3,0},{4,5},{5,6},{6,7},{7,4},{8,9},{9,10},{10,1... | collective-permute-start | bytes 122888 | tf_op jit(solution)/shard_map/ppermute | solution.py:113
  406.7 35.7 %collective-permute-start.29 = (f32[80,128]{1,0:T(8,128)S(1)}, f32[80,128]{1,0:T(8,128)S(1)}, u32[]{:S(2)}, u32[]{:S(2)}) collective-permute-start(f32[80,128]{1,0:T(8,128)S(1)} %copy-done.31), channel_id=1, source_target_pairs={{0,2},{1,3},{2,0},{3,1},{4,6},{5,7},{6,4},{7,5},{8,10},{9,11},{10,... | collective-permute-start | bytes 122888 | tf_op jit(solution)/shard_map/ppermute | solution.py:113
  407.7 34.8 %collective-permute-start.30 = (f32[80,128]{1,0:T(8,128)S(1)}, f32[80,128]{1,0:T(8,128)S(1)}, u32[]{:S(2)}, u32[]{:S(2)}) collective-permute-start(f32[80,128]{1,0:T(8,128)S(1)} %copy-done.31), channel_id=1, source_target_pairs={{0,3},{1,0},{2,1},{3,2},{4,7},{5,4},{6,5},{7,6},{8,11},{9,8},{10,9... | collective-permute-start | bytes 122888 | tf_op jit(solution)/shard_map/ppermute | solution.py:113
  410.2 36.5 %collective-permute-start.32 = (bf16[512,768]{1,0:T(8,128)(2,1)S(1)}, bf16[512,768]{1,0:T(8,128)(2,1)S(1)}, u32[]{:S(2)}, u32[]{:S(2)}) collective-permute-start(bf16[512,768]{1,0:T(8,128)(2,1)S(1)} %copy-done.5), channel_id=1, source_target_pairs={{0,8},{4,12},{8,16},{12,20},{16,24},{20,28},{1,9},{5,13},{9,17},{1... | collective-permute-start | bytes 2359304 | tf_op jit(solution)/shard_map/ppermute | solution.py:202
  413.2 54.8 %collective-permute-start.33 = (bf16[512,768]{1,0:T(8,128)(2,1)S(1)}, bf16[512,768]{1,0:T(8,128)(2,1)S(1)}, u32[]{:S(2)}, u32[]{:S(2)}) collective-permute-start(bf16[512,768]{1,0:T(8,128)(2,1)S(1)} %copy-done.5), channel_id=1, source_target_pairs={{8,0},{12,4},{16,8},{20,12},{24,16},{28,20},{9,1},{13,5},{17,9},{2... | collective-permute-start | bytes 2359304 | tf_op jit(solution)/shard_map/ppermute | solution.py:202
  468.9 29.1 %collective-permute-start.34 = (bf16[256,2048]{1,0:T(8,128)(2,1)}, bf16[256,2048]{1,0:T(8,128)(2,1)S(1)}, u32[]{:S(2)}, u32[]{:S(2)}) collective-permute-start(bf16[256,2048]{1,0:T(8,128)(2,1)} %get-tuple-element.163), channel_id=1, source_target_pairs={{0,8},{4,12},{1,9},{5,13},{2,10},{6,14},{3,11},{7,15}} | collective-permute-start | bytes 3145736 | tf_op jit(solution)/shard_map/ppermute | solution.py:202
  474.2 23.8 %collective-permute-start.35 = (bf16[256,2048]{1,0:T(8,128)(2,1)}, bf16[256,2048]{1,0:T(8,128)(2,1)S(1)}, u32[]{:S(2)}, u32[]{:S(2)}) collective-permute-start(bf16[256,2048]{1,0:T(8,128)(2,1)} %get-tuple-element.164), channel_id=1, source_target_pairs={{24,16},{28,20},{25,17},{29,21},{26,18},{30,22},{27,19},{31,23}} | collective-permute-start | bytes 3145736 | tf_op jit(solution)/shard_map/ppermute | solution.py:202
  476.5 21.5 %collective-permute-start.37 = (bf16[512,768]{1,0:T(8,128)(2,1)}, bf16[512,768]{1,0:T(8,128)(2,1)}, u32[]{:S(2)}, u32[]{:S(2)}) collective-permute-start(bf16[512,768]{1,0:T(8,128)(2,1)} %get-tuple-element.166), channel_id=1, source_target_pairs={{8,0},{12,4},{16,8},{20,12},{9,1},{13,5},{17,9},{21,13},{10,2},{14... | collective-permute-start | bytes 2359304 | tf_op jit(solution)/shard_map/ppermute | solution.py:202
  499.3 33.4 %collective-permute-start.43 = (bf16[3,512,768]{2,1,0:T(8,128)(2,1)}, bf16[3,512,768]{2,1,0:T(8,128)(2,1)S(1)}, u32[]{:S(2)}, u32[]{:S(2)}) collective-permute-start(bf16[3,512,768]{2,1,0:T(8,128)(2,1)} %get-tuple-element.177), channel_id=1, source_target_pairs={{0,4},{4,0},{8,12},{12,8},{16,20},{20,16},{24,28},{28,24},{1,5},{5... | collective-permute-start | bytes 7077896 | tf_op jit(solution)/shard_map/ppermute | solution.py:33
  503.3 29.4 %collective-permute-start.39 = (bf16[256,2048]{1,0:T(8,128)(2,1)}, bf16[256,2048]{1,0:T(8,128)(2,1)}, u32[]{:S(2)}, u32[]{:S(2)}) collective-permute-start(bf16[256,2048]{1,0:T(8,128)(2,1)} %get-tuple-element.229), channel_id=1, source_target_pairs={{0,8},{4,12},{8,16},{12,20},{1,9},{5,13},{9,17},{13,21},{2,10},{6,... | collective-permute-start | bytes 3145736 | tf_op jit(solution)/shard_map/ppermute | solution.py:202
  507.7 25.1 %collective-permute-start.40 = (bf16[256,2048]{1,0:T(8,128)(2,1)}, bf16[256,2048]{1,0:T(8,128)(2,1)}, u32[]{:S(2)}, u32[]{:S(2)}) collective-permute-start(bf16[256,2048]{1,0:T(8,128)(2,1)} %get-tuple-element.228), channel_id=1, source_target_pairs={{16,8},{20,12},{24,16},{28,20},{17,9},{21,13},{25,17},{29,21},{18,... | collective-permute-start | bytes 3145736 | tf_op jit(solution)/shard_map/ppermute | solution.py:202
  509.4 19.4 %collective-permute-start.41 = (bf16[512,768]{1,0:T(8,128)(2,1)}, bf16[512,768]{1,0:T(8,128)(2,1)}, u32[]{:S(2)}, u32[]{:S(2)}) collective-permute-start(bf16[512,768]{1,0:T(8,128)(2,1)} %get-tuple-element.175), channel_id=1, source_target_pairs={{16,24},{20,28},{17,25},{21,29},{18,26},{22,30},{19,27},{23,31}} | collective-permute-start | bytes 2359304 | tf_op jit(solution)/shard_map/ppermute | solution.py:202
  510.9 21.8 %collective-permute-start.42 = (bf16[512,768]{1,0:T(8,128)(2,1)}, bf16[512,768]{1,0:T(8,128)(2,1)}, u32[]{:S(2)}, u32[]{:S(2)}) collective-permute-start(bf16[512,768]{1,0:T(8,128)(2,1)} %get-tuple-element.176), channel_id=1, source_target_pairs={{8,0},{12,4},{9,1},{13,5},{10,2},{14,6},{11,3},{15,7}} | collective-permute-start | bytes 2359304 | tf_op jit(solution)/shard_map/ppermute | solution.py:202
  534.2 16.1 %collective-permute-start.44 = (bf16[2,512,768]{2,1,0:T(8,128)(2,1)}, bf16[2,512,768]{2,1,0:T(8,128)(2,1)}, u32[]{:S(2)}, u32[]{:S(2)}) collective-permute-start(bf16[2,512,768]{2,1,0:T(8,128)(2,1)} %get-tuple-element.185), channel_id=1, source_target_pairs={{0,4},{4,0},{8,12},{12,8},{16,20},{20,16},{24,28},{28,24},{1,5},{5... | collective-permute-start | bytes 4718600 | tf_op jit(solution)/shard_map/ppermute | solution.py:33
  538.8 34.9 %collective-permute-start.50 = (bf16[256,2048]{1,0:T(8,128)(2,1)}, bf16[256,2048]{1,0:T(8,128)(2,1)}, u32[]{:S(2)}, u32[]{:S(2)}) collective-permute-start(bf16[256,2048]{1,0:T(8,128)(2,1)} %get-tuple-element.227), channel_id=1, source_target_pairs={{0,8},{4,12},{8,16},{12,20},{16,24},{20,28},{1,9},{5,13},{9,17},{1... | collective-permute-start | bytes 3145736 | tf_op jit(solution)/shard_map/ppermute | solution.py:202
  543.7 30.0 %collective-permute-start.51 = (bf16[256,2048]{1,0:T(8,128)(2,1)}, bf16[256,2048]{1,0:T(8,128)(2,1)}, u32[]{:S(2)}, u32[]{:S(2)}) collective-permute-start(bf16[256,2048]{1,0:T(8,128)(2,1)} %get-tuple-element.226), channel_id=1, source_target_pairs={{8,0},{12,4},{16,8},{20,12},{24,16},{28,20},{9,1},{13,5},{17,9},{2... | collective-permute-start | bytes 3145736 | tf_op jit(solution)/shard_map/ppermute | solution.py:202
  547.7 22.5 %collective-permute-start.47 = (f32[80,128]{1,0:T(8,128)S(1)}, f32[80,128]{1,0:T(8,128)S(1)}, u32[]{:S(2)}, u32[]{:S(2)}) collective-permute-start(f32[80,128]{1,0:T(8,128)S(1)} %copy-done.32), channel_id=1, source_target_pairs={{0,8},{4,12},{8,16},{12,20},{16,24},{20,28},{24,0},{28,4},{1,9},{5... | collective-permute-start | bytes 122888 | tf_op jit(solution)/shard_map/ppermute | solution.py:113
  550.3 22.5 %collective-permute-start.48 = (f32[80,128]{1,0:T(8,128)S(1)}, f32[80,128]{1,0:T(8,128)S(1)}, u32[]{:S(2)}, u32[]{:S(2)}) collective-permute-start(f32[80,128]{1,0:T(8,128)S(1)} %copy-done.32), channel_id=1, source_target_pairs={{0,16},{4,20},{8,24},{12,28},{16,0},{20,4},{24,8},{28,12},{1,17},{... | collective-permute-start | bytes 122888 | tf_op jit(solution)/shard_map/ppermute | solution.py:113
  550.3 23.4 %collective-permute-start.49 = (f32[80,128]{1,0:T(8,128)S(1)}, f32[80,128]{1,0:T(8,128)S(1)}, u32[]{:S(2)}, u32[]{:S(2)}) collective-permute-start(f32[80,128]{1,0:T(8,128)S(1)} %copy-done.32), channel_id=1, source_target_pairs={{0,24},{4,28},{8,0},{12,4},{16,8},{20,12},{24,16},{28,20},{1,25},{... | collective-permute-start | bytes 122888 | tf_op jit(solution)/shard_map/ppermute | solution.py:113
  (64 other events, 472.6 us)
Sparse Core Ops, SparseCore 0:
  9.6 84.7 all-gather.9
  96.0 80.5 all-gather.11
  181.9 90.2 reduce-scatter.1
  273.7 76.0 all-gather.7
  351.3 123.3 all-gather.13
